TPU v7x, 256 devices: a whole 4x4x8 slice. The times are simulated.
256 devices in a mesh: dp: 64 (over x, z, core), tensor: 4 (over y).
Axes of the slice: x: 4, y: 4, z: 8, core: 2. Of those that a mesh axis runs over, the one named last changes fastest.
Arguments:
- gradient: bfloat16 [8, 5120, 13824], P(None, 'dp', 'tensor'), may hold values from -16 to 16
- error_buffer: bfloat16 [8, 5120, 13824], P(None, 'dp', 'tensor'), may hold values from -6 to 6
- q_start: bfloat16 [13824, 64], P('tensor'), may hold values from -6 to 6
Outputs:
- new_error: bfloat16 [8, 5120, 13824], P(None, 'dp', 'tensor')
- q_factor: float32 [13824, 64], P('tensor')
All inputs are finite; a program needn't handle non-finite values.
Results may differ from a plain program's by a relative error of at most 0.015.
Values may be sent and summed in bfloat16 or wider, within the bound.
No kernel may reach another device: no remote copies, remote signals or barrier semaphores. Data moves between devices by JAX's collectives and lax.ppermute only.
A program may use at most 64 MiB of HBM per device.

v0:
```python
import jax
import jax.numpy as jnp
from jax import lax
from jax.sharding import PartitionSpec as P

ITERS = 2


def per_device(gradient, error_buffer, q_start):
    replicas = gradient.shape[0]
    corrected = (gradient.astype(jnp.float32) + error_buffer.astype(jnp.float32)).astype(
        jnp.bfloat16
    )
    q_half = q_start
    q_now = None
    p_half = None
    for step in range(ITERS):
        partial_p = jnp.einsum("rdc,ck->dk", corrected, q_half, preferred_element_type=jnp.float32)
        p_mean = lax.psum(partial_p, "tensor") / replicas
        local_gram = jnp.dot(p_mean.T, p_mean, precision=lax.Precision.HIGHEST)
        gram = lax.psum(local_gram, "dp")
        lower = jnp.linalg.cholesky(gram)
        p_orth = jax.scipy.linalg.solve_triangular(lower, p_mean.T, lower=True).T
        p_half = p_orth.astype(jnp.bfloat16)
        partial_q = jnp.einsum("rdc,dk->ck", corrected, p_half, preferred_element_type=jnp.float32)
        q_now = lax.psum(partial_q, "dp") / replicas
        q_half = q_now.astype(jnp.bfloat16)
    recon = jnp.dot(p_half, q_half.T, preferred_element_type=jnp.float32)
    new_error = (corrected.astype(jnp.float32) - recon[None]).astype(jnp.bfloat16)
    return (new_error, q_now)


def solution(mesh):
    placed = (P(None, "dp", "tensor"), P(None, "dp", "tensor"), P("tensor", None))
    return jax.shard_map(
        per_device,
        mesh=mesh,
        in_specs=placed,
        out_specs=(P(None, "dp", "tensor"), P("tensor", None)),
        check_vma=False,
    )
```

profile of v0, /device:TPU:1, one launch (start us, length us, event | category | flops | bytes accessed | tf_op | source)
XLA Modules:
  0.0 941.6 jit_solution(11187475678344716016)
XLA Ops:
  7.2 0.0 copy-start
  7.2 0.0 all-reduce.3.cloned.1.call-start
  7.2 4.8 convert_reduce_fusion
  12.0 0.0 copy-done
  12.0 0.3 fusion.30
  12.3 14.4 %psum.42 = f32[80,64]{0,1:T(8,128)S(1)} all-reduce(f32[80,64]{0,1:T(8,128)S(1)} %fusion.30), channel_id=1, replica_groups=mesh['dp'=64,'tensor'=4] {'tensor'}, use_global_device_ids=true, to_apply=%region_1.0 | all-reduce | flops 5120 | bytes 40960 | tf_op jit(solution)/shard_map/psum | solution.py:19
  26.7 0.2 fusion.19
  26.9 248.6 %psum.43 = f32[64,64]{0,1:T(8,128)S(1)} all-reduce(f32[64,64]{0,1:T(8,128)S(1)} %fusion.19), channel_id=1, replica_groups=mesh['dp'=64,'tensor'=4] {'dp'}, use_global_device_ids=true, to_apply=%region_2.0 | all-reduce | flops 4096 | bytes 32768 | tf_op jit(solution)/shard_map/psum | solution.py:21
  275.6 0.1 copy.6
  275.6 5.8 cholesky.44
  281.5 0.6 compare_reduce_fusion.1
  282.2 0.7 fusion.5
  282.8 4.9 custom-call.6
  287.7 0.3 convolution_convert_fusion.1
  288.0 1.2 fusion.31
  289.2 0.0 all-reduce.3.cloned.1.call-update
  289.2 0.0 all-reduce.5.cloned.1.call-start
  289.2 180.1 %all-reduce.3.cloned.1.call-done = f32[3456,64]{0,1:T(8,128)} async-done(((f32[3456,64]{0,1:T(8,128)}), f32[3456,64]{0,1:T(8,128)}) %all-reduce.3.cloned.1.call-update) | async-done | bytes 884752 | tf_op jit(solution)/shard_map/psum | solution.py:26
  469.3 1.5 fusion.1
  470.8 13.3 %psum.45 = f32[80,64]{0,1:T(8,128)S(1)} all-reduce(f32[80,64]{0,1:T(8,128)S(1)} %fusion.1), channel_id=1, replica_groups=mesh['dp'=64,'tensor'=4] {'tensor'}, use_global_device_ids=true, to_apply=%region_6.0 | all-reduce | flops 5120 | bytes 40960 | tf_op jit(solution)/shard_map/psum | solution.py:19
  484.1 0.2 fusion.16
  484.3 248.1 %psum.46 = f32[64,64]{0,1:T(8,128)S(1)} all-reduce(f32[64,64]{0,1:T(8,128)S(1)} %fusion.16), channel_id=1, replica_groups=mesh['dp'=64,'tensor'=4] {'dp'}, use_global_device_ids=true, to_apply=%region_7.0 | all-reduce | flops 4096 | bytes 32768 | tf_op jit(solution)/shard_map/psum | solution.py:21
  732.3 0.1 copy.8
  732.4 5.8 cholesky.55
  738.3 0.6 compare_reduce_fusion
  739.0 0.7 fusion.6
  739.6 4.9 custom-call.7
  744.5 0.3 convolution_convert_fusion
  744.8 1.2 fusion.32
  746.0 0.0 all-reduce.5.cloned.1.call-update
  746.0 180.2 %all-reduce.5.cloned.1.call-done = f32[3456,64]{0,1:T(8,128)} async-done(((f32[3456,64]{0,1:T(8,128)}), f32[3456,64]{0,1:T(8,128)}) %all-reduce.5.cloned.1.call-update) | async-done | bytes 884752 | tf_op jit(solution)/shard_map/psum | solution.py:26
  926.2 1.2 broadcast_multiply_fusion
  927.4 0.0 copy-start.1
  927.4 0.3 fusion.2
  927.7 7.0 fusion
  934.7 0.0 copy-done.1
  (4 shorter events, 0.1 us)
Async XLA Ops:
  7.2 4.9 copy-start
  7.2 462.2 %all-reduce.3.cloned.1.call-start = ((), (), s32[]{:S(2)}) async-start(), calls=%async_computation | async-start | bytes 1769472 | tf_op jit(solution)/shard_map/psum | solution.py:26
  289.2 637.0 %all-reduce.5.cloned.1.call-start = ((), (), s32[]{:S(2)}) async-start(), calls=%async_computation.1 | async-start | bytes 1769472 | tf_op jit(solution)/shard_map/psum | solution.py:26
  927.4 7.3 copy-start.1
Sparse Core Ops, SparseCore 0:
  289.3 179.9 all-reduce.2
  746.1 180.0 all-reduce.4
where the time goes:
time: 944 us; the launch traced here: 942 us
  blocking collectives  524 us (56%)
  waiting for transfers between devices  360 us (38%)
  other arithmetic  37.2 us (4%)
  between operations  14.2 us (2%)
    psum x2, blocking collectives, per_device(): gram = lax.psum(local_gram, 'dp')  497 us
    psum x2, waiting for transfers between devices, per_device(): q_now = lax.psum(partial_q, 'dp') / replicas  360 us
    psum x2, blocking collectives, per_device(): p_mean = lax.psum(partial_p, 'tensor') / replicas  27.7 us
  transfers between devices with their start and end apart: 2, of which 2 were waited for; matrix products, arithmetic and copies ran while one was open for 0% of the time, Pallas kernels for 0%

commit v1 on v0

v1 whole, which is shorter than its diff:
```python
import functools

import jax
import jax.numpy as jnp
from jax import lax
from jax.experimental import pallas as pl
from jax.experimental.pallas import tpu as pltpu
from jax.sharding import Mesh
from jax.sharding import PartitionSpec as P

X, Z, CORES, Y = 4, 8, 2, 4
PEERS = X * Z
LANES = 128
F32, BF16 = jnp.float32, jnp.bfloat16
HIGH = lax.Precision.HIGHEST
VMEM = pl.BlockSpec(memory_space=pltpu.VMEM)
SMEM = pl.BlockSpec(memory_space=pltpu.SMEM)


def split(value):
    high = value.astype(BF16)
    return high, (value - high.astype(F32)).astype(BF16)


def dot(a, b, contract=((1,), (0,)), precision=None):
    return lax.dot_general(a, b, (contract, ((), ())), precision=precision, preferred_element_type=F32)


def params(mib, **more):
    return pltpu.CompilerParams(vmem_limit_bytes=mib << 20, **more)


def start_kernel(g_ref, e_ref, q_ref, corrected_ref, high_ref, low_ref, p_ref):
    replicas = g_ref.shape[0]
    total = jnp.zeros(g_ref.shape[1:], F32)
    for index in range(replicas):
        corrected = (g_ref[index].astype(F32) + e_ref[index].astype(F32)).astype(BF16)
        corrected_ref[index] = corrected
        total = total + corrected.astype(F32)
    high, low = split(total * (1.0 / replicas))
    high_ref[...] = high
    low_ref[...] = low
    term = dot(high, q_ref[...]) + dot(low, q_ref[...])

    @pl.when(pl.program_id(0) == 0)
    def _():
        p_ref[...] = term

    @pl.when(pl.program_id(0) > 0)
    def _():
        p_ref[...] += term


def start(gradient, error, q_start, width=384):
    replicas, rows, columns = gradient.shape
    rank = q_start.shape[1]
    wide = pl.BlockSpec((replicas, rows, width), lambda j: (0, 0, j))
    flat = pl.BlockSpec((rows, width), lambda j: (0, j))
    return pl.pallas_call(
        start_kernel,
        grid=(columns // width,),
        in_specs=[wide, wide, pl.BlockSpec((width, rank), lambda j: (j, 0))],
        out_specs=[wide, flat, flat, pl.BlockSpec((rows, rank), lambda j: (0, 0))],
        out_shape=[
            jax.ShapeDtypeStruct(gradient.shape, BF16),
            jax.ShapeDtypeStruct((rows, columns), BF16),
            jax.ShapeDtypeStruct((rows, columns), BF16),
            jax.ShapeDtypeStruct((rows, rank), F32),
        ],
        compiler_params=params(24),
    )(gradient, error, q_start)


def right_kernel(blocks, normed, core_ref, *refs):
    if normed:
        inverse_ref, *refs = refs
    own, one, two, three, high_ref, low_ref, mine_ref, theirs_ref, p_ref = refs
    p = (own[...] + two[...]) + (one[...] + three[...])
    if normed:
        p = dot(p, inverse_ref[...], ((1,), (1,)), HIGH)
    p_ref[...] = p
    rank = p.shape[1]
    half = rank // 2
    first = core_ref[0] == 0
    turned = p.T
    p_high, p_low = split(turned)
    both = jnp.concatenate([p_high, p_low], axis=0)
    for block in range(blocks):
        at = pl.ds(block * LANES, LANES)
        wide = dot(both, high_ref[:, at])
        u = wide[:rank] + (wide[rank:] + dot(p_high, low_ref[:, at]))
        mine_ref[block] = jnp.where(first, u[:half], u[half:])
        theirs_ref[block] = jnp.where(first, u[half:], u[:half])
    gram = dot(turned, p, ((1,), (0,)), HIGH)
    gram = jnp.concatenate([gram, jnp.zeros((rank, LANES - rank), F32)], axis=1)
    mine_ref[blocks] = jnp.where(first, gram[:half], gram[half:])
    theirs_ref[blocks] = jnp.where(first, gram[half:], gram[:half])


def right(core, parts, high, low, inverse=None):
    rows, columns = high.shape
    rank = parts[0].shape[1]
    blocks = columns // LANES
    shape = jax.ShapeDtypeStruct((blocks + 1, rank // 2, LANES), F32)
    operands = ([] if inverse is None else [inverse]) + list(parts) + [high, low]
    return pl.pallas_call(
        functools.partial(right_kernel, blocks, inverse is not None),
        in_specs=[SMEM] + [VMEM] * len(operands),
        out_specs=[VMEM] * 3,
        out_shape=[shape, shape, jax.ShapeDtypeStruct((rows, rank), F32)],
        compiler_params=params(24),
    )(core, *operands)


def add_kernel(a_ref, b_ref, out_ref):
    blocks = a_ref.shape[0]
    out_ref[:blocks] = a_ref[...] + b_ref[...]
    out_ref[blocks:] = jnp.zeros((out_ref.shape[0] - blocks,) + out_ref.shape[1:], F32)


def sum_kernel(in_ref, out_ref):
    total = in_ref[0]
    for peer in range(1, in_ref.shape[0]):
        total = total + in_ref[peer]
    for peer in range(out_ref.shape[0]):
        out_ref[peer] = total


def all_sum(mine, theirs):
    arrived = lax.ppermute(theirs, "core", [(0, 1), (1, 0)])
    shape = jax.ShapeDtypeStruct((PEERS,) + mine.shape[1:], F32)
    terms = pl.pallas_call(
        add_kernel, in_specs=[VMEM] * 2, out_specs=VMEM, out_shape=shape, compiler_params=params(8)
    )(mine, arrived)
    terms = lax.all_to_all(terms, ("x", "z"), 0, 0)
    sums = pl.pallas_call(
        sum_kernel, in_specs=[VMEM], out_specs=VMEM, out_shape=shape, compiler_params=params(8)
    )(terms)
    here = lax.all_to_all(sums, ("x", "z"), 0, 0)
    return here, lax.ppermute(here, "core", [(0, 1), (1, 0)])


def whole(first, a, b):
    return jnp.concatenate([jnp.where(first, a, b), jnp.where(first, b, a)], axis=0)


def left_kernel(core_ref, a_ref, b_ref, high_ref, low_ref, t_ref, gram_ref, u_ref):
    rank = gram_ref.shape[0]
    blocks = high_ref.shape[1] // LANES
    first = core_ref[0] == 0
    gram_ref[...] = whole(first, a_ref[blocks], b_ref[blocks])[:, :rank]
    for block in range(blocks):
        u_high, u_low = split(whole(first, a_ref[block], b_ref[block]))
        u_ref[:, pl.ds(block * LANES, LANES)] = jnp.concatenate([u_high, u_low], axis=0)
    wide = dot(high_ref[...], u_ref[...], ((1,), (1,)))
    t_ref[...] = wide[:, :rank] + (wide[:, rank:] + dot(low_ref[...], u_ref[:rank], ((1,), (1,))))


def left(core, a, b, high, low):
    rows, columns = high.shape
    rank = 2 * a.shape[1]
    return pl.pallas_call(
        left_kernel,
        in_specs=[SMEM] + [VMEM] * 4,
        out_specs=[VMEM] * 2,
        out_shape=[jax.ShapeDtypeStruct((rows, rank), F32), jax.ShapeDtypeStruct((rank, rank), F32)],
        scratch_shapes=[pltpu.VMEM((2 * rank, columns), BF16)],
        compiler_params=params(24),
    )(core, a, b, high, low)


def lower_inverse(gram):
    rank = gram.shape[0]
    at_row = lax.broadcasted_iota(jnp.int32, (rank, rank), 0)
    at_col = lax.broadcasted_iota(jnp.int32, (rank, rank), 1)
    work = jnp.concatenate([gram, (at_row == at_col).astype(F32)], axis=1)
    done = []
    for step in range(rank):
        low = step // 8 * 8
        here = work[low:]
        column = jnp.broadcast_to(here[:, step : step + 1], here.shape)
        at = step - low
        pivot = column[at : at + 1]
        row = here[at : at + 1]
        scale = lax.rsqrt(pivot)
        done.append((row * scale)[:, rank:])
        work = work[low:] - column * (row * (scale * scale)) if low == 0 else jnp.concatenate(
            [work[:low], here - column * (row * (scale * scale))], axis=0
        )
    return jnp.concatenate(done, axis=0)


def inverse_kernel(gram_ref, out_ref):
    out_ref[...] = lower_inverse(gram_ref[...])


def inverse_of(gram):
    return pl.pallas_call(
        inverse_kernel,
        in_specs=[VMEM],
        out_specs=VMEM,
        out_shape=jax.ShapeDtypeStruct(gram.shape, F32),
        compiler_params=params(4),
        cost_estimate=pl.CostEstimate(flops=10_000_000, bytes_accessed=5_000_000, transcendentals=0),
    )(gram)


def end_kernel(core_ref, a_ref, b_ref, p_ref, corrected_ref, new_ref, q_ref, inverse_ref, half_ref):
    rank = p_ref.shape[1]
    first = core_ref[0] == 0
    per = corrected_ref.shape[2] // LANES
    step = pl.program_id(0)
    last = pl.num_programs(0) * per

    @pl.when(step == 0)
    def _():
        inverse_ref[...] = lower_inverse(whole(first, a_ref[last], b_ref[last])[:, :rank])
        half_ref[...] = dot(p_ref[...], inverse_ref[...], ((1,), (1,)), HIGH).astype(BF16)

    for index in range(per):
        block = step * per + index
        u = whole(first, a_ref[block], b_ref[block])
        q = dot(inverse_ref[...], u, ((1,), (0,)), HIGH)
        q_ref[pl.ds(index * LANES, LANES), :] = q.T
        recon = dot(half_ref[...], q.astype(BF16))
        at = pl.ds(index * LANES, LANES)
        for replica in range(corrected_ref.shape[0]):
            new_ref[replica, :, at] = (corrected_ref[replica, :, at].astype(F32) - recon).astype(BF16)


def end(core, a, b, p, corrected, width=384):
    replicas, rows, columns = corrected.shape
    rank = p.shape[1]
    wide = pl.BlockSpec((replicas, rows, width), lambda j: (0, 0, j))
    return pl.pallas_call(
        end_kernel,
        grid=(columns // width,),
        in_specs=[SMEM, VMEM, VMEM, VMEM, wide],
        out_specs=[wide, pl.BlockSpec((width, rank), lambda j: (j, 0))],
        out_shape=[
            jax.ShapeDtypeStruct(corrected.shape, BF16),
            jax.ShapeDtypeStruct((columns, rank), F32),
        ],
        scratch_shapes=[pltpu.VMEM((rank, rank), F32), pltpu.VMEM((rows, rank), BF16)],
        compiler_params=params(24),
    )(core, a, b, p, corrected)


def around(value):
    return [value] + [lax.ppermute(value, "y", [(i, (i + k) % Y) for i in range(Y)]) for k in range(1, Y)]


def per_device(gradient, error_buffer, q_start):
    core = lax.axis_index("core").astype(jnp.int32).reshape(1)
    corrected, high, low, term = start(gradient, error_buffer, q_start)
    mine, theirs, _ = right(core, around(term), high, low)
    a, b = all_sum(mine, theirs)
    term, gram = left(core, a, b, high, low)
    parts = around(term)
    mine, theirs, p = right(core, parts, high, low, inverse_of(gram))
    a, b = all_sum(mine, theirs)
    return tuple(end(core, a, b, p, corrected))


def solution(mesh):
    fine = Mesh(mesh.devices.reshape(X, Z, CORES, Y), ("x", "z", "core", "y"))
    rows = ("x", "z", "core")
    return jax.shard_map(
        per_device,
        mesh=fine,
        in_specs=(P(None, rows, "y"), P(None, rows, "y"), P("y", None)),
        out_specs=(P(None, rows, "y"), P("y", None)),
        check_vma=False,
    )
```

time: 944 us -> 153 us (0.16)
  blocking collectives: 524 us -> 88.2 us
  waiting for transfers between devices: 360 us -> 9.78 us
  other arithmetic: 37.2 us -> 0.01 us
  Pallas kernels: 0 us -> 26.5 us
  starting transfers between devices: 0.08 us -> 18.3 us
  between operations: 14.2 us -> 0.73 us
    psum x4 -> x0, blocking collectives: 524 us -> none  [the longest x2 497 us: per_device(): gram = lax.psum(local_gram, 'dp')]
    psum x2 -> x0, waiting for transfers between devices: 360 us -> none  [per_device(): q_now = lax.psum(partial_q, 'dp') / replicas]
    all_to_all x0 -> x4, blocking collectives: none -> 88.2 us  [the longest x2 44.3 us: all_sum(): terms = lax.all_to_all(terms, ('x', 'z'), 0, 0)]
    pallas_call x0 -> x10, Pallas kernels: none -> 26.5 us  [the longest x1 13.3 us: end(): pl.pallas_call(end_kernel, grid=(columns // width,), in_specs=[SMEM, VMEM...]
    another operation x10 -> x0, other arithmetic: 24.1 us -> none  [the longest x6 13 us: per_device(): lower = jnp.linalg.cholesky(gram)]
    ppermute x0 -> x10, starting transfers between devices: none -> 18.3 us  [the longest x2 8.06 us: all_sum(): return (here, lax.ppermute(here, 'core', [(0, 1), (1, 0)]))]
    ppermute x0 -> x10, waiting for transfers between devices: none -> 9.78 us  [the longest x6 3.82 us: around(): lax.ppermute(value, 'y', [(i, (i + k) % Y) for i in range(Y)])]
  transfers between devices with their start and end apart: 2 -> 10, of which waited for: 2 -> 8; matrix products, arithmetic and copies ran while one was open for 0% -> 0% of each run, Pallas kernels for 0% -> 4%
where the time goes in v1:
time: 153 us
  blocking collectives  88.2 us (58%)
  Pallas kernels  26.5 us (17%)
  starting transfers between devices  18.3 us (12%)
  waiting for transfers between devices  9.78 us (6%)
  local copies, waits for them, and re-layouts  9.46 us (6%)
    all_to_all x2, blocking collectives, all_sum(): terms = lax.all_to_all(terms, ('x', 'z'), 0, 0)  44.3 us
    all_to_all x2, blocking collectives, all_sum(): here = lax.all_to_all(sums, ('x', 'z'), 0, 0)  44 us
    pallas_call x1, Pallas kernels, end(): pl.pallas_call(end_kernel, grid=(columns // width,), in_specs=[SMEM, VMEM...  13.3 us
    ppermute x2, starting transfers between devices, all_sum(): return (here, lax.ppermute(here, 'core', [(0, 1), (1, 0)]))  8.06 us
    unnamed x11, local copies, waits for them, and re-layouts  8.02 us
    ppermute x6, starting transfers between devices, around(): lax.ppermute(value, 'y', [(i, (i + k) % Y) for i in range(Y)])  6.85 us
    pallas_call x1, Pallas kernels, inverse_of(): pl.pallas_call(inverse_kernel, in_specs=[VMEM], out_specs=VMEM, out_shape...  5.46 us
    pallas_call x1, Pallas kernels, start(): pl.pallas_call(start_kernel, grid=(columns // width,), in_specs=[wide, wi...  4.98 us
  transfers between devices with their start and end apart: 10, of which 8 were waited for; matrix products, arithmetic and copies ran while one was open for 0% of the time, Pallas kernels for 4%

profile of v1, /device:TPU:1, one launch (start us, length us, event | category | flops | bytes accessed | tf_op | source)
XLA Modules:
  0.0 152.9 jit_solution(10028353089369844344)
XLA Ops:
  0.6 1.4 copy.5.q_ref
  2.1 0.0 copy-start
  2.1 2.2 %copy-done = bf16[8,80,3456]{2,1,0:T(8,128)(2,1)S(1)} copy-done((bf16[8,80,3456]{2,1,0:T(8,128)(2,1)S(1)}, bf16[8,80,3456]{2,1,0:T(8,128)(2,1)}, u32[]{:S(2)}) %copy-start) | copy-done | bytes 4423704
  4.3 0.0 copy-start.1
  4.3 2.3 %copy-done.1 = bf16[8,80,3456]{2,1,0:T(8,128)(2,1)S(1)} copy-done((bf16[8,80,3456]{2,1,0:T(8,128)(2,1)S(1)}, bf16[8,80,3456]{2,1,0:T(8,128)(2,1)}, u32[]{:S(2)}) %copy-start.1) | copy-done | bytes 4423704
  6.6 5.0 %shard_map.50 = (bf16[8,80,3456]{2,1,0:T(8,128)(2,1)S(1)}, bf16[80,3456]{1,0:T(8,128)(2,1)S(1)}, bf16[80,3456]{1,0:T(8,128)(2,1)S(1)}, f32[80,64]{1,0:T(8,128)S(1)}) custom-call(bf16[8,80,3456]{2,1,0:T(8,128)(2,1)S(1)} %copy-done, bf16[8,80,3456]{2,1,0:T(8,128)(2,1)S(1)} %copy-done.1, bf16[3456,64]{1,0:T(8,128)(2,1)S(1)} %copy.5.q_ref), custom_call_target="tpu_custom_call" | custom-call | tf_op jit(solution)/shard_map/pallas_call | solution.py:59
  11.6 0.0 copy-start.2
  11.6 2.1 %copy-done.2 = bf16[8,80,3456]{2,1,0:T(8,128)(2,1)} copy-done((bf16[8,80,3456]{2,1,0:T(8,128)(2,1)}, bf16[8,80,3456]{2,1,0:T(8,128)(2,1)S(1)}, u32[]{:S(2)}) %copy-start.2) | copy-done | bytes 4423704
  13.7 3.6 %collective-permute-start.2 = (f32[80,64]{1,0:T(8,128)S(1)}, f32[80,64]{1,0:T(8,128)S(1)}, u32[]{:S(2)}, u32[]{:S(2)}) collective-permute-start(f32[80,64]{1,0:T(8,128)S(1)} %get-tuple-element.13.refs_0_), channel_id=1, source_target_pairs={{0,3},{1,0},{2,1},{3,2},{4,7},{5,4},{6,5},{7,6},{8,11},{9,8},{10,9... | collective-permute-start | bytes 61448 | tf_op jit(solution)/shard_map/ppermute | solution.py:250
  17.2 0.3 collective-permute-start.1
  17.6 0.7 collective-permute-start
  18.3 0.1 collective-permute-done.2.refs_3_
  18.3 3.3 %collective-permute-done.1.refs_2_ = f32[80,64]{1,0:T(8,128)S(1)} collective-permute-done((f32[80,64]{1,0:T(8,128)S(1)}, f32[80,64]{1,0:T(8,128)S(1)}, u32[]{:S(2)}, u32[]{:S(2)}) %collective-permute-start.1) | collective-permute-done | bytes 20512 | tf_op jit(solution)/shard_map/ppermute | solution.py:250
  21.6 0.4 collective-permute-done.refs_1_
  22.0 0.8 shard_map.51
  22.8 2.1 %collective-permute-start.3 = (f32[28,32,128]{2,1,0:T(8,128)S(1)}, f32[28,32,128]{2,1,0:T(8,128)S(1)}, u32[]{:S(2)}, u32[]{:S(2)}) collective-permute-start(f32[28,32,128]{2,1,0:T(8,128)S(1)} %get-tuple-element.17), channel_id=1, source_target_pairs={{0,4},{4,0},{1,5},{5,1},{2,6},{6,2},{3,7},{7,3},{8,12},{12,8},{9,1... | collective-permute-start | bytes 1376264 | tf_op jit(solution)/shard_map/ppermute | solution.py:130
  24.9 1.4 collective-permute-done.3.b_ref
  26.3 0.0 slice-start
  26.3 0.1 shard_map.52
  26.4 25.2 %all_to_all.20.in_ref = f32[32,32,128]{2,1,0:T(8,128)S(1)} all-to-all(f32[32,32,128]{2,1,0:T(8,128)S(1)} %shard_map.52), channel_id=1, replica_groups=mesh['x'=4,'z'=8,'core'=2,'y'=4] {'x','z'}, dimensions={0} | all-to-all | bytes 1048576 | tf_op jit(solution)/shard_map/all_to_all | solution.py:135
  51.6 0.1 shard_map.53
  51.7 22.0 %all_to_all.21.a_ref = f32[32,32,128]{2,1,0:T(8,128)S(1)} all-to-all(f32[32,32,128]{2,1,0:T(8,128)S(1)} %shard_map.53), channel_id=1, replica_groups=mesh['x'=4,'z'=8,'core'=2,'y'=4] {'x','z'}, dimensions={0} | all-to-all | bytes 1048576 | tf_op jit(solution)/shard_map/all_to_all | solution.py:139
  73.7 0.0 slice-start.1
  73.7 4.0 %collective-permute-start.4 = (f32[32,32,128]{2,1,0:T(8,128)S(1)}, f32[32,32,128]{2,1,0:T(8,128)S(1)}, u32[]{:S(2)}, u32[]{:S(2)}) collective-permute-start(f32[32,32,128]{2,1,0:T(8,128)S(1)} %all_to_all.21.a_ref), channel_id=1, source_target_pairs={{0,4},{4,0},{1,5},{5,1},{2,6},{6,2},{3,7},{7,3},{8,12},{12,8},{9,1... | collective-permute-start | bytes 1572872 | tf_op jit(solution)/shard_map/ppermute | solution.py:140
  77.7 1.5 %collective-permute-done.4.b_ref = f32[32,32,128]{2,1,0:T(8,128)S(1)} collective-permute-done((f32[32,32,128]{2,1,0:T(8,128)S(1)}, f32[32,32,128]{2,1,0:T(8,128)S(1)}, u32[]{:S(2)}, u32[]{:S(2)}) %collective-permute-start.4) | collective-permute-done | bytes 524320 | tf_op jit(solution)/shard_map/ppermute | solution.py:140
  79.3 0.8 shard_map.54
  80.0 0.4 collective-permute-start.7
  80.4 1.1 collective-permute-start.6
  81.5 0.8 collective-permute-start.5
  82.3 5.5 %shard_map.55.refs_0_ = f32[64,64]{1,0:T(8,128)S(1)} custom-call(f32[64,64]{1,0:T(8,128)S(1)} %get-tuple-element.18.gram_ref), custom_call_target="tpu_custom_call" | custom-call | flops 10000000 | bytes 5000000 | tf_op jit(solution)/shard_map/pallas_call | solution.py:198
  87.8 0.0 collective-permute-done.7.refs_4_
  87.8 0.0 collective-permute-done.6.refs_3_
  87.8 0.1 collective-permute-done.5.refs_2_
  87.8 0.9 shard_map.56
  88.7 1.3 collective-permute-start.8
  90.0 1.4 collective-permute-done.8.b_ref
  91.5 0.1 shard_map.57
  91.5 19.0 %all_to_all.22.in_ref = f32[32,32,128]{2,1,0:T(8,128)S(1)} all-to-all(f32[32,32,128]{2,1,0:T(8,128)S(1)} %shard_map.57), channel_id=1, replica_groups=mesh['x'=4,'z'=8,'core'=2,'y'=4] {'x','z'}, dimensions={0} | all-to-all | bytes 1048576 | tf_op jit(solution)/shard_map/all_to_all | solution.py:135
  110.5 0.1 shard_map.58
  110.6 22.0 %all_to_all.23.a_ref = f32[32,32,128]{2,1,0:T(8,128)S(1)} all-to-all(f32[32,32,128]{2,1,0:T(8,128)S(1)} %shard_map.58), channel_id=1, replica_groups=mesh['x'=4,'z'=8,'core'=2,'y'=4] {'x','z'}, dimensions={0} | all-to-all | bytes 1048576 | tf_op jit(solution)/shard_map/all_to_all | solution.py:139
  132.6 4.0 %collective-permute-start.9 = (f32[32,32,128]{2,1,0:T(8,128)S(1)}, f32[32,32,128]{2,1,0:T(8,128)S(1)}, u32[]{:S(2)}, u32[]{:S(2)}) collective-permute-start(f32[32,32,128]{2,1,0:T(8,128)S(1)} %all_to_all.23.a_ref), channel_id=1, source_target_pairs={{0,4},{4,0},{1,5},{5,1},{2,6},{6,2},{3,7},{7,3},{8,12},{12,8},{9,1... | collective-permute-start | bytes 1572872 | tf_op jit(solution)/shard_map/ppermute | solution.py:140
  136.6 1.5 %collective-permute-done.9.b_ref = f32[32,32,128]{2,1,0:T(8,128)S(1)} collective-permute-done((f32[32,32,128]{2,1,0:T(8,128)S(1)}, f32[32,32,128]{2,1,0:T(8,128)S(1)}, u32[]{:S(2)}, u32[]{:S(2)}) %collective-permute-start.9) | collective-permute-done | bytes 524320 | tf_op jit(solution)/shard_map/ppermute | solution.py:140
  138.2 0.0 slice-done
  138.2 0.0 slice-done.1
  138.2 13.3 %shard_map.59 = (bf16[8,80,3456]{2,1,0:T(8,128)(2,1)}, f32[3456,64]{1,0:T(8,128)S(1)}) custom-call(s32[1]{0:T(128)} %bitcast.core_ref, f32[32,32,128]{2,1,0:T(8,128)S(1)} %all_to_all.23.a_ref, f32[32,32,128]{2,1,0:T(8,128)S(1)} %collective-permute-done.9.b_ref, f32[80,64]{1,0:T(8,128)S(1)} %get-tuple-element.22.p_ref, bf16[8,80,3456]{2,1,0:T(8,128)(2,1)S(1)} %bitcast.2), custom_call_target="tpu_custom_call" | custom-call | tf_op jit(solution)/shard_map/pallas_call | solution.py:235
  151.5 1.4 copy.6
  (1 shorter events, 0.0 us)
Async XLA Ops:
  2.1 2.3 %copy-start = (bf16[8,80,3456]{2,1,0:T(8,128)(2,1)S(1)}, bf16[8,80,3456]{2,1,0:T(8,128)(2,1)}, u32[]{:S(2)}) copy-start(bf16[8,80,3456]{2,1,0:T(8,128)(2,1)} %g_ref.1) | copy-start | bytes 13271044
  4.3 2.3 %copy-start.1 = (bf16[8,80,3456]{2,1,0:T(8,128)(2,1)S(1)}, bf16[8,80,3456]{2,1,0:T(8,128)(2,1)}, u32[]{:S(2)}) copy-start(bf16[8,80,3456]{2,1,0:T(8,128)(2,1)} %e_ref.1) | copy-start | bytes 13271044
  11.6 2.1 %copy-start.2 = (bf16[8,80,3456]{2,1,0:T(8,128)(2,1)}, bf16[8,80,3456]{2,1,0:T(8,128)(2,1)S(1)}, u32[]{:S(2)}) copy-start(bf16[8,80,3456]{2,1,0:T(8,128)(2,1)S(1)} %get-tuple-element.23.corrected_ref) | copy-start | bytes 13271044
  13.7 4.7 %collective-permute-start.2 = (f32[80,64]{1,0:T(8,128)S(1)}, f32[80,64]{1,0:T(8,128)S(1)}, u32[]{:S(2)}, u32[]{:S(2)}) collective-permute-start(f32[80,64]{1,0:T(8,128)S(1)} %get-tuple-element.13.refs_0_), channel_id=1, source_target_pairs={{0,3},{1,0},{2,1},{3,2},{4,7},{5,4},{6,5},{7,6},{8,11},{9,8},{10,9... | collective-permute-start | bytes 61448 | tf_op jit(solution)/shard_map/ppermute | solution.py:250
  17.2 4.4 %collective-permute-start.1 = (f32[80,64]{1,0:T(8,128)S(1)}, f32[80,64]{1,0:T(8,128)S(1)}, u32[]{:S(2)}, u32[]{:S(2)}) collective-permute-start(f32[80,64]{1,0:T(8,128)S(1)} %get-tuple-element.13.refs_0_), channel_id=1, source_target_pairs={{0,2},{1,3},{2,0},{3,1},{4,6},{5,7},{6,4},{7,5},{8,10},{9,11},{10,... | collective-permute-start | bytes 61448 | tf_op jit(solution)/shard_map/ppermute | solution.py:250
  17.6 4.4 %collective-permute-start = (f32[80,64]{1,0:T(8,128)S(1)}, f32[80,64]{1,0:T(8,128)S(1)}, u32[]{:S(2)}, u32[]{:S(2)}) collective-permute-start(f32[80,64]{1,0:T(8,128)S(1)} %get-tuple-element.13.refs_0_), channel_id=1, source_target_pairs={{0,1},{1,2},{2,3},{3,0},{4,5},{5,6},{6,7},{7,4},{8,9},{9,10},{10,1... | collective-permute-start | bytes 61448 | tf_op jit(solution)/shard_map/ppermute | solution.py:250
  22.8 3.5 %collective-permute-start.3 = (f32[28,32,128]{2,1,0:T(8,128)S(1)}, f32[28,32,128]{2,1,0:T(8,128)S(1)}, u32[]{:S(2)}, u32[]{:S(2)}) collective-permute-start(f32[28,32,128]{2,1,0:T(8,128)S(1)} %get-tuple-element.17), channel_id=1, source_target_pairs={{0,4},{4,0},{1,5},{5,1},{2,6},{6,2},{3,7},{7,3},{8,12},{12,8},{9,1... | collective-permute-start | bytes 1376264 | tf_op jit(solution)/shard_map/ppermute | solution.py:130
  26.3 111.8 %slice-start = ((s8[4423680]{0:T(1024)(128)(4,1)}), s8[4194304]{0:T(1024)(128)(4,1)S(1)}, s32[]{:S(2)}) async-start(s8[4423680]{0:T(1024)(128)(4,1)} %bitcast.1), calls=%async_computation.4 | async-start | bytes 8388608
  73.7 64.5 %slice-start.1 = ((s8[4423680]{0:T(1024)(128)(4,1)}), s8[229376]{0:T(1024)(128)(4,1)S(1)}, s32[]{:S(2)}) async-start(s8[4423680]{0:T(1024)(128)(4,1)} %bitcast.1), calls=%async_computation.5 | async-start | bytes 458752
  73.7 5.6 %collective-permute-start.4 = (f32[32,32,128]{2,1,0:T(8,128)S(1)}, f32[32,32,128]{2,1,0:T(8,128)S(1)}, u32[]{:S(2)}, u32[]{:S(2)}) collective-permute-start(f32[32,32,128]{2,1,0:T(8,128)S(1)} %all_to_all.21.a_ref), channel_id=1, source_target_pairs={{0,4},{4,0},{1,5},{5,1},{2,6},{6,2},{3,7},{7,3},{8,12},{12,8},{9,1... | collective-permute-start | bytes 1572872 | tf_op jit(solution)/shard_map/ppermute | solution.py:140
  80.0 7.7 %collective-permute-start.7 = (f32[80,64]{1,0:T(8,128)S(1)}, f32[80,64]{1,0:T(8,128)S(1)}, u32[]{:S(2)}, u32[]{:S(2)}) collective-permute-start(f32[80,64]{1,0:T(8,128)S(1)} %get-tuple-element.19.refs_1_), channel_id=1, source_target_pairs={{0,3},{1,0},{2,1},{3,2},{4,7},{5,4},{6,5},{7,6},{8,11},{9,8},{10,9... | collective-permute-start | bytes 61448 | tf_op jit(solution)/shard_map/ppermute | solution.py:250
  80.4 7.4 %collective-permute-start.6 = (f32[80,64]{1,0:T(8,128)S(1)}, f32[80,64]{1,0:T(8,128)S(1)}, u32[]{:S(2)}, u32[]{:S(2)}) collective-permute-start(f32[80,64]{1,0:T(8,128)S(1)} %get-tuple-element.19.refs_1_), channel_id=1, source_target_pairs={{0,2},{1,3},{2,0},{3,1},{4,6},{5,7},{6,4},{7,5},{8,10},{9,11},{10,... | collective-permute-start | bytes 61448 | tf_op jit(solution)/shard_map/ppermute | solution.py:250
  81.5 6.3 %collective-permute-start.5 = (f32[80,64]{1,0:T(8,128)S(1)}, f32[80,64]{1,0:T(8,128)S(1)}, u32[]{:S(2)}, u32[]{:S(2)}) collective-permute-start(f32[80,64]{1,0:T(8,128)S(1)} %get-tuple-element.19.refs_1_), channel_id=1, source_target_pairs={{0,1},{1,2},{2,3},{3,0},{4,5},{5,6},{6,7},{7,4},{8,9},{9,10},{10,1... | collective-permute-start | bytes 61448 | tf_op jit(solution)/shard_map/ppermute | solution.py:250
  88.7 2.7 %collective-permute-start.8 = (f32[28,32,128]{2,1,0:T(8,128)S(1)}, f32[28,32,128]{2,1,0:T(8,128)S(1)}, u32[]{:S(2)}, u32[]{:S(2)}) collective-permute-start(f32[28,32,128]{2,1,0:T(8,128)S(1)} %get-tuple-element.21), channel_id=1, source_target_pairs={{0,4},{4,0},{1,5},{5,1},{2,6},{6,2},{3,7},{7,3},{8,12},{12,8},{9,1... | collective-permute-start | bytes 1376264 | tf_op jit(solution)/shard_map/ppermute | solution.py:130
  132.6 5.6 %collective-permute-start.9 = (f32[32,32,128]{2,1,0:T(8,128)S(1)}, f32[32,32,128]{2,1,0:T(8,128)S(1)}, u32[]{:S(2)}, u32[]{:S(2)}) collective-permute-start(f32[32,32,128]{2,1,0:T(8,128)S(1)} %all_to_all.23.a_ref), channel_id=1, source_target_pairs={{0,4},{4,0},{1,5},{5,1},{2,6},{6,2},{3,7},{7,3},{8,12},{12,8},{9,1... | collective-permute-start | bytes 1572872 | tf_op jit(solution)/shard_map/ppermute | solution.py:140

commit v2 on v0

v2 whole, which is shorter than its diff:
```python
import functools

import jax
import jax.numpy as jnp
from jax import lax
from jax.experimental import pallas as pl
from jax.experimental.pallas import tpu as pltpu
from jax.sharding import Mesh
from jax.sharding import PartitionSpec as P

X, FAR, NEAR, CORES, Y = 4, 4, 2, 2, 4
LANES = 128
F32, BF16 = jnp.float32, jnp.bfloat16
HIGH = lax.Precision.HIGHEST
VMEM = pl.BlockSpec(memory_space=pltpu.VMEM)
SMEM = pl.BlockSpec(memory_space=pltpu.SMEM)


def split(value, parts):
    found = []
    for _ in range(parts):
        found.append(value.astype(BF16))
        value = value - found[-1].astype(F32)
    return found


def dot(a, b, contract=((1,), (0,)), precision=None):
    return lax.dot_general(a, b, (contract, ((), ())), precision=precision, preferred_element_type=F32)


def params(mib, **more):
    return pltpu.CompilerParams(vmem_limit_bytes=mib << 20, **more)


def start_kernel(height, g_ref, e_ref, q_ref, high_ref, low_ref, p_ref, g_near, e_near, q_near, sems, q_sem):
    replicas, rows, columns = g_ref.shape
    steps = rows // height
    copies = []
    for index in range(steps):
        at = (slice(None), pl.ds(index * height, height))
        copies.append([
            pltpu.make_async_copy(far.at[at], near.at[at], sems.at[which, index])
            for which, (far, near) in enumerate([(g_ref, g_near), (e_ref, e_near)])
        ])
        for copy in copies[-1]:
            copy.start()
        if index == 0:
            q_copy = pltpu.make_async_copy(q_ref, q_near, q_sem)
            q_copy.start()
    for index, pair in enumerate(copies):
        for copy in pair:
            copy.wait()
        row = pl.ds(index * height, height)
        for block in range(columns // LANES):
            at = pl.ds(block * LANES, LANES)
            total = (g_near[0, row, at] + e_near[0, row, at]).astype(F32)
            for replica in range(1, replicas):
                total = total + (g_near[replica, row, at] + e_near[replica, row, at]).astype(F32)
            high_ref[row, at], low_ref[row, at] = split(total * (1.0 / replicas), 2)
        if index >= steps - 2:
            if index == steps - 2:
                q_copy.wait()
                row = pl.ds(0, rows - height)
            both = jnp.concatenate([high_ref[row], low_ref[row]], axis=0)
            term = dot(both, q_near[...], ((1,), (1,)))
            p_ref[row] = term[: row.size] + term[row.size :]


def in_hbm(*values):
    return [pltpu.with_memory_space_constraint(value, pltpu.HBM) for value in values]


def start(gradient, error, q_turned, height=16):
    replicas, rows, columns = gradient.shape
    far = pl.BlockSpec(memory_space=pltpu.HBM)
    return pl.pallas_call(
        functools.partial(start_kernel, height),
        in_specs=[far] * 3,
        out_specs=[VMEM] * 3,
        out_shape=[
            jax.ShapeDtypeStruct((rows, columns), BF16),
            jax.ShapeDtypeStruct((rows, columns), BF16),
            jax.ShapeDtypeStruct((rows, q_turned.shape[0]), F32),
        ],
        scratch_shapes=[
            pltpu.VMEM(gradient.shape, BF16),
            pltpu.VMEM(error.shape, BF16),
            pltpu.VMEM(q_turned.shape, BF16),
            pltpu.SemaphoreType.DMA((2, rows // height)),
            pltpu.SemaphoreType.DMA,
        ],
        compiler_params=params(24),
    )(*in_hbm(gradient, error, q_turned))


def right_kernel(blocks, normed, core_ref, *refs):
    if normed:
        inverse_ref, *refs = refs
    own, one, two, three, high_ref, low_ref, mine_ref, theirs_ref, p_ref = refs
    p = (own[...] + two[...]) + (one[...] + three[...])
    if normed:
        p = dot(p, inverse_ref[...], ((1,), (1,)), HIGH)
    p_ref[...] = p
    rank = p.shape[1]
    half = rank // 2
    first = core_ref[0] == 0
    turned = p.T
    stack = jnp.concatenate(split(turned, 3), axis=0)
    for block in range(blocks):
        at = pl.ds(block * LANES, LANES)
        top = dot(stack, high_ref[:, at])
        low = dot(stack[: 2 * rank], low_ref[:, at])
        u = top[:rank] + ((top[rank : 2 * rank] + low[:rank]) + (top[2 * rank :] + low[rank:]))
        mine_ref[block] = jnp.where(first, u[:half], u[half:])
        theirs_ref[block] = jnp.where(first, u[half:], u[:half]).astype(theirs_ref.dtype)
    gram = dot(turned, p, ((1,), (0,)), HIGH)
    gram = jnp.concatenate([gram[:half], gram[half:]], axis=1)
    mine_ref[blocks] = gram
    if theirs_ref.dtype == F32:
        theirs_ref[blocks] = gram
    else:
        for index, part in enumerate(split(gram, 3)):
            theirs_ref[blocks + index] = part


def right(core, parts, high, low, inverse=None, kind=F32):
    rows, columns = high.shape
    rank = parts[0].shape[1]
    blocks = columns // LANES
    mine = jax.ShapeDtypeStruct((blocks + 1, rank // 2, LANES), F32)
    theirs = mine if kind == F32 else jax.ShapeDtypeStruct((blocks + 3, rank // 2, LANES), kind)
    operands = ([] if inverse is None else [inverse]) + list(parts) + [high, low]
    return pl.pallas_call(
        functools.partial(right_kernel, blocks, inverse is not None),
        in_specs=[SMEM] + [VMEM] * len(operands),
        out_specs=[VMEM] * 3,
        out_shape=[mine, theirs, jax.ShapeDtypeStruct((rows, rank), F32)],
        compiler_params=params(24),
    )(core, *operands)


def cut_kernel(x_ref, a_ref, b_ref, *out_refs):
    last = a_ref.shape[0] - 1
    per = out_refs[0].shape[0] - 1
    gram = a_ref[last] + b_ref[last]
    for flip, out_ref in enumerate(out_refs):
        at = pl.ds((x_ref[0] ^ flip) * per, per)
        out_ref[:per] = a_ref[at] + b_ref[at]
        out_ref[per] = gram


def four(refs, *at):
    own, one, two, three = [ref[at] if at else ref[...] for ref in refs]
    return (own + two) + (one + three)


def halve_kernel(near_ref, *refs):
    *in_refs, keep_ref, give_ref = refs
    rows = keep_ref.shape[1]
    place = near_ref[0] * rows
    keep_ref[...] = four(in_refs, slice(None), pl.ds(pl.multiple_of(place, rows), rows))
    give_ref[...] = four(in_refs, slice(None), pl.ds(pl.multiple_of(rows - place, rows), rows))


def two_kernel(a_ref, b_ref, out_ref):
    out_ref[...] = a_ref[...] + b_ref[...]


def four_kernel(*refs):
    refs[-1][...] = four(refs[:-1])


def join_kernel(near_ref, here_ref, there_ref, chunk_ref, gram_ref):
    per, rows = chunk_ref.shape[0], here_ref.shape[1]
    place = near_ref[0] * rows
    chunk_ref[:, pl.ds(pl.multiple_of(place, rows), rows)] = here_ref[:per]
    chunk_ref[:, pl.ds(pl.multiple_of(rows - place, rows), rows)] = there_ref[:per]
    first = near_ref[0] == 0
    here, there = here_ref[per], there_ref[per]
    packed = jnp.concatenate([jnp.where(first, here, there), jnp.where(first, there, here)], axis=0)
    half, rank = packed.shape[0], gram_ref.shape[0]
    gram_ref[:half] = packed[:, :rank]
    gram_ref[half:] = packed[:, rank:]


def small(kernel, operands, shapes, scalars=0, kind=F32, scratch=()):
    return pl.pallas_call(
        kernel,
        in_specs=[SMEM] * scalars + [VMEM] * (len(operands) - scalars),
        out_specs=[VMEM] * len(shapes),
        out_shape=[jax.ShapeDtypeStruct(shape, kind) for shape in shapes],
        scratch_shapes=scratch,
        compiler_params=params(8),
    )(*operands)


def pack(ref, u, gram):
    per = u.shape[0]
    ref[:per] = u.astype(BF16)
    parts = [part.astype(F32) for part in split(gram, 3)]
    spare = ref.shape[1] - 3 * gram.shape[0]
    ref[per] = jnp.concatenate(parts + [jnp.zeros((spare, LANES), F32)], axis=0).astype(BF16)


def unpack(ref):
    per, rows, _ = ref.shape
    block = ref[per - 1].astype(F32)
    part = rows // X
    return ref[: per - 1].astype(F32), block[:part] + (block[part : 2 * part] + block[2 * part : 3 * part])


def cut_coarse_kernel(x_ref, a_ref, b_ref, *refs):
    *out_refs, gram_ref = refs
    last = a_ref.shape[0] - 1
    per = out_refs[0].shape[0] - 1
    part = gram_ref.shape[0] // X
    gram = b_ref[last].astype(F32) + (b_ref[last + 1].astype(F32) + b_ref[last + 2].astype(F32))
    gram_ref[...] = a_ref[last] + gram
    for flip, out_ref in enumerate(out_refs):
        owner = x_ref[0] ^ flip
        at = pl.ds(owner * per, per)
        rows = pl.ds(pl.multiple_of(owner * part, part), part)
        pack(out_ref, a_ref[at] + b_ref[at].astype(F32), gram_ref[rows])


def sum_coarse_kernel(*refs):
    found = [unpack(ref) for ref in refs[:-1]]
    if len(found) == 4:
        found = [[a + b for a, b in zip(found[k], found[k + 2])] for k in range(2)]
    pack(refs[-1], *[a + b for a, b in zip(*found)])


def coarse_sum(place, mine, theirs):
    per, (rows, lanes) = mine.shape[0] // X, mine.shape[1:]
    shape = (per + 1, rows, lanes)
    scratch = [pltpu.VMEM((rows, lanes), F32)]
    cuts = small(cut_coarse_kernel, (place["x"], mine, swap(theirs, "core")), [shape] * X, 1, BF16, scratch)
    (part,) = small(sum_coarse_kernel, around(cuts, "x"), [shape], 0, BF16)
    (part,) = small(sum_coarse_kernel, (part, swap(part, "near")), [shape], 0, BF16)
    (part,) = small(sum_coarse_kernel, around(part, "far"), [shape], 0, BF16)
    here = around(part, "x")
    return here, [swap(part, "core") for part in here]


def around(value, axis):
    if not isinstance(value, (list, tuple)):
        value = [value] * 4
    return [value[0]] + [lax.ppermute(value[flip], axis, [(i, i ^ flip) for i in range(4)]) for flip in range(1, 4)]


def swap(value, axis):
    return lax.ppermute(value, axis, [(0, 1), (1, 0)])


def all_sum(place, mine, theirs, gradient, error):
    blocks, rows, lanes = mine.shape
    per = blocks // X
    full, half = (per + 1, rows, lanes), (per + 1, rows // 2, lanes)
    cuts = small(cut_kernel, (place["x"], mine, swap(theirs, "core")), [full] * X, 1)
    keep, give = small(halve_kernel, (place["near"], *around(cuts, "x")), [half] * 2, 1)
    (both,) = small(two_kernel, (keep, swap(give, "near")), [half])
    (total,) = small(four_kernel, around(both, "far"), [half])
    rank = 2 * rows
    chunk, gram = small(
        join_kernel, (place["near"], total, swap(total, "near")), [(per, rows, lanes), (rank, rank)], 1
    )
    ready = inverse_and_fetch(gram, gradient, error)
    here = around(chunk, "x")
    first = swap(here[0], "core")
    *ready, here[1], here[2], here[3] = lax.optimization_barrier([*ready, *here[1:]])
    return here, [first] + [swap(part, "core") for part in here[1:]], ready


def whole(first, a, b):
    return jnp.concatenate([jnp.where(first, a, b), jnp.where(first, b, a)], axis=0)


def gather(core_ref, x_ref, refs, u_ref, per):
    first = core_ref[0] == 0
    parts = u_ref.shape[0] // (2 * refs[0].shape[1])
    for flip in range(X):
        owner = x_ref[0] ^ flip
        a_ref, b_ref = refs[flip], refs[X + flip]
        for index in range(per):
            at = pl.ds(pl.multiple_of((owner * per + index) * LANES, LANES), LANES)
            u = whole(first, a_ref[index].astype(F32), b_ref[index].astype(F32))
            u_ref[:, at] = jnp.concatenate(split(u, parts), axis=0)


def left_kernel(core_ref, x_ref, *refs):
    *refs, high_ref, low_ref, t_ref, gram_ref, u_ref, packed_ref = refs
    rows, rank = t_ref.shape
    columns = high_ref.shape[1]
    gather(core_ref, x_ref, refs, u_ref, refs[0].shape[0] - 1)
    u = u_ref[:, :columns]
    t_ref[...] = dot(high_ref[...], u, ((1,), (1,))) + dot(low_ref[...], u, ((1,), (1,)))
    half = packed_ref.shape[0]
    part = half // X
    for flip in range(X):
        at = pl.ds(pl.multiple_of((x_ref[0] ^ flip) * part, part), part)
        packed_ref[at] = unpack(refs[flip])[1]
    gram_ref[:half] = packed_ref[:, :rank]
    gram_ref[half:] = packed_ref[:, rank:]


def left(place, here, there, high, low):
    rows, columns = high.shape
    per, half, _ = here[0].shape
    rank = 2 * half
    return pl.pallas_call(
        left_kernel,
        in_specs=[SMEM] * 2 + [VMEM] * (2 * X + 2),
        out_specs=[VMEM] * 2,
        out_shape=[jax.ShapeDtypeStruct((rows, rank), F32), jax.ShapeDtypeStruct((rank, rank), F32)],
        scratch_shapes=[pltpu.VMEM((rank, X * (per - 1) * LANES), BF16), pltpu.VMEM((half, LANES), F32)],
        compiler_params=params(24),
    )(place["core"], place["x"], *here, *there, high, low)


def lower_inverse(gram):
    rank = gram.shape[0]
    at_row = lax.broadcasted_iota(jnp.int32, (rank, rank), 0)
    at_col = lax.broadcasted_iota(jnp.int32, (rank, rank), 1)
    diagonal = jnp.where(at_row == at_col, gram, 0.0)
    down = lax.rsqrt(jnp.sum(diagonal, axis=1, keepdims=True))
    across = lax.rsqrt(jnp.sum(diagonal, axis=0, keepdims=True))
    work = jnp.concatenate([gram * down * across, jnp.where(at_row == at_col, across, 0.0)], axis=1)
    done = []
    for step in range(0, rank, 2):
        low = step // 8 * 8
        at = step - low
        work = work[at // 8 * 8 :] if at else (work[8:] if step else work)
        one = jnp.broadcast_to(work[:, step : step + 1], work.shape)
        two = jnp.broadcast_to(work[:, step + 1 : step + 2], work.shape)
        first, second = work[at : at + 1], work[at + 1 : at + 2]
        a, b, c = one[at : at + 1], one[at + 1 : at + 2], two[at + 1 : at + 2]
        det = a * c - b * b
        left_over = a * second - b * first
        inverse = 1.0 / det
        done.append((first * lax.rsqrt(a))[:, rank:])
        done.append((left_over * lax.rsqrt(a * det))[:, rank:])
        work = work - (one * ((c * first - b * second) * inverse) + two * (left_over * inverse))
    return jnp.concatenate(done, axis=0)


def inverse_kernel(gram_ref, out_ref):
    out_ref[...] = lower_inverse(gram_ref[...])


def inverse_of(gram):
    return pl.pallas_call(
        inverse_kernel,
        in_specs=[VMEM],
        out_specs=VMEM,
        out_shape=jax.ShapeDtypeStruct(gram.shape, F32),
        compiler_params=params(4),
        cost_estimate=pl.CostEstimate(flops=10_000_000, bytes_accessed=5_000_000, transcendentals=0),
    )(gram)


def fetch_kernel(gram_ref, g_ref, e_ref, out_ref, g_near, e_near, sems):
    copies = [
        pltpu.make_async_copy(far, near, sems.at[index])
        for index, (far, near) in enumerate([(g_ref, g_near), (e_ref, e_near)])
    ]
    for copy in copies:
        copy.start()
    out_ref[...] = lower_inverse(gram_ref[...])
    for copy in copies:
        copy.wait()


def inverse_and_fetch(gram, gradient, error):
    far = pl.BlockSpec(memory_space=pltpu.HBM)
    return pl.pallas_call(
        fetch_kernel,
        in_specs=[VMEM, far, far],
        out_specs=[VMEM] * 3,
        out_shape=[
            jax.ShapeDtypeStruct(gram.shape, F32),
            pltpu.VMEM(gradient.shape, BF16),
            pltpu.VMEM(error.shape, BF16),
        ],
        scratch_shapes=[pltpu.SemaphoreType.DMA((2,))],
        compiler_params=params(24),
        cost_estimate=pl.CostEstimate(flops=10_000_000, bytes_accessed=5_000_000, transcendentals=0),
    )(gram, *in_hbm(gradient, error))


def end_kernel(core_ref, x_ref, *refs):
    *refs, inverse_ref, p_ref, g_ref, e_ref, new_ref, q_ref, u_ref, half_ref = refs
    rank = p_ref.shape[1]
    width = q_ref.shape[1]
    step = pl.program_id(0)

    @pl.when(step == 0)
    def _():
        gather(core_ref, x_ref, refs, u_ref, refs[0].shape[0])
        half_ref[...] = dot(p_ref[...], inverse_ref[...], ((1,), (1,)), HIGH).astype(BF16)

    at = pl.ds(pl.multiple_of(step * width, LANES), width)
    high, mid, low = split(inverse_ref[...], 3)
    q = dot(low, u_ref[:rank, at]) + dot(jnp.concatenate([mid] * 2, axis=1), u_ref[: 2 * rank, at])
    q = dot(jnp.concatenate([high] * 3, axis=1), u_ref[:, at]) + q
    q_ref[...] = q
    for block in range(width // LANES):
        recon = dot(half_ref[...], q[:, block * LANES : (block + 1) * LANES].astype(BF16))
        part = pl.ds(block * LANES, LANES)
        far = pl.ds(pl.multiple_of(step * width + block * LANES, LANES), LANES)
        for replica in range(g_ref.shape[0]):
            corrected = g_ref[replica, :, far] + e_ref[replica, :, far]
            new_ref[replica, :, part] = (corrected.astype(F32) - recon).astype(BF16)


def end(place, here, there, p, inverse, gradient, error, width=1152):
    replicas, rows, columns = gradient.shape
    rank = p.shape[1]
    per = here[0].shape[0]
    wide = pl.BlockSpec((replicas, rows, width), lambda j: (0, 0, j))
    return pl.pallas_call(
        end_kernel,
        grid=(columns // width,),
        in_specs=[SMEM] * 2 + [VMEM] * (2 * X + 4),
        out_specs=[wide, pl.BlockSpec((rank, width), lambda j: (0, j))],
        out_shape=[
            jax.ShapeDtypeStruct(gradient.shape, BF16),
            jax.ShapeDtypeStruct((rank, columns), F32),
        ],
        scratch_shapes=[pltpu.VMEM((3 * rank, X * per * LANES), BF16), pltpu.VMEM((rows, rank), BF16)],
        compiler_params=params(24),
    )(place["core"], place["x"], *here, *there, inverse, p, gradient, error)


def per_device(gradient, error_buffer, q_start):
    place = {axis: lax.axis_index(axis).astype(jnp.int32).reshape(1) for axis in ("x", "near", "core")}
    core = place["core"]
    high, low, term = start(gradient, error_buffer, q_start.T)
    mine, theirs, _ = right(core, around(term, "y"), high, low, kind=BF16)
    here, there = coarse_sum(place, mine, theirs)
    term, gram = left(place, here, there, high, low)
    mine, theirs, p = right(core, around(term, "y"), high, low, inverse_of(gram))
    here, there, ready = all_sum(place, mine, theirs, gradient, error_buffer)
    new_error, q_factor = end(place, here, there, p, *ready)
    return new_error, q_factor.T


def solution(mesh):
    fine = Mesh(mesh.devices.reshape(X, FAR, NEAR, CORES, Y), ("x", "far", "near", "core", "y"))
    rows = ("x", "far", "near", "core")
    return jax.shard_map(
        per_device,
        mesh=fine,
        in_specs=(P(None, rows, "y"), P(None, rows, "y"), P("y", None)),
        out_specs=(P(None, rows, "y"), P("y", None)),
        check_vma=False,
    )
```

time: 944 us -> 114 us (0.12)
  blocking collectives: 524 us -> 0 us
  waiting for transfers between devices: 360 us -> 37.8 us
  starting transfers between devices: 0.08 us -> 56.8 us
  other arithmetic: 37.2 us -> 0 us
  Pallas kernels: 0 us -> 18.6 us
  between operations: 14.2 us -> 0.75 us
    psum x4 -> x0, blocking collectives: 524 us -> none  [the longest x2 497 us: per_device(): gram = lax.psum(local_gram, 'dp')]
    psum x2 -> x0, waiting for transfers between devices: 360 us -> none  [per_device(): q_now = lax.psum(partial_q, 'dp') / replicas]
    ppermute x0 -> x37, starting transfers between devices: none -> 56.8 us  [the longest x24 36 us: around(): lax.ppermute(value[flip], axis, [(i, i ^ flip) for i in range(4)])]
    ppermute x0 -> x37, waiting for transfers between devices: none -> 37.8 us  [the longest x24 25.8 us: around(): lax.ppermute(value[flip], axis, [(i, i ^ flip) for i in range(4)])]
    another operation x10 -> x0, other arithmetic: 24.1 us -> none  [the longest x6 13 us: per_device(): lower = jnp.linalg.cholesky(gram)]
    pallas_call x0 -> x16, Pallas kernels: none -> 18.6 us  [the longest x1 4.47 us: end(): pl.pallas_call(end_kernel, grid=(columns // width,), in_specs=[SMEM] * 2...]
  transfers between devices with their start and end apart: 2 -> 37, of which waited for: 2 -> 21; matrix products, arithmetic and copies ran while one was open for 0% -> 0% of each run, Pallas kernels for 0% -> 6%
where the time goes in v2:
time: 114 us
  starting transfers between devices  56.8 us (50%)
  waiting for transfers between devices  37.8 us (33%)
  Pallas kernels  18.6 us (16%)
    ppermute x24, starting transfers between devices, around(): lax.ppermute(value[flip], axis, [(i, i ^ flip) for i in range(4)])  36 us
    ppermute x24, waiting for transfers between devices, around(): lax.ppermute(value[flip], axis, [(i, i ^ flip) for i in range(4)])  25.8 us
    ppermute x13, starting transfers between devices, swap(): return lax.ppermute(value, axis, [(0, 1), (1, 0)])  20.8 us
    ppermute x13, waiting for transfers between devices, swap(): return lax.ppermute(value, axis, [(0, 1), (1, 0)])  12 us
    pallas_call x1, Pallas kernels, end(): pl.pallas_call(end_kernel, grid=(columns // width,), in_specs=[SMEM] * 2...  4.47 us
    pallas_call x1, Pallas kernels, start(): pl.pallas_call(functools.partial(start_kernel, height), in_specs=[far] *...  4.38 us
    pallas_call x1, Pallas kernels, inverse_and_fetch(): pl.pallas_call(fetch_kernel, in_specs=[VMEM, far, far], out_specs=[VMEM]...  3.62 us
    pallas_call x1, Pallas kernels, inverse_of(): pl.pallas_call(inverse_kernel, in_specs=[VMEM], out_specs=VMEM, out_shape...  3.24 us
  transfers between devices with their start and end apart: 37, of which 21 were waited for; matrix products, arithmetic and copies ran while one was open for 0% of the time, Pallas kernels for 6%

profile of v2, /device:TPU:1, one launch (start us, length us, event | category | flops | bytes accessed | tf_op | source)
XLA Modules:
  0.0 114.0 jit_solution(15446891799056415422)
XLA Ops:
  0.6 4.4 %shard_map.50 = (bf16[80,3456]{1,0:T(8,128)(2,1)S(1)}, bf16[80,3456]{1,0:T(8,128)(2,1)S(1)}, f32[80,64]{1,0:T(8,128)S(1)}) custom-call(bf16[8,80,3456]{2,1,0:T(8,128)(2,1)} %g_ref.3, bf16[8,80,3456]{2,1,0:T(8,128)(2,1)} %e_ref.3, bf16[64,3456]{1,0:T(8,128)(2,1)} %bitcast.5), custom_call_target="tpu_custom_call" | custom-call | tf_op jit(solution)/shard_map/pallas_call | solution.py:76
  5.0 3.7 %collective-permute-start.2 = (f32[80,64]{1,0:T(8,128)S(1)}, f32[80,64]{1,0:T(8,128)S(1)}, u32[]{:S(2)}, u32[]{:S(2)}) collective-permute-start(f32[80,64]{1,0:T(8,128)S(1)} %get-tuple-element.35.refs_0_), channel_id=1, source_target_pairs={{0,3},{1,2},{2,1},{3,0},{4,7},{5,6},{6,5},{7,4},{8,11},{9,10},{10,... | collective-permute-start | bytes 61448 | tf_op jit(solution)/shard_map/ppermute | solution.py:248
  8.7 0.3 collective-permute-start.1
  9.0 0.3 collective-permute-start
  9.3 0.7 collective-permute-done.2.refs_3_
  10.1 3.1 %collective-permute-done.1.refs_2_ = f32[80,64]{1,0:T(8,128)S(1)} collective-permute-done((f32[80,64]{1,0:T(8,128)S(1)}, f32[80,64]{1,0:T(8,128)S(1)}, u32[]{:S(2)}, u32[]{:S(2)}) %collective-permute-start.1) | collective-permute-done | bytes 20512 | tf_op jit(solution)/shard_map/ppermute | solution.py:248
  13.1 0.9 shard_map.51
  14.1 2.1 %collective-permute-start.3 = (bf16[30,32,128]{2,1,0:T(8,128)(2,1)S(1)}, bf16[30,32,128]{2,1,0:T(8,128)(2,1)S(1)}, u32[]{:S(2)}, u32[]{:S(2)}) collective-permute-start(bf16[30,32,128]{2,1,0:T(8,128)(2,1)S(1)} %get-tuple-element.39), channel_id=1, source_target_pairs={{0,4},{4,0},{1,5},{5,1},{2,6},{6,2},{3,7},{7,3},{8,12},{12,8},{9,1... | collective-permute-start | bytes 737288 | tf_op jit(solution)/shard_map/ppermute | solution.py:252
  16.1 1.1 collective-permute-done.3.b_ref
  17.3 1.3 %collective-permute-start.4 = (bf16[8,32,128]{2,1,0:T(8,128)(2,1)S(1)}, bf16[8,32,128]{2,1,0:T(8,128)(2,1)S(1)}, u32[]{:S(2)}, u32[]{:S(2)}) collective-permute-start(bf16[8,32,128]{2,1,0:T(8,128)(2,1)S(1)} %get-tuple-element.41), channel_id=1, source_target_pairs={{0,64},{64,0},{128,192},{192,128},{1,65},{65,1},{129,193},{193,129... | collective-permute-start | bytes 196616 | tf_op jit(solution)/shard_map/ppermute | solution.py:248
  18.6 2.4 %collective-permute-start.5 = (bf16[8,32,128]{2,1,0:T(8,128)(2,1)S(1)}, bf16[8,32,128]{2,1,0:T(8,128)(2,1)S(1)}, u32[]{:S(2)}, u32[]{:S(2)}) collective-permute-start(bf16[8,32,128]{2,1,0:T(8,128)(2,1)S(1)} %get-tuple-element.42), channel_id=1, source_target_pairs={{0,128},{64,192},{128,0},{192,64},{1,129},{65,193},{129,1},{193,65... | collective-permute-start | bytes 196616 | tf_op jit(solution)/shard_map/ppermute | solution.py:248
  21.1 0.2 collective-permute-start.6
  21.3 2.8 %collective-permute-done.5.refs_2_ = bf16[8,32,128]{2,1,0:T(8,128)(2,1)S(1)} collective-permute-done((bf16[8,32,128]{2,1,0:T(8,128)(2,1)S(1)}, bf16[8,32,128]{2,1,0:T(8,128)(2,1)S(1)}, u32[]{:S(2)}, u32[]{:S(2)}) %collective-permute-start.5) | collective-permute-done | bytes 65568 | tf_op jit(solution)/shard_map/ppermute | solution.py:248
  24.0 1.5 %collective-permute-done.6.refs_3_ = bf16[8,32,128]{2,1,0:T(8,128)(2,1)S(1)} collective-permute-done((bf16[8,32,128]{2,1,0:T(8,128)(2,1)S(1)}, bf16[8,32,128]{2,1,0:T(8,128)(2,1)S(1)}, u32[]{:S(2)}, u32[]{:S(2)}) %collective-permute-start.6) | collective-permute-done | bytes 65568 | tf_op jit(solution)/shard_map/ppermute | solution.py:248
  25.6 1.7 %collective-permute-start.7 = (bf16[8,32,128]{2,1,0:T(8,128)(2,1)S(1)}, bf16[8,32,128]{2,1,0:T(8,128)(2,1)S(1)}, u32[]{:S(2)}, u32[]{:S(2)}) collective-permute-start(bf16[8,32,128]{2,1,0:T(8,128)(2,1)S(1)} %shard_map.53.refs_0_), channel_id=1, source_target_pairs={{0,8},{8,0},{1,9},{9,1},{2,10},{10,2},{3,11},{11,3},{4,12},{12,4},... | collective-permute-start | bytes 196616 | tf_op jit(solution)/shard_map/ppermute | solution.py:252
  27.3 1.7 %collective-permute-done.7.refs_1_ = bf16[8,32,128]{2,1,0:T(8,128)(2,1)S(1)} collective-permute-done((bf16[8,32,128]{2,1,0:T(8,128)(2,1)S(1)}, bf16[8,32,128]{2,1,0:T(8,128)(2,1)S(1)}, u32[]{:S(2)}, u32[]{:S(2)}) %collective-permute-start.7) | collective-permute-done | bytes 65568 | tf_op jit(solution)/shard_map/ppermute | solution.py:252
  29.0 5.9 %collective-permute-start.10 = (bf16[8,32,128]{2,1,0:T(8,128)(2,1)S(1)}, bf16[8,32,128]{2,1,0:T(8,128)(2,1)S(1)}, u32[]{:S(2)}, u32[]{:S(2)}) collective-permute-start(bf16[8,32,128]{2,1,0:T(8,128)(2,1)S(1)} %shard_map.54.refs_0_), channel_id=1, source_target_pairs={{0,48},{16,32},{32,16},{48,0},{1,49},{17,33},{33,17},{49,1},{2,50}... | collective-permute-start | bytes 196616 | tf_op jit(solution)/shard_map/ppermute | solution.py:248
  34.9 1.0 collective-permute-start.9
  35.9 1.2 %collective-permute-start.8 = (bf16[8,32,128]{2,1,0:T(8,128)(2,1)S(1)}, bf16[8,32,128]{2,1,0:T(8,128)(2,1)S(1)}, u32[]{:S(2)}, u32[]{:S(2)}) collective-permute-start(bf16[8,32,128]{2,1,0:T(8,128)(2,1)S(1)} %shard_map.54.refs_0_), channel_id=1, source_target_pairs={{0,16},{16,0},{32,48},{48,32},{1,17},{17,1},{33,49},{49,33},{2,18}... | collective-permute-start | bytes 196616 | tf_op jit(solution)/shard_map/ppermute | solution.py:248
  37.1 0.1 collective-permute-done.10.refs_3_
  37.2 5.3 %collective-permute-done.9.refs_2_ = bf16[8,32,128]{2,1,0:T(8,128)(2,1)S(1)} collective-permute-done((bf16[8,32,128]{2,1,0:T(8,128)(2,1)S(1)}, bf16[8,32,128]{2,1,0:T(8,128)(2,1)S(1)}, u32[]{:S(2)}, u32[]{:S(2)}) %collective-permute-start.9) | collective-permute-done | bytes 65568 | tf_op jit(solution)/shard_map/ppermute | solution.py:248
  42.6 1.4 %collective-permute-start.13 = (bf16[8,32,128]{2,1,0:T(8,128)(2,1)S(1)}, bf16[8,32,128]{2,1,0:T(8,128)(2,1)S(1)}, u32[]{:S(2)}, u32[]{:S(2)}) collective-permute-start(bf16[8,32,128]{2,1,0:T(8,128)(2,1)S(1)} %shard_map.55.refs_0_), channel_id=1, source_target_pairs={{0,192},{64,128},{128,64},{192,0},{1,193},{65,129},{129,65},{193,1... | collective-permute-start | bytes 196616 | tf_op jit(solution)/shard_map/ppermute | solution.py:248
  44.0 0.6 collective-permute-start.12
  44.6 1.3 %collective-permute-start.11 = (bf16[8,32,128]{2,1,0:T(8,128)(2,1)S(1)}, bf16[8,32,128]{2,1,0:T(8,128)(2,1)S(1)}, u32[]{:S(2)}, u32[]{:S(2)}) collective-permute-start(bf16[8,32,128]{2,1,0:T(8,128)(2,1)S(1)} %shard_map.55.refs_0_), channel_id=1, source_target_pairs={{0,64},{64,0},{128,192},{192,128},{1,65},{65,1},{129,193},{193,129... | collective-permute-start | bytes 196616 | tf_op jit(solution)/shard_map/ppermute | solution.py:248
  45.9 5.2 %collective-permute-start.14 = (bf16[8,32,128]{2,1,0:T(8,128)(2,1)S(1)}, bf16[8,32,128]{2,1,0:T(8,128)(2,1)S(1)}, u32[]{:S(2)}, u32[]{:S(2)}) collective-permute-start(bf16[8,32,128]{2,1,0:T(8,128)(2,1)S(1)} %shard_map.55.refs_0_), channel_id=1, source_target_pairs={{0,4},{4,0},{1,5},{5,1},{2,6},{6,2},{3,7},{7,3},{8,12},{12,8},{9,1... | collective-permute-start | bytes 196616 | tf_op jit(solution)/shard_map/ppermute | solution.py:252
  51.1 1.4 %collective-permute-start.17 = (bf16[8,32,128]{2,1,0:T(8,128)(2,1)S(1)}, bf16[8,32,128]{2,1,0:T(8,128)(2,1)S(1)}, u32[]{:S(2)}, u32[]{:S(2)}) collective-permute-start(bf16[8,32,128]{2,1,0:T(8,128)(2,1)S(1)} %collective-permute-done.13.refs_3_), channel_id=1, source_target_pairs={{0,4},{4,0},{1,5},{5,1},{2,6},{6,2},{3,7},{7,3},{8,12},{12,8},{9,1... | collective-permute-start | bytes 196616 | tf_op jit(solution)/shard_map/ppermute | solution.py:252
  52.5 0.9 collective-permute-start.16
  53.5 0.6 collective-permute-start.15
  54.1 0.3 collective-permute-done.16.refs_6_
  54.4 0.6 collective-permute-done.15.refs_5_
  55.0 0.5 shard_map.56
  55.5 1.1 collective-permute-start.20
  56.6 0.8 collective-permute-start.19
  57.5 1.4 %collective-permute-start.18 = (f32[80,64]{1,0:T(8,128)S(1)}, f32[80,64]{1,0:T(8,128)S(1)}, u32[]{:S(2)}, u32[]{:S(2)}) collective-permute-start(f32[80,64]{1,0:T(8,128)S(1)} %get-tuple-element.45.refs_1_), channel_id=1, source_target_pairs={{0,1},{1,0},{2,3},{3,2},{4,5},{5,4},{6,7},{7,6},{8,9},{9,8},{10,11... | collective-permute-start | bytes 61448 | tf_op jit(solution)/shard_map/ppermute | solution.py:248
  58.9 3.2 %shard_map.57.refs_0_ = f32[64,64]{1,0:T(8,128)S(1)} custom-call(f32[64,64]{1,0:T(8,128)S(1)} %get-tuple-element.44.gram_ref), custom_call_target="tpu_custom_call" | custom-call | flops 10000000 | bytes 5000000 | tf_op jit(solution)/shard_map/pallas_call | solution.py:351
  62.1 1.1 shard_map.58
  63.2 1.3 %collective-permute-start.21 = (f32[28,32,128]{2,1,0:T(8,128)S(1)}, f32[28,32,128]{2,1,0:T(8,128)S(1)}, u32[]{:S(2)}, u32[]{:S(2)}) collective-permute-start(f32[28,32,128]{2,1,0:T(8,128)S(1)} %get-tuple-element.47), channel_id=1, source_target_pairs={{0,4},{4,0},{1,5},{5,1},{2,6},{6,2},{3,7},{7,3},{8,12},{12,8},{9,1... | collective-permute-start | bytes 1376264 | tf_op jit(solution)/shard_map/ppermute | solution.py:252
  64.5 1.4 %collective-permute-done.21.b_ref = f32[28,32,128]{2,1,0:T(8,128)S(1)} collective-permute-done((f32[28,32,128]{2,1,0:T(8,128)S(1)}, f32[28,32,128]{2,1,0:T(8,128)S(1)}, u32[]{:S(2)}, u32[]{:S(2)}) %collective-permute-start.21) | collective-permute-done | bytes 458784 | tf_op jit(solution)/shard_map/ppermute | solution.py:252
  66.0 1.1 collective-permute-start.22
  67.1 2.0 %collective-permute-start.23 = (f32[8,32,128]{2,1,0:T(8,128)S(1)}, f32[8,32,128]{2,1,0:T(8,128)S(1)}, u32[]{:S(2)}, u32[]{:S(2)}) collective-permute-start(f32[8,32,128]{2,1,0:T(8,128)S(1)} %get-tuple-element.50), channel_id=1, source_target_pairs={{0,128},{64,192},{128,0},{192,64},{1,129},{65,193},{129,1},{193,65... | collective-permute-start | bytes 393224 | tf_op jit(solution)/shard_map/ppermute | solution.py:248
  69.1 0.8 collective-permute-start.24
  70.0 0.9 collective-permute-done.22.refs_1_
  70.8 4.4 %collective-permute-done.23.refs_2_ = f32[8,32,128]{2,1,0:T(8,128)S(1)} collective-permute-done((f32[8,32,128]{2,1,0:T(8,128)S(1)}, f32[8,32,128]{2,1,0:T(8,128)S(1)}, u32[]{:S(2)}, u32[]{:S(2)}) %collective-permute-start.23) | collective-permute-done | bytes 131104 | tf_op jit(solution)/shard_map/ppermute | solution.py:248
  75.2 2.5 %collective-permute-done.24.refs_3_ = f32[8,32,128]{2,1,0:T(8,128)S(1)} collective-permute-done((f32[8,32,128]{2,1,0:T(8,128)S(1)}, f32[8,32,128]{2,1,0:T(8,128)S(1)}, u32[]{:S(2)}, u32[]{:S(2)}) %collective-permute-start.24) | collective-permute-done | bytes 131104 | tf_op jit(solution)/shard_map/ppermute | solution.py:248
  77.8 1.0 collective-permute-start.25
  78.8 2.2 %collective-permute-done.25.b_ref = f32[8,16,128]{2,1,0:T(8,128)S(1)} collective-permute-done((f32[8,16,128]{2,1,0:T(8,128)S(1)}, f32[8,16,128]{2,1,0:T(8,128)S(1)}, u32[]{:S(2)}, u32[]{:S(2)}) %collective-permute-start.25) | collective-permute-done | bytes 65568 | tf_op jit(solution)/shard_map/ppermute | solution.py:252
  81.0 1.8 %collective-permute-start.28 = (f32[8,16,128]{2,1,0:T(8,128)S(1)}, f32[8,16,128]{2,1,0:T(8,128)S(1)}, u32[]{:S(2)}, u32[]{:S(2)}) collective-permute-start(f32[8,16,128]{2,1,0:T(8,128)S(1)} %shard_map.61.refs_0_), channel_id=1, source_target_pairs={{0,48},{16,32},{32,16},{48,0},{1,49},{17,33},{33,17},{49,1},{2,50}... | collective-permute-start | bytes 196616 | tf_op jit(solution)/shard_map/ppermute | solution.py:248
  82.8 2.8 %collective-permute-start.27 = (f32[8,16,128]{2,1,0:T(8,128)S(1)}, f32[8,16,128]{2,1,0:T(8,128)S(1)}, u32[]{:S(2)}, u32[]{:S(2)}) collective-permute-start(f32[8,16,128]{2,1,0:T(8,128)S(1)} %shard_map.61.refs_0_), channel_id=1, source_target_pairs={{0,32},{16,48},{32,0},{48,16},{1,33},{17,49},{33,1},{49,17},{2,34}... | collective-permute-start | bytes 196616 | tf_op jit(solution)/shard_map/ppermute | solution.py:248
  85.6 1.1 %collective-permute-start.26 = (f32[8,16,128]{2,1,0:T(8,128)S(1)}, f32[8,16,128]{2,1,0:T(8,128)S(1)}, u32[]{:S(2)}, u32[]{:S(2)}) collective-permute-start(f32[8,16,128]{2,1,0:T(8,128)S(1)} %shard_map.61.refs_0_), channel_id=1, source_target_pairs={{0,16},{16,0},{32,48},{48,32},{1,17},{17,1},{33,49},{49,33},{2,18}... | collective-permute-start | bytes 196616 | tf_op jit(solution)/shard_map/ppermute | solution.py:248
  86.7 3.3 %collective-permute-done.27.refs_2_ = f32[8,16,128]{2,1,0:T(8,128)S(1)} collective-permute-done((f32[8,16,128]{2,1,0:T(8,128)S(1)}, f32[8,16,128]{2,1,0:T(8,128)S(1)}, u32[]{:S(2)}, u32[]{:S(2)}) %collective-permute-start.27) | collective-permute-done | bytes 65568 | tf_op jit(solution)/shard_map/ppermute | solution.py:248
  90.0 1.2 %collective-permute-done.26.refs_1_ = f32[8,16,128]{2,1,0:T(8,128)S(1)} collective-permute-done((f32[8,16,128]{2,1,0:T(8,128)S(1)}, f32[8,16,128]{2,1,0:T(8,128)S(1)}, u32[]{:S(2)}, u32[]{:S(2)}) %collective-permute-start.26) | collective-permute-done | bytes 65568 | tf_op jit(solution)/shard_map/ppermute | solution.py:248
  91.3 0.2 collective-permute-start.29
  91.4 3.6 %collective-permute-done.29.there_ref = f32[8,16,128]{2,1,0:T(8,128)S(1)} collective-permute-done((f32[8,16,128]{2,1,0:T(8,128)S(1)}, f32[8,16,128]{2,1,0:T(8,128)S(1)}, u32[]{:S(2)}, u32[]{:S(2)}) %collective-permute-start.29) | collective-permute-done | bytes 65568 | tf_op jit(solution)/shard_map/ppermute | solution.py:252
  95.1 0.5 collective-permute-start.32
  95.7 2.8 %collective-permute-start.30 = (f32[7,32,128]{2,1,0:T(8,128)S(1)}, f32[7,32,128]{2,1,0:T(8,128)S(1)}, u32[]{:S(2)}, u32[]{:S(2)}) collective-permute-start(f32[7,32,128]{2,1,0:T(8,128)S(1)} %get-tuple-element.54.refs_0_), channel_id=1, source_target_pairs={{0,64},{64,0},{128,192},{192,128},{1,65},{65,1},{129,193},{193,129... | collective-permute-start | bytes 344072 | tf_op jit(solution)/shard_map/ppermute | solution.py:248
  98.4 5.5 %collective-permute-start.33 = (f32[7,32,128]{2,1,0:T(8,128)S(1)}, f32[7,32,128]{2,1,0:T(8,128)S(1)}, u32[]{:S(2)}, u32[]{:S(2)}) collective-permute-start(f32[7,32,128]{2,1,0:T(8,128)S(1)} %get-tuple-element.54.refs_0_), channel_id=1, source_target_pairs={{0,4},{4,0},{1,5},{5,1},{2,6},{6,2},{3,7},{7,3},{8,12},{12,8},{9,1... | collective-permute-start | bytes 344072 | tf_op jit(solution)/shard_map/ppermute | solution.py:252
  103.9 3.6 %shard_map.64 = (f32[64,64]{1,0:T(8,128)S(1)}, bf16[8,80,3456]{2,1,0:T(8,128)(2,1)S(1)}, bf16[8,80,3456]{2,1,0:T(8,128)(2,1)S(1)}) custom-call(f32[64,64]{1,0:T(8,128)S(1)} %get-tuple-element.55.gram_ref, bf16[8,80,3456]{2,1,0:T(8,128)(2,1)} %g_ref.3, bf16[8,80,3456]{2,1,0:T(8,128)(2,1)} %e_ref.3), custom_call_target="tpu_custom_call" | custom-call | flops 10000000 | bytes 5000000 | tf_op jit(solution)/shard_map/pallas_call | solution.py:375
  107.6 0.3 collective-permute-start.34
  107.9 0.3 collective-permute-start.35
  108.2 0.2 collective-permute-start.36
  108.4 0.6 collective-permute-done.34.refs_5_
  109.0 0.2 collective-permute-done.35.refs_6_
  109.2 0.3 collective-permute-done.36.refs_7_
  109.5 4.5 %shard_map.65 = (bf16[8,80,3456]{2,1,0:T(8,128)(2,1)}, f32[64,3456]{1,0:T(8,128)}) custom-call(s32[1]{0:T(128)} %bitcast.core_ref, s32[1]{0:T(128)} %bitcast.1.x_ref, f32[7,32,128]{2,1,0:T(8,128)S(1)} %get-tuple-element.54.refs_0_, f32[7,32,128]{2,1,0:T(8,128)S(1)} %collective-permute-done.30.refs_1_, f32[7,32,128]{2,1,0:T(8,128)S(1)} %collective-permute-done.31.refs_2_, ...), custom_call_target="tpu_custom_call" | custom-call | tf_op jit(solution)/shard_map/pallas_call | solution.py:420
  (26 shorter events, 0.4 us)
Async XLA Ops:
  5.0 5.0 %collective-permute-start.2 = (f32[80,64]{1,0:T(8,128)S(1)}, f32[80,64]{1,0:T(8,128)S(1)}, u32[]{:S(2)}, u32[]{:S(2)}) collective-permute-start(f32[80,64]{1,0:T(8,128)S(1)} %get-tuple-element.35.refs_0_), channel_id=1, source_target_pairs={{0,3},{1,2},{2,1},{3,0},{4,7},{5,6},{6,5},{7,4},{8,11},{9,10},{10,... | collective-permute-start | bytes 61448 | tf_op jit(solution)/shard_map/ppermute | solution.py:248
  8.7 4.5 %collective-permute-start.1 = (f32[80,64]{1,0:T(8,128)S(1)}, f32[80,64]{1,0:T(8,128)S(1)}, u32[]{:S(2)}, u32[]{:S(2)}) collective-permute-start(f32[80,64]{1,0:T(8,128)S(1)} %get-tuple-element.35.refs_0_), channel_id=1, source_target_pairs={{0,2},{1,3},{2,0},{3,1},{4,6},{5,7},{6,4},{7,5},{8,10},{9,11},{10,... | collective-permute-start | bytes 61448 | tf_op jit(solution)/shard_map/ppermute | solution.py:248
  9.0 4.1 %collective-permute-start = (f32[80,64]{1,0:T(8,128)S(1)}, f32[80,64]{1,0:T(8,128)S(1)}, u32[]{:S(2)}, u32[]{:S(2)}) collective-permute-start(f32[80,64]{1,0:T(8,128)S(1)} %get-tuple-element.35.refs_0_), channel_id=1, source_target_pairs={{0,1},{1,0},{2,3},{3,2},{4,5},{5,4},{6,7},{7,6},{8,9},{9,8},{10,11... | collective-permute-start | bytes 61448 | tf_op jit(solution)/shard_map/ppermute | solution.py:248
  14.1 3.2 %collective-permute-start.3 = (bf16[30,32,128]{2,1,0:T(8,128)(2,1)S(1)}, bf16[30,32,128]{2,1,0:T(8,128)(2,1)S(1)}, u32[]{:S(2)}, u32[]{:S(2)}) collective-permute-start(bf16[30,32,128]{2,1,0:T(8,128)(2,1)S(1)} %get-tuple-element.39), channel_id=1, source_target_pairs={{0,4},{4,0},{1,5},{5,1},{2,6},{6,2},{3,7},{7,3},{8,12},{12,8},{9,1... | collective-permute-start | bytes 737288 | tf_op jit(solution)/shard_map/ppermute | solution.py:252
  17.3 3.9 %collective-permute-start.4 = (bf16[8,32,128]{2,1,0:T(8,128)(2,1)S(1)}, bf16[8,32,128]{2,1,0:T(8,128)(2,1)S(1)}, u32[]{:S(2)}, u32[]{:S(2)}) collective-permute-start(bf16[8,32,128]{2,1,0:T(8,128)(2,1)S(1)} %get-tuple-element.41), channel_id=1, source_target_pairs={{0,64},{64,0},{128,192},{192,128},{1,65},{65,1},{129,193},{193,129... | collective-permute-start | bytes 196616 | tf_op jit(solution)/shard_map/ppermute | solution.py:248
  18.6 5.4 %collective-permute-start.5 = (bf16[8,32,128]{2,1,0:T(8,128)(2,1)S(1)}, bf16[8,32,128]{2,1,0:T(8,128)(2,1)S(1)}, u32[]{:S(2)}, u32[]{:S(2)}) collective-permute-start(bf16[8,32,128]{2,1,0:T(8,128)(2,1)S(1)} %get-tuple-element.42), channel_id=1, source_target_pairs={{0,128},{64,192},{128,0},{192,64},{1,129},{65,193},{129,1},{193,65... | collective-permute-start | bytes 196616 | tf_op jit(solution)/shard_map/ppermute | solution.py:248
  21.1 4.5 %collective-permute-start.6 = (bf16[8,32,128]{2,1,0:T(8,128)(2,1)S(1)}, bf16[8,32,128]{2,1,0:T(8,128)(2,1)S(1)}, u32[]{:S(2)}, u32[]{:S(2)}) collective-permute-start(bf16[8,32,128]{2,1,0:T(8,128)(2,1)S(1)} %get-tuple-element.43), channel_id=1, source_target_pairs={{0,192},{64,128},{128,64},{192,0},{1,193},{65,129},{129,65},{193,1... | collective-permute-start | bytes 196616 | tf_op jit(solution)/shard_map/ppermute | solution.py:248
  25.6 3.4 %collective-permute-start.7 = (bf16[8,32,128]{2,1,0:T(8,128)(2,1)S(1)}, bf16[8,32,128]{2,1,0:T(8,128)(2,1)S(1)}, u32[]{:S(2)}, u32[]{:S(2)}) collective-permute-start(bf16[8,32,128]{2,1,0:T(8,128)(2,1)S(1)} %shard_map.53.refs_0_), channel_id=1, source_target_pairs={{0,8},{8,0},{1,9},{9,1},{2,10},{10,2},{3,11},{11,3},{4,12},{12,4},... | collective-permute-start | bytes 196616 | tf_op jit(solution)/shard_map/ppermute | solution.py:252
  29.0 8.2 %collective-permute-start.10 = (bf16[8,32,128]{2,1,0:T(8,128)(2,1)S(1)}, bf16[8,32,128]{2,1,0:T(8,128)(2,1)S(1)}, u32[]{:S(2)}, u32[]{:S(2)}) collective-permute-start(bf16[8,32,128]{2,1,0:T(8,128)(2,1)S(1)} %shard_map.54.refs_0_), channel_id=1, source_target_pairs={{0,48},{16,32},{32,16},{48,0},{1,49},{17,33},{33,17},{49,1},{2,50}... | collective-permute-start | bytes 196616 | tf_op jit(solution)/shard_map/ppermute | solution.py:248
  34.9 7.6 %collective-permute-start.9 = (bf16[8,32,128]{2,1,0:T(8,128)(2,1)S(1)}, bf16[8,32,128]{2,1,0:T(8,128)(2,1)S(1)}, u32[]{:S(2)}, u32[]{:S(2)}) collective-permute-start(bf16[8,32,128]{2,1,0:T(8,128)(2,1)S(1)} %shard_map.54.refs_0_), channel_id=1, source_target_pairs={{0,32},{16,48},{32,0},{48,16},{1,33},{17,49},{33,1},{49,17},{2,34}... | collective-permute-start | bytes 196616 | tf_op jit(solution)/shard_map/ppermute | solution.py:248
  35.9 6.6 %collective-permute-start.8 = (bf16[8,32,128]{2,1,0:T(8,128)(2,1)S(1)}, bf16[8,32,128]{2,1,0:T(8,128)(2,1)S(1)}, u32[]{:S(2)}, u32[]{:S(2)}) collective-permute-start(bf16[8,32,128]{2,1,0:T(8,128)(2,1)S(1)} %shard_map.54.refs_0_), channel_id=1, source_target_pairs={{0,16},{16,0},{32,48},{48,32},{1,17},{17,1},{33,49},{49,33},{2,18}... | collective-permute-start | bytes 196616 | tf_op jit(solution)/shard_map/ppermute | solution.py:248
  42.6 8.6 %collective-permute-start.13 = (bf16[8,32,128]{2,1,0:T(8,128)(2,1)S(1)}, bf16[8,32,128]{2,1,0:T(8,128)(2,1)S(1)}, u32[]{:S(2)}, u32[]{:S(2)}) collective-permute-start(bf16[8,32,128]{2,1,0:T(8,128)(2,1)S(1)} %shard_map.55.refs_0_), channel_id=1, source_target_pairs={{0,192},{64,128},{128,64},{192,0},{1,193},{65,129},{129,65},{193,1... | collective-permute-start | bytes 196616 | tf_op jit(solution)/shard_map/ppermute | solution.py:248
  44.0 8.5 %collective-permute-start.12 = (bf16[8,32,128]{2,1,0:T(8,128)(2,1)S(1)}, bf16[8,32,128]{2,1,0:T(8,128)(2,1)S(1)}, u32[]{:S(2)}, u32[]{:S(2)}) collective-permute-start(bf16[8,32,128]{2,1,0:T(8,128)(2,1)S(1)} %shard_map.55.refs_0_), channel_id=1, source_target_pairs={{0,128},{64,192},{128,0},{192,64},{1,129},{65,193},{129,1},{193,65... | collective-permute-start | bytes 196616 | tf_op jit(solution)/shard_map/ppermute | solution.py:248
  44.6 8.9 %collective-permute-start.11 = (bf16[8,32,128]{2,1,0:T(8,128)(2,1)S(1)}, bf16[8,32,128]{2,1,0:T(8,128)(2,1)S(1)}, u32[]{:S(2)}, u32[]{:S(2)}) collective-permute-start(bf16[8,32,128]{2,1,0:T(8,128)(2,1)S(1)} %shard_map.55.refs_0_), channel_id=1, source_target_pairs={{0,64},{64,0},{128,192},{192,128},{1,65},{65,1},{129,193},{193,129... | collective-permute-start | bytes 196616 | tf_op jit(solution)/shard_map/ppermute | solution.py:248
  45.9 8.2 %collective-permute-start.14 = (bf16[8,32,128]{2,1,0:T(8,128)(2,1)S(1)}, bf16[8,32,128]{2,1,0:T(8,128)(2,1)S(1)}, u32[]{:S(2)}, u32[]{:S(2)}) collective-permute-start(bf16[8,32,128]{2,1,0:T(8,128)(2,1)S(1)} %shard_map.55.refs_0_), channel_id=1, source_target_pairs={{0,4},{4,0},{1,5},{5,1},{2,6},{6,2},{3,7},{7,3},{8,12},{12,8},{9,1... | collective-permute-start | bytes 196616 | tf_op jit(solution)/shard_map/ppermute | solution.py:252
  51.1 2.9 %collective-permute-start.17 = (bf16[8,32,128]{2,1,0:T(8,128)(2,1)S(1)}, bf16[8,32,128]{2,1,0:T(8,128)(2,1)S(1)}, u32[]{:S(2)}, u32[]{:S(2)}) collective-permute-start(bf16[8,32,128]{2,1,0:T(8,128)(2,1)S(1)} %collective-permute-done.13.refs_3_), channel_id=1, source_target_pairs={{0,4},{4,0},{1,5},{5,1},{2,6},{6,2},{3,7},{7,3},{8,12},{12,8},{9,1... | collective-permute-start | bytes 196616 | tf_op jit(solution)/shard_map/ppermute | solution.py:252
  52.5 1.8 %collective-permute-start.16 = (bf16[8,32,128]{2,1,0:T(8,128)(2,1)S(1)}, bf16[8,32,128]{2,1,0:T(8,128)(2,1)S(1)}, u32[]{:S(2)}, u32[]{:S(2)}) collective-permute-start(bf16[8,32,128]{2,1,0:T(8,128)(2,1)S(1)} %collective-permute-done.12.refs_2_), channel_id=1, source_target_pairs={{0,4},{4,0},{1,5},{5,1},{2,6},{6,2},{3,7},{7,3},{8,12},{12,8},{9,1... | collective-permute-start | bytes 196616 | tf_op jit(solution)/shard_map/ppermute | solution.py:252
  53.5 1.5 %collective-permute-start.15 = (bf16[8,32,128]{2,1,0:T(8,128)(2,1)S(1)}, bf16[8,32,128]{2,1,0:T(8,128)(2,1)S(1)}, u32[]{:S(2)}, u32[]{:S(2)}) collective-permute-start(bf16[8,32,128]{2,1,0:T(8,128)(2,1)S(1)} %collective-permute-done.11.refs_1_), channel_id=1, source_target_pairs={{0,4},{4,0},{1,5},{5,1},{2,6},{6,2},{3,7},{7,3},{8,12},{12,8},{9,1... | collective-permute-start | bytes 196616 | tf_op jit(solution)/shard_map/ppermute | solution.py:252
  55.5 6.6 %collective-permute-start.20 = (f32[80,64]{1,0:T(8,128)S(1)}, f32[80,64]{1,0:T(8,128)S(1)}, u32[]{:S(2)}, u32[]{:S(2)}) collective-permute-start(f32[80,64]{1,0:T(8,128)S(1)} %get-tuple-element.45.refs_1_), channel_id=1, source_target_pairs={{0,3},{1,2},{2,1},{3,0},{4,7},{5,6},{6,5},{7,4},{8,11},{9,10},{10,... | collective-permute-start | bytes 61448 | tf_op jit(solution)/shard_map/ppermute | solution.py:248
  56.6 5.5 %collective-permute-start.19 = (f32[80,64]{1,0:T(8,128)S(1)}, f32[80,64]{1,0:T(8,128)S(1)}, u32[]{:S(2)}, u32[]{:S(2)}) collective-permute-start(f32[80,64]{1,0:T(8,128)S(1)} %get-tuple-element.45.refs_1_), channel_id=1, source_target_pairs={{0,2},{1,3},{2,0},{3,1},{4,6},{5,7},{6,4},{7,5},{8,10},{9,11},{10,... | collective-permute-start | bytes 61448 | tf_op jit(solution)/shard_map/ppermute | solution.py:248
  57.5 4.7 %collective-permute-start.18 = (f32[80,64]{1,0:T(8,128)S(1)}, f32[80,64]{1,0:T(8,128)S(1)}, u32[]{:S(2)}, u32[]{:S(2)}) collective-permute-start(f32[80,64]{1,0:T(8,128)S(1)} %get-tuple-element.45.refs_1_), channel_id=1, source_target_pairs={{0,1},{1,0},{2,3},{3,2},{4,5},{5,4},{6,7},{7,6},{8,9},{9,8},{10,11... | collective-permute-start | bytes 61448 | tf_op jit(solution)/shard_map/ppermute | solution.py:248
  63.2 2.7 %collective-permute-start.21 = (f32[28,32,128]{2,1,0:T(8,128)S(1)}, f32[28,32,128]{2,1,0:T(8,128)S(1)}, u32[]{:S(2)}, u32[]{:S(2)}) collective-permute-start(f32[28,32,128]{2,1,0:T(8,128)S(1)} %get-tuple-element.47), channel_id=1, source_target_pairs={{0,4},{4,0},{1,5},{5,1},{2,6},{6,2},{3,7},{7,3},{8,12},{12,8},{9,1... | collective-permute-start | bytes 1376264 | tf_op jit(solution)/shard_map/ppermute | solution.py:252
  66.0 4.8 %collective-permute-start.22 = (f32[8,32,128]{2,1,0:T(8,128)S(1)}, f32[8,32,128]{2,1,0:T(8,128)S(1)}, u32[]{:S(2)}, u32[]{:S(2)}) collective-permute-start(f32[8,32,128]{2,1,0:T(8,128)S(1)} %get-tuple-element.49), channel_id=1, source_target_pairs={{0,64},{64,0},{128,192},{192,128},{1,65},{65,1},{129,193},{193,129... | collective-permute-start | bytes 393224 | tf_op jit(solution)/shard_map/ppermute | solution.py:248
  67.1 8.1 %collective-permute-start.23 = (f32[8,32,128]{2,1,0:T(8,128)S(1)}, f32[8,32,128]{2,1,0:T(8,128)S(1)}, u32[]{:S(2)}, u32[]{:S(2)}) collective-permute-start(f32[8,32,128]{2,1,0:T(8,128)S(1)} %get-tuple-element.50), channel_id=1, source_target_pairs={{0,128},{64,192},{128,0},{192,64},{1,129},{65,193},{129,1},{193,65... | collective-permute-start | bytes 393224 | tf_op jit(solution)/shard_map/ppermute | solution.py:248
  69.1 8.6 %collective-permute-start.24 = (f32[8,32,128]{2,1,0:T(8,128)S(1)}, f32[8,32,128]{2,1,0:T(8,128)S(1)}, u32[]{:S(2)}, u32[]{:S(2)}) collective-permute-start(f32[8,32,128]{2,1,0:T(8,128)S(1)} %get-tuple-element.51), channel_id=1, source_target_pairs={{0,192},{64,128},{128,64},{192,0},{1,193},{65,129},{129,65},{193,1... | collective-permute-start | bytes 393224 | tf_op jit(solution)/shard_map/ppermute | solution.py:248
  77.8 3.2 %collective-permute-start.25 = (f32[8,16,128]{2,1,0:T(8,128)S(1)}, f32[8,16,128]{2,1,0:T(8,128)S(1)}, u32[]{:S(2)}, u32[]{:S(2)}) collective-permute-start(f32[8,16,128]{2,1,0:T(8,128)S(1)} %get-tuple-element.53), channel_id=1, source_target_pairs={{0,8},{8,0},{1,9},{9,1},{2,10},{10,2},{3,11},{11,3},{4,12},{12,4},... | collective-permute-start | bytes 196616 | tf_op jit(solution)/shard_map/ppermute | solution.py:252
  81.0 5.7 %collective-permute-start.28 = (f32[8,16,128]{2,1,0:T(8,128)S(1)}, f32[8,16,128]{2,1,0:T(8,128)S(1)}, u32[]{:S(2)}, u32[]{:S(2)}) collective-permute-start(f32[8,16,128]{2,1,0:T(8,128)S(1)} %shard_map.61.refs_0_), channel_id=1, source_target_pairs={{0,48},{16,32},{32,16},{48,0},{1,49},{17,33},{33,17},{49,1},{2,50}... | collective-permute-start | bytes 196616 | tf_op jit(solution)/shard_map/ppermute | solution.py:248
  82.8 7.2 %collective-permute-start.27 = (f32[8,16,128]{2,1,0:T(8,128)S(1)}, f32[8,16,128]{2,1,0:T(8,128)S(1)}, u32[]{:S(2)}, u32[]{:S(2)}) collective-permute-start(f32[8,16,128]{2,1,0:T(8,128)S(1)} %shard_map.61.refs_0_), channel_id=1, source_target_pairs={{0,32},{16,48},{32,0},{48,16},{1,33},{17,49},{33,1},{49,17},{2,34}... | collective-permute-start | bytes 196616 | tf_op jit(solution)/shard_map/ppermute | solution.py:248
  85.6 5.7 %collective-permute-start.26 = (f32[8,16,128]{2,1,0:T(8,128)S(1)}, f32[8,16,128]{2,1,0:T(8,128)S(1)}, u32[]{:S(2)}, u32[]{:S(2)}) collective-permute-start(f32[8,16,128]{2,1,0:T(8,128)S(1)} %shard_map.61.refs_0_), channel_id=1, source_target_pairs={{0,16},{16,0},{32,48},{48,32},{1,17},{17,1},{33,49},{49,33},{2,18}... | collective-permute-start | bytes 196616 | tf_op jit(solution)/shard_map/ppermute | solution.py:248
  91.3 3.8 %collective-permute-start.29 = (f32[8,16,128]{2,1,0:T(8,128)S(1)}, f32[8,16,128]{2,1,0:T(8,128)S(1)}, u32[]{:S(2)}, u32[]{:S(2)}) collective-permute-start(f32[8,16,128]{2,1,0:T(8,128)S(1)} %shard_map.62.here_ref), channel_id=1, source_target_pairs={{0,8},{8,0},{1,9},{9,1},{2,10},{10,2},{3,11},{11,3},{4,12},{12,4},... | collective-permute-start | bytes 196616 | tf_op jit(solution)/shard_map/ppermute | solution.py:252
  95.1 12.4 %collective-permute-start.32 = (f32[7,32,128]{2,1,0:T(8,128)S(1)}, f32[7,32,128]{2,1,0:T(8,128)S(1)}, u32[]{:S(2)}, u32[]{:S(2)}) collective-permute-start(f32[7,32,128]{2,1,0:T(8,128)S(1)} %get-tuple-element.54.refs_0_), channel_id=1, source_target_pairs={{0,192},{64,128},{128,64},{192,0},{1,193},{65,129},{129,65},{193,1... | collective-permute-start | bytes 344072 | tf_op jit(solution)/shard_map/ppermute | solution.py:248
  95.6 11.9 %collective-permute-start.31 = (f32[7,32,128]{2,1,0:T(8,128)S(1)}, f32[7,32,128]{2,1,0:T(8,128)S(1)}, u32[]{:S(2)}, u32[]{:S(2)}) collective-permute-start(f32[7,32,128]{2,1,0:T(8,128)S(1)} %get-tuple-element.54.refs_0_), channel_id=1, source_target_pairs={{0,128},{64,192},{128,0},{192,64},{1,129},{65,193},{129,1},{193,65... | collective-permute-start | bytes 344072 | tf_op jit(solution)/shard_map/ppermute | solution.py:248
  95.7 11.9 %collective-permute-start.30 = (f32[7,32,128]{2,1,0:T(8,128)S(1)}, f32[7,32,128]{2,1,0:T(8,128)S(1)}, u32[]{:S(2)}, u32[]{:S(2)}) collective-permute-start(f32[7,32,128]{2,1,0:T(8,128)S(1)} %get-tuple-element.54.refs_0_), channel_id=1, source_target_pairs={{0,64},{64,0},{128,192},{192,128},{1,65},{65,1},{129,193},{193,129... | collective-permute-start | bytes 344072 | tf_op jit(solution)/shard_map/ppermute | solution.py:248
  98.4 10.0 %collective-permute-start.33 = (f32[7,32,128]{2,1,0:T(8,128)S(1)}, f32[7,32,128]{2,1,0:T(8,128)S(1)}, u32[]{:S(2)}, u32[]{:S(2)}) collective-permute-start(f32[7,32,128]{2,1,0:T(8,128)S(1)} %get-tuple-element.54.refs_0_), channel_id=1, source_target_pairs={{0,4},{4,0},{1,5},{5,1},{2,6},{6,2},{3,7},{7,3},{8,12},{12,8},{9,1... | collective-permute-start | bytes 344072 | tf_op jit(solution)/shard_map/ppermute | solution.py:252
  107.6 1.4 %collective-permute-start.34 = (f32[7,32,128]{2,1,0:T(8,128)S(1)}, f32[7,32,128]{2,1,0:T(8,128)S(1)}, u32[]{:S(2)}, u32[]{:S(2)}) collective-permute-start(f32[7,32,128]{2,1,0:T(8,128)S(1)} %collective-permute-done.30.refs_1_), channel_id=1, source_target_pairs={{0,4},{4,0},{1,5},{5,1},{2,6},{6,2},{3,7},{7,3},{8,12},{12,8},{9,1... | collective-permute-start | bytes 344072 | tf_op jit(solution)/shard_map/ppermute | solution.py:252
  107.9 1.3 %collective-permute-start.35 = (f32[7,32,128]{2,1,0:T(8,128)S(1)}, f32[7,32,128]{2,1,0:T(8,128)S(1)}, u32[]{:S(2)}, u32[]{:S(2)}) collective-permute-start(f32[7,32,128]{2,1,0:T(8,128)S(1)} %collective-permute-done.31.refs_2_), channel_id=1, source_target_pairs={{0,4},{4,0},{1,5},{5,1},{2,6},{6,2},{3,7},{7,3},{8,12},{12,8},{9,1... | collective-permute-start | bytes 344072 | tf_op jit(solution)/shard_map/ppermute | solution.py:252
  108.2 1.3 %collective-permute-start.36 = (f32[7,32,128]{2,1,0:T(8,128)S(1)}, f32[7,32,128]{2,1,0:T(8,128)S(1)}, u32[]{:S(2)}, u32[]{:S(2)}) collective-permute-start(f32[7,32,128]{2,1,0:T(8,128)S(1)} %collective-permute-done.32.refs_3_), channel_id=1, source_target_pairs={{0,4},{4,0},{1,5},{5,1},{2,6},{6,2},{3,7},{7,3},{8,12},{12,8},{9,1... | collective-permute-start | bytes 344072 | tf_op jit(solution)/shard_map/ppermute | solution.py:252

commit v3 on v2

--- a/solution.py
+++ b/solution.py
@@ -32,7 +32,8 @@
     return pltpu.CompilerParams(vmem_limit_bytes=mib << 20, **more)
 
 
-def start_kernel(height, g_ref, e_ref, q_ref, high_ref, low_ref, p_ref, g_near, e_near, q_near, sems, q_sem):
+def start_kernel(height, x_ref, g_ref, e_ref, q_ref, high_ref, low_ref, p_ref, *refs):
+    *piece_refs, g_near, e_near, q_near, sems, q_sem = refs
     replicas, rows, columns = g_ref.shape
     steps = rows // height
     copies = []
@@ -61,27 +62,33 @@
             if index == steps - 2:
                 q_copy.wait()
                 row = pl.ds(0, rows - height)
-            both = jnp.concatenate([high_ref[row], low_ref[row]], axis=0)
+            both = jnp.concatenate([high_ref[row, :columns], low_ref[row]], axis=0)
             term = dot(both, q_near[...], ((1,), (1,)))
             p_ref[row] = term[: row.size] + term[row.size :]
+    high_ref[:, columns:] = jnp.zeros((rows, high_ref.shape[1] - columns), BF16)
+    for flip, piece_ref in enumerate(piece_refs):
+        width = piece_ref.shape[1]
+        piece_ref[...] = high_ref[:, pl.ds(pl.multiple_of((x_ref[0] ^ flip) * width, LANES), width)]
 
 
 def in_hbm(*values):
     return [pltpu.with_memory_space_constraint(value, pltpu.HBM) for value in values]
 
 
-def start(gradient, error, q_turned, height=16):
+def start(place, gradient, error, q_turned, height=16):
     replicas, rows, columns = gradient.shape
+    width = -(-columns // (X * LANES)) * LANES
     far = pl.BlockSpec(memory_space=pltpu.HBM)
     return pl.pallas_call(
         functools.partial(start_kernel, height),
-        in_specs=[far] * 3,
-        out_specs=[VMEM] * 3,
+        in_specs=[SMEM] + [far] * 3,
+        out_specs=[VMEM] * (3 + X),
         out_shape=[
-            jax.ShapeDtypeStruct((rows, columns), BF16),
+            jax.ShapeDtypeStruct((rows, X * width), BF16),
             jax.ShapeDtypeStruct((rows, columns), BF16),
             jax.ShapeDtypeStruct((rows, q_turned.shape[0]), F32),
-        ],
+        ]
+        + [jax.ShapeDtypeStruct((rows, width), BF16)] * X,
         scratch_shapes=[
             pltpu.VMEM(gradient.shape, BF16),
             pltpu.VMEM(error.shape, BF16),
@@ -90,17 +97,16 @@
             pltpu.SemaphoreType.DMA,
         ],
         compiler_params=params(24),
-    )(*in_hbm(gradient, error, q_turned))
-
-
-def right_kernel(blocks, normed, core_ref, *refs):
-    if normed:
-        inverse_ref, *refs = refs
-    own, one, two, three, high_ref, low_ref, mine_ref, theirs_ref, p_ref = refs
+    )(place["x"], *in_hbm(gradient, error, q_turned))
+
+
+def fold(gram):
+    half = gram.shape[0] // 2
+    return jnp.concatenate([gram[:half], gram[half:]], axis=1)
+
+
+def right_kernel(blocks, core_ref, own, one, two, three, high_ref, low_ref, mine_ref, theirs_ref):
     p = (own[...] + two[...]) + (one[...] + three[...])
-    if normed:
-        p = dot(p, inverse_ref[...], ((1,), (1,)), HIGH)
-    p_ref[...] = p
     rank = p.shape[1]
     half = rank // 2
     first = core_ref[0] == 0
@@ -112,62 +118,80 @@
         low = dot(stack[: 2 * rank], low_ref[:, at])
         u = top[:rank] + ((top[rank : 2 * rank] + low[:rank]) + (top[2 * rank :] + low[rank:]))
         mine_ref[block] = jnp.where(first, u[:half], u[half:])
-        theirs_ref[block] = jnp.where(first, u[half:], u[:half]).astype(theirs_ref.dtype)
-    gram = dot(turned, p, ((1,), (0,)), HIGH)
-    gram = jnp.concatenate([gram[:half], gram[half:]], axis=1)
+        theirs_ref[block] = jnp.where(first, u[half:], u[:half]).astype(BF16)
+    gram = fold(dot(turned, p, ((1,), (0,)), HIGH))
     mine_ref[blocks] = gram
-    if theirs_ref.dtype == F32:
-        theirs_ref[blocks] = gram
-    else:
-        for index, part in enumerate(split(gram, 3)):
-            theirs_ref[blocks + index] = part
-
-
-def right(core, parts, high, low, inverse=None, kind=F32):
-    rows, columns = high.shape
+    for index, part in enumerate(split(gram, 3)):
+        theirs_ref[blocks + index] = part
+
+
+def right(place, parts, high, low):
     rank = parts[0].shape[1]
-    blocks = columns // LANES
-    mine = jax.ShapeDtypeStruct((blocks + 1, rank // 2, LANES), F32)
-    theirs = mine if kind == F32 else jax.ShapeDtypeStruct((blocks + 3, rank // 2, LANES), kind)
-    operands = ([] if inverse is None else [inverse]) + list(parts) + [high, low]
-    return pl.pallas_call(
-        functools.partial(right_kernel, blocks, inverse is not None),
-        in_specs=[SMEM] + [VMEM] * len(operands),
+    blocks = low.shape[1] // LANES
+    return pl.pallas_call(
+        functools.partial(right_kernel, blocks),
+        in_specs=[SMEM] + [VMEM] * 6,
+        out_specs=[VMEM] * 2,
+        out_shape=[
+            jax.ShapeDtypeStruct((blocks + 1, rank // 2, LANES), F32),
+            jax.ShapeDtypeStruct((blocks + 3, rank // 2, LANES), BF16),
+        ],
+        compiler_params=params(24),
+    )(place["core"], *parts, high, low)
+
+
+def next_right_kernel(core_ref, x_ref, inverse_ref, *refs):
+    *in_refs, mean_ref, mine_ref, theirs_ref, p_ref, all_ref = refs
+    first = core_ref[0] == 0
+    turned = dot(inverse_ref[...], total_of(in_refs), ((1,), (0,)), HIGH)
+    rank = turned.shape[0]
+    half = rank // 2
+    blocks = mine_ref.shape[0] - 1
+    stack = jnp.concatenate(split(turned, 3), axis=0)
+    for block in range(blocks):
+        top = dot(stack, mean_ref[:, pl.ds(block * LANES, LANES)])
+        u = top[:rank] + (top[rank : 2 * rank] + top[2 * rank :])
+        mine_ref[block] = jnp.where(first, u[:half], u[half:])
+        theirs_ref[block] = jnp.where(first, u[half:], u[:half])
+    gram = fold(dot(turned, turned, ((1,), (1,)), HIGH))
+    mine_ref[blocks] = gram
+    theirs_ref[blocks] = gram
+    all_ref[...] = turned.T
+    rows = p_ref.shape[0]
+    p_ref[...] = all_ref[pl.ds(pl.multiple_of(x_ref[0] * rows, rows), rows)]
+
+
+def next_right(place, inverse, parts, mean):
+    rows, width = mean.shape
+    half = inverse.shape[0] // 2
+    shape = jax.ShapeDtypeStruct((width // LANES + 1, half, LANES), F32)
+    return pl.pallas_call(
+        next_right_kernel,
+        in_specs=[SMEM] * 2 + [VMEM] * (2 + Y),
         out_specs=[VMEM] * 3,
-        out_shape=[mine, theirs, jax.ShapeDtypeStruct((rows, rank), F32)],
-        compiler_params=params(24),
-    )(core, *operands)
-
-
-def cut_kernel(x_ref, a_ref, b_ref, *out_refs):
-    last = a_ref.shape[0] - 1
-    per = out_refs[0].shape[0] - 1
-    gram = a_ref[last] + b_ref[last]
-    for flip, out_ref in enumerate(out_refs):
-        at = pl.ds((x_ref[0] ^ flip) * per, per)
-        out_ref[:per] = a_ref[at] + b_ref[at]
-        out_ref[per] = gram
-
-
-def four(refs, *at):
-    own, one, two, three = [ref[at] if at else ref[...] for ref in refs]
-    return (own + two) + (one + three)
+        out_shape=[shape, shape, jax.ShapeDtypeStruct((rows // X, 2 * half), F32)],
+        scratch_shapes=[pltpu.VMEM((rows, 2 * half), F32)],
+        compiler_params=params(24),
+    )(place["core"], place["x"], inverse, *parts, mean)
+
+
+def total_of(refs, *at):
+    found = [ref[at] if at else ref[...] for ref in refs]
+    if len(found) == 4:
+        found = [found[0] + found[2], found[1] + found[3]]
+    return found[0] + found[1]
 
 
 def halve_kernel(near_ref, *refs):
     *in_refs, keep_ref, give_ref = refs
     rows = keep_ref.shape[1]
     place = near_ref[0] * rows
-    keep_ref[...] = four(in_refs, slice(None), pl.ds(pl.multiple_of(place, rows), rows))
-    give_ref[...] = four(in_refs, slice(None), pl.ds(pl.multiple_of(rows - place, rows), rows))
-
-
-def two_kernel(a_ref, b_ref, out_ref):
-    out_ref[...] = a_ref[...] + b_ref[...]
-
-
-def four_kernel(*refs):
-    refs[-1][...] = four(refs[:-1])
+    keep_ref[...] = total_of(in_refs, slice(None), pl.ds(pl.multiple_of(place, rows), rows))
+    give_ref[...] = total_of(in_refs, slice(None), pl.ds(pl.multiple_of(rows - place, rows), rows))
+
+
+def sum_kernel(*refs):
+    refs[-1][...] = total_of(refs[:-1])
 
 
 def join_kernel(near_ref, here_ref, there_ref, chunk_ref, gram_ref):
@@ -238,8 +262,7 @@
     (part,) = small(sum_coarse_kernel, around(cuts, "x"), [shape], 0, BF16)
     (part,) = small(sum_coarse_kernel, (part, swap(part, "near")), [shape], 0, BF16)
     (part,) = small(sum_coarse_kernel, around(part, "far"), [shape], 0, BF16)
-    here = around(part, "x")
-    return here, [swap(part, "core") for part in here]
+    return part
 
 
 def around(value, axis):
@@ -254,15 +277,13 @@
 
 def all_sum(place, mine, theirs, gradient, error):
     blocks, rows, lanes = mine.shape
-    per = blocks // X
-    full, half = (per + 1, rows, lanes), (per + 1, rows // 2, lanes)
-    cuts = small(cut_kernel, (place["x"], mine, swap(theirs, "core")), [full] * X, 1)
-    keep, give = small(halve_kernel, (place["near"], *around(cuts, "x")), [half] * 2, 1)
-    (both,) = small(two_kernel, (keep, swap(give, "near")), [half])
-    (total,) = small(four_kernel, around(both, "far"), [half])
+    half = (blocks, rows // 2, lanes)
+    keep, give = small(halve_kernel, (place["near"], mine, swap(theirs, "core")), [half] * 2, 1)
+    (both,) = small(sum_kernel, (keep, swap(give, "near")), [half])
+    (total,) = small(sum_kernel, around(both, "far"), [half])
     rank = 2 * rows
     chunk, gram = small(
-        join_kernel, (place["near"], total, swap(total, "near")), [(per, rows, lanes), (rank, rank)], 1
+        join_kernel, (place["near"], total, swap(total, "near")), [(blocks - 1, rows, lanes), (rank, rank)], 1
     )
     ready = inverse_and_fetch(gram, gradient, error)
     here = around(chunk, "x")
@@ -287,34 +308,50 @@
             u_ref[:, at] = jnp.concatenate(split(u, parts), axis=0)
 
 
-def left_kernel(core_ref, x_ref, *refs):
-    *refs, high_ref, low_ref, t_ref, gram_ref, u_ref, packed_ref = refs
-    rows, rank = t_ref.shape
-    columns = high_ref.shape[1]
-    gather(core_ref, x_ref, refs, u_ref, refs[0].shape[0] - 1)
-    u = u_ref[:, :columns]
-    t_ref[...] = dot(high_ref[...], u, ((1,), (1,))) + dot(low_ref[...], u, ((1,), (1,)))
-    half = packed_ref.shape[0]
+def left_kernel(core_ref, x_ref, part_ref, other_ref, *refs):
+    *piece_refs, mean_ref, out_ref = refs
+    height = piece_refs[0].shape[0]
+    for flip, piece_ref in enumerate(piece_refs):
+        mean_ref[pl.ds(pl.multiple_of((x_ref[0] ^ flip) * height, height), height)] = piece_ref[...]
+    per = part_ref.shape[0] - 1
+    first = core_ref[0] == 0
+    u = jnp.concatenate([whole(first, part_ref[block], other_ref[block]) for block in range(per)], axis=1)
+    rows = mean_ref.shape[0]
+    out_ref[:, :rows] = dot(u, mean_ref[...], ((1,), (1,)))
+    quarter = unpack(part_ref)[1]
+    side = quarter.shape[1] // 2
+    quarter = jnp.concatenate([quarter[:, :side], quarter[:, side:]], axis=0)
+    spare = out_ref.shape[0] - quarter.shape[0]
+    out_ref[:, rows:] = jnp.concatenate([quarter, jnp.zeros((spare, side), F32)], axis=0)
+
+
+def left(place, part, pieces):
+    height, width = pieces[0].shape
+    rows = X * height
+    half, lanes = part.shape[1:]
+    return pl.pallas_call(
+        left_kernel,
+        in_specs=[SMEM] * 2 + [VMEM] * (2 + X),
+        out_specs=[VMEM] * 2,
+        out_shape=[
+            jax.ShapeDtypeStruct((rows, width), BF16),
+            jax.ShapeDtypeStruct((2 * half, rows + lanes // 2), F32),
+        ],
+        compiler_params=params(24),
+    )(place["core"], place["x"], part, swap(part, "core"), *pieces)
+
+
+def left_sum_kernel(x_ref, *refs):
+    *in_refs, t_ref, gram_ref = refs
+    rows = t_ref.shape[1]
+    t_ref[...] = total_of(in_refs, slice(None), slice(0, rows))
+    half = gram_ref.shape[0] // 2
     part = half // X
-    for flip in range(X):
-        at = pl.ds(pl.multiple_of((x_ref[0] ^ flip) * part, part), part)
-        packed_ref[at] = unpack(refs[flip])[1]
-    gram_ref[:half] = packed_ref[:, :rank]
-    gram_ref[half:] = packed_ref[:, rank:]
-
-
-def left(place, here, there, high, low):
-    rows, columns = high.shape
-    per, half, _ = here[0].shape
-    rank = 2 * half
-    return pl.pallas_call(
-        left_kernel,
-        in_specs=[SMEM] * 2 + [VMEM] * (2 * X + 2),
-        out_specs=[VMEM] * 2,
-        out_shape=[jax.ShapeDtypeStruct((rows, rank), F32), jax.ShapeDtypeStruct((rank, rank), F32)],
-        scratch_shapes=[pltpu.VMEM((rank, X * (per - 1) * LANES), BF16), pltpu.VMEM((half, LANES), F32)],
-        compiler_params=params(24),
-    )(place["core"], place["x"], *here, *there, high, low)
+    for flip, in_ref in enumerate(in_refs):
+        quarter = in_ref[: 2 * part, rows:]
+        place = (x_ref[0] ^ flip) * part
+        gram_ref[pl.ds(pl.multiple_of(place, part), part)] = quarter[:part]
+        gram_ref[pl.ds(pl.multiple_of(half + place, part), part)] = quarter[part:]
 
 
 def lower_inverse(gram):
@@ -433,12 +470,16 @@
 
 def per_device(gradient, error_buffer, q_start):
     place = {axis: lax.axis_index(axis).astype(jnp.int32).reshape(1) for axis in ("x", "near", "core")}
-    core = place["core"]
-    high, low, term = start(gradient, error_buffer, q_start.T)
-    mine, theirs, _ = right(core, around(term, "y"), high, low, kind=BF16)
-    here, there = coarse_sum(place, mine, theirs)
-    term, gram = left(place, here, there, high, low)
-    mine, theirs, p = right(core, around(term, "y"), high, low, inverse_of(gram))
+    high, low, term, *pieces = start(place, gradient, error_buffer, q_start.T)
+    parts = around(term, "y")
+    pieces = around(pieces, "x")
+    part = coarse_sum(place, *right(place, parts, high, low))
+    mean, term = left(place, part, pieces)
+    rank, width = term.shape
+    term, gram = small(
+        left_sum_kernel, (place["x"], *around(term, "x")), [(rank, width - rank), (rank, rank)], 1
+    )
+    mine, theirs, p = next_right(place, inverse_of(gram), around(term, "y"), mean)
     here, there, ready = all_sum(place, mine, theirs, gradient, error_buffer)
     new_error, q_factor = end(place, here, there, p, *ready)
     return new_error, q_factor.T

time: 114 us -> 108 us (0.947)
  starting transfers between devices: 56.8 us -> 52.7 us
  waiting for transfers between devices: 37.8 us -> 36.2 us
    ppermute x13 -> x10, starting transfers between devices: 20.8 us -> 16.8 us  [swap(): return lax.ppermute(value, axis, [(0, 1), (1, 0)])]
    ppermute x13 -> x10, waiting for transfers between devices: 12 us -> 10.8 us  [swap(): return lax.ppermute(value, axis, [(0, 1), (1, 0)])]
  transfers between devices with their start and end apart: 37 -> 34, of which waited for: 21 -> 19; matrix products, arithmetic and copies ran while one was open for 0% -> 0% of each run, Pallas kernels for 6% -> 6%
where the time goes in v3:
time: 108 us
  starting transfers between devices  52.7 us (49%)
  waiting for transfers between devices  36.2 us (34%)
  Pallas kernels  18.4 us (17%)
    ppermute x24, starting transfers between devices, around(): lax.ppermute(value[flip], axis, [(i, i ^ flip) for i in range(4)])  35.9 us
    ppermute x24, waiting for transfers between devices, around(): lax.ppermute(value[flip], axis, [(i, i ^ flip) for i in range(4)])  25.4 us
    ppermute x10, starting transfers between devices, swap(): return lax.ppermute(value, axis, [(0, 1), (1, 0)])  16.8 us
    ppermute x10, waiting for transfers between devices, swap(): return lax.ppermute(value, axis, [(0, 1), (1, 0)])  10.8 us
    pallas_call x1, Pallas kernels, start(): pl.pallas_call(functools.partial(start_kernel, height), in_specs=[SMEM] +...  4.54 us
    pallas_call x1, Pallas kernels, end(): pl.pallas_call(end_kernel, grid=(columns // width,), in_specs=[SMEM] * 2...  4.48 us
    pallas_call x1, Pallas kernels, inverse_and_fetch(): pl.pallas_call(fetch_kernel, in_specs=[VMEM, far, far], out_specs=[VMEM]...  3.62 us
    pallas_call x1, Pallas kernels, inverse_of(): pl.pallas_call(inverse_kernel, in_specs=[VMEM], out_specs=VMEM, out_shape...  3.24 us
  transfers between devices with their start and end apart: 34, of which 19 were waited for; matrix products, arithmetic and copies ran while one was open for 0% of the time, Pallas kernels for 6%

profile of v3, /device:TPU:1, one launch (start us, length us, event | category | flops | bytes accessed | tf_op | source)
XLA Modules:
  0.0 108.0 jit_solution(7133244390595982522)
XLA Ops:
  0.6 4.5 %shard_map.50 = (bf16[80,3584]{1,0:T(8,128)(2,1)S(1)}, bf16[80,3456]{1,0:T(8,128)(2,1)S(1)}, f32[80,64]{1,0:T(8,128)S(1)}, bf16[80,896]{1,0:T(8,128)(2,1)S(1)}, ...) custom-call(s32[1]{0:T(128)} %bitcast.1.x_ref, bf16[8,80,3456]{2,1,0:T(8,128)(2,1)} %g_ref.3, ...), custom_call_target="tpu_custom_call" | custom-call | tf_op jit(solution)/shard_map/pallas_call | solution.py:82
  5.2 3.7 %collective-permute-start.2 = (f32[80,64]{1,0:T(8,128)S(1)}, f32[80,64]{1,0:T(8,128)S(1)}, u32[]{:S(2)}, u32[]{:S(2)}) collective-permute-start(f32[80,64]{1,0:T(8,128)S(1)} %get-tuple-element.37.own), channel_id=1, source_target_pairs={{0,3},{1,2},{2,1},{3,0},{4,7},{5,6},{6,5},{7,4},{8,11},{9,10},{10,... | collective-permute-start | bytes 61448 | tf_op jit(solution)/shard_map/ppermute | solution.py:271
  8.8 0.3 collective-permute-start.1
  9.2 0.3 collective-permute-start
  9.5 0.7 collective-permute-done.2.three
  10.2 3.1 %collective-permute-done.1.two = f32[80,64]{1,0:T(8,128)S(1)} collective-permute-done((f32[80,64]{1,0:T(8,128)S(1)}, f32[80,64]{1,0:T(8,128)S(1)}, u32[]{:S(2)}, u32[]{:S(2)}) %collective-permute-start.1) | collective-permute-done | bytes 20512 | tf_op jit(solution)/shard_map/ppermute | solution.py:271
  13.3 0.0 collective-permute-done.one
  13.3 0.9 shard_map.51
  14.2 2.1 %collective-permute-start.3 = (bf16[30,32,128]{2,1,0:T(8,128)(2,1)S(1)}, bf16[30,32,128]{2,1,0:T(8,128)(2,1)S(1)}, u32[]{:S(2)}, u32[]{:S(2)}) collective-permute-start(bf16[30,32,128]{2,1,0:T(8,128)(2,1)S(1)} %get-tuple-element.41), channel_id=1, source_target_pairs={{0,4},{4,0},{1,5},{5,1},{2,6},{6,2},{3,7},{7,3},{8,12},{12,8},{9,1... | collective-permute-start | bytes 737288 | tf_op jit(solution)/shard_map/ppermute | solution.py:275
  16.3 1.1 %collective-permute-done.3.b_ref = bf16[30,32,128]{2,1,0:T(8,128)(2,1)S(1)} collective-permute-done((bf16[30,32,128]{2,1,0:T(8,128)(2,1)S(1)}, bf16[30,32,128]{2,1,0:T(8,128)(2,1)S(1)}, u32[]{:S(2)}, u32[]{:S(2)}) %collective-permute-start.3) | collective-permute-done | bytes 245792 | tf_op jit(solution)/shard_map/ppermute | solution.py:275
  17.4 0.1 shard_map.52
  17.5 1.3 %collective-permute-start.4 = (bf16[8,32,128]{2,1,0:T(8,128)(2,1)S(1)}, bf16[8,32,128]{2,1,0:T(8,128)(2,1)S(1)}, u32[]{:S(2)}, u32[]{:S(2)}) collective-permute-start(bf16[8,32,128]{2,1,0:T(8,128)(2,1)S(1)} %get-tuple-element.43), channel_id=1, source_target_pairs={{0,64},{64,0},{128,192},{192,128},{1,65},{65,1},{129,193},{193,129... | collective-permute-start | bytes 196616 | tf_op jit(solution)/shard_map/ppermute | solution.py:271
  18.8 2.4 %collective-permute-start.5 = (bf16[8,32,128]{2,1,0:T(8,128)(2,1)S(1)}, bf16[8,32,128]{2,1,0:T(8,128)(2,1)S(1)}, u32[]{:S(2)}, u32[]{:S(2)}) collective-permute-start(bf16[8,32,128]{2,1,0:T(8,128)(2,1)S(1)} %get-tuple-element.44), channel_id=1, source_target_pairs={{0,128},{64,192},{128,0},{192,64},{1,129},{65,193},{129,1},{193,65... | collective-permute-start | bytes 196616 | tf_op jit(solution)/shard_map/ppermute | solution.py:271
  21.3 0.2 collective-permute-start.6
  21.5 2.7 %collective-permute-done.5.refs_2_ = bf16[8,32,128]{2,1,0:T(8,128)(2,1)S(1)} collective-permute-done((bf16[8,32,128]{2,1,0:T(8,128)(2,1)S(1)}, bf16[8,32,128]{2,1,0:T(8,128)(2,1)S(1)}, u32[]{:S(2)}, u32[]{:S(2)}) %collective-permute-start.5) | collective-permute-done | bytes 65568 | tf_op jit(solution)/shard_map/ppermute | solution.py:271
  24.2 1.5 %collective-permute-done.6.refs_3_ = bf16[8,32,128]{2,1,0:T(8,128)(2,1)S(1)} collective-permute-done((bf16[8,32,128]{2,1,0:T(8,128)(2,1)S(1)}, bf16[8,32,128]{2,1,0:T(8,128)(2,1)S(1)}, u32[]{:S(2)}, u32[]{:S(2)}) %collective-permute-start.6) | collective-permute-done | bytes 65568 | tf_op jit(solution)/shard_map/ppermute | solution.py:271
  25.8 1.7 %collective-permute-start.7 = (bf16[8,32,128]{2,1,0:T(8,128)(2,1)S(1)}, bf16[8,32,128]{2,1,0:T(8,128)(2,1)S(1)}, u32[]{:S(2)}, u32[]{:S(2)}) collective-permute-start(bf16[8,32,128]{2,1,0:T(8,128)(2,1)S(1)} %shard_map.53.refs_0_), channel_id=1, source_target_pairs={{0,8},{8,0},{1,9},{9,1},{2,10},{10,2},{3,11},{11,3},{4,12},{12,4},... | collective-permute-start | bytes 196616 | tf_op jit(solution)/shard_map/ppermute | solution.py:275
  27.5 1.7 %collective-permute-done.7.refs_1_ = bf16[8,32,128]{2,1,0:T(8,128)(2,1)S(1)} collective-permute-done((bf16[8,32,128]{2,1,0:T(8,128)(2,1)S(1)}, bf16[8,32,128]{2,1,0:T(8,128)(2,1)S(1)}, u32[]{:S(2)}, u32[]{:S(2)}) %collective-permute-start.7) | collective-permute-done | bytes 65568 | tf_op jit(solution)/shard_map/ppermute | solution.py:275
  29.2 5.9 %collective-permute-start.10 = (bf16[8,32,128]{2,1,0:T(8,128)(2,1)S(1)}, bf16[8,32,128]{2,1,0:T(8,128)(2,1)S(1)}, u32[]{:S(2)}, u32[]{:S(2)}) collective-permute-start(bf16[8,32,128]{2,1,0:T(8,128)(2,1)S(1)} %shard_map.54.refs_0_), channel_id=1, source_target_pairs={{0,48},{16,32},{32,16},{48,0},{1,49},{17,33},{33,17},{49,1},{2,50}... | collective-permute-start | bytes 196616 | tf_op jit(solution)/shard_map/ppermute | solution.py:271
  35.1 0.2 collective-permute-start.12
  35.2 2.4 %collective-permute-start.13 = (bf16[80,896]{1,0:T(8,128)(2,1)S(1)}, bf16[80,896]{1,0:T(8,128)(2,1)S(1)}, u32[]{:S(2)}, u32[]{:S(2)}) collective-permute-start(bf16[80,896]{1,0:T(8,128)(2,1)S(1)} %get-tuple-element.48), channel_id=1, source_target_pairs={{0,128},{64,192},{128,0},{192,64},{1,129},{65,193},{129,1},{193,65... | collective-permute-start | bytes 430088 | tf_op jit(solution)/shard_map/ppermute | solution.py:271
  37.6 1.3 %collective-permute-start.14 = (bf16[80,896]{1,0:T(8,128)(2,1)S(1)}, bf16[80,896]{1,0:T(8,128)(2,1)S(1)}, u32[]{:S(2)}, u32[]{:S(2)}) collective-permute-start(bf16[80,896]{1,0:T(8,128)(2,1)S(1)} %get-tuple-element.49), channel_id=1, source_target_pairs={{0,192},{64,128},{128,64},{192,0},{1,193},{65,129},{129,65},{193,1... | collective-permute-start | bytes 430088 | tf_op jit(solution)/shard_map/ppermute | solution.py:271
  39.0 1.0 collective-permute-start.9
  39.9 1.2 %collective-permute-start.8 = (bf16[8,32,128]{2,1,0:T(8,128)(2,1)S(1)}, bf16[8,32,128]{2,1,0:T(8,128)(2,1)S(1)}, u32[]{:S(2)}, u32[]{:S(2)}) collective-permute-start(bf16[8,32,128]{2,1,0:T(8,128)(2,1)S(1)} %shard_map.54.refs_0_), channel_id=1, source_target_pairs={{0,16},{16,0},{32,48},{48,32},{1,17},{17,1},{33,49},{49,33},{2,18}... | collective-permute-start | bytes 196616 | tf_op jit(solution)/shard_map/ppermute | solution.py:271
  41.1 5.4 %collective-permute-done.9.refs_2_ = bf16[8,32,128]{2,1,0:T(8,128)(2,1)S(1)} collective-permute-done((bf16[8,32,128]{2,1,0:T(8,128)(2,1)S(1)}, bf16[8,32,128]{2,1,0:T(8,128)(2,1)S(1)}, u32[]{:S(2)}, u32[]{:S(2)}) %collective-permute-start.9) | collective-permute-done | bytes 65568 | tf_op jit(solution)/shard_map/ppermute | solution.py:271
  46.6 5.1 %collective-permute-start.11 = (bf16[8,32,128]{2,1,0:T(8,128)(2,1)S(1)}, bf16[8,32,128]{2,1,0:T(8,128)(2,1)S(1)}, u32[]{:S(2)}, u32[]{:S(2)}) collective-permute-start(bf16[8,32,128]{2,1,0:T(8,128)(2,1)S(1)} %shard_map.55.part_ref), channel_id=1, source_target_pairs={{0,4},{4,0},{1,5},{5,1},{2,6},{6,2},{3,7},{7,3},{8,12},{12,8},{9,1... | collective-permute-start | bytes 196616 | tf_op jit(solution)/shard_map/ppermute | solution.py:275
  51.7 0.9 collective-permute-done.11.other_ref
  52.6 0.3 shard_map.56
  53.0 0.5 collective-permute-start.17
  53.4 0.0 collective-permute-start.16
  53.5 2.9 %collective-permute-start.15 = (f32[64,384]{1,0:T(8,128)S(1)}, f32[64,384]{1,0:T(8,128)S(1)}, u32[]{:S(2)}, u32[]{:S(2)}) collective-permute-start(f32[64,384]{1,0:T(8,128)S(1)} %get-tuple-element.50.refs_0_), channel_id=1, source_target_pairs={{0,64},{64,0},{128,192},{192,128},{1,65},{65,1},{129,193},{193,129... | collective-permute-start | bytes 294920 | tf_op jit(solution)/shard_map/ppermute | solution.py:271
  56.3 3.7 %collective-permute-done.17.refs_3_ = f32[64,384]{1,0:T(8,128)S(1)} collective-permute-done((f32[64,384]{1,0:T(8,128)S(1)}, f32[64,384]{1,0:T(8,128)S(1)}, u32[]{:S(2)}, u32[]{:S(2)}) %collective-permute-start.17) | collective-permute-done | bytes 98336 | tf_op jit(solution)/shard_map/ppermute | solution.py:271
  60.0 0.6 collective-permute-done.15.refs_1_
  60.7 0.1 shard_map.57
  60.7 1.1 collective-permute-start.20
  61.8 0.8 collective-permute-start.19
  62.6 1.4 %collective-permute-start.18 = (f32[64,320]{1,0:T(8,128)S(1)}, f32[64,320]{1,0:T(8,128)S(1)}, u32[]{:S(2)}, u32[]{:S(2)}) collective-permute-start(f32[64,320]{1,0:T(8,128)S(1)} %get-tuple-element.52.refs_0_), channel_id=1, source_target_pairs={{0,1},{1,0},{2,3},{3,2},{4,5},{5,4},{6,7},{7,6},{8,9},{9,8},{10,11... | collective-permute-start | bytes 245768 | tf_op jit(solution)/shard_map/ppermute | solution.py:271
  64.0 3.2 %shard_map.58.inverse_ref = f32[64,64]{1,0:T(8,128)S(1)} custom-call(f32[64,64]{1,0:T(8,128)S(1)} %get-tuple-element.51.gram_ref), custom_call_target="tpu_custom_call" | custom-call | flops 10000000 | bytes 5000000 | tf_op jit(solution)/shard_map/pallas_call | solution.py:388
  67.3 0.1 collective-permute-done.18.refs_1_
  67.4 0.9 shard_map.59
  68.3 2.7 %collective-permute-start.21 = (f32[8,32,128]{2,1,0:T(8,128)S(1)}, f32[8,32,128]{2,1,0:T(8,128)S(1)}, u32[]{:S(2)}, u32[]{:S(2)}) collective-permute-start(f32[8,32,128]{2,1,0:T(8,128)S(1)} %get-tuple-element.55), channel_id=1, source_target_pairs={{0,4},{4,0},{1,5},{5,1},{2,6},{6,2},{3,7},{7,3},{8,12},{12,8},{9,1... | collective-permute-start | bytes 393224 | tf_op jit(solution)/shard_map/ppermute | solution.py:275
  71.0 1.0 collective-permute-done.21.refs_1_
  72.0 1.2 %collective-permute-start.22 = (f32[8,16,128]{2,1,0:T(8,128)S(1)}, f32[8,16,128]{2,1,0:T(8,128)S(1)}, u32[]{:S(2)}, u32[]{:S(2)}) collective-permute-start(f32[8,16,128]{2,1,0:T(8,128)S(1)} %get-tuple-element.57), channel_id=1, source_target_pairs={{0,8},{8,0},{1,9},{9,1},{2,10},{10,2},{3,11},{11,3},{4,12},{12,4},... | collective-permute-start | bytes 196616 | tf_op jit(solution)/shard_map/ppermute | solution.py:275
  73.2 2.0 %collective-permute-done.22.refs_1_ = f32[8,16,128]{2,1,0:T(8,128)S(1)} collective-permute-done((f32[8,16,128]{2,1,0:T(8,128)S(1)}, f32[8,16,128]{2,1,0:T(8,128)S(1)}, u32[]{:S(2)}, u32[]{:S(2)}) %collective-permute-start.22) | collective-permute-done | bytes 65568 | tf_op jit(solution)/shard_map/ppermute | solution.py:275
  75.2 2.0 %collective-permute-start.25 = (f32[8,16,128]{2,1,0:T(8,128)S(1)}, f32[8,16,128]{2,1,0:T(8,128)S(1)}, u32[]{:S(2)}, u32[]{:S(2)}) collective-permute-start(f32[8,16,128]{2,1,0:T(8,128)S(1)} %shard_map.61.refs_0_), channel_id=1, source_target_pairs={{0,48},{16,32},{32,16},{48,0},{1,49},{17,33},{33,17},{49,1},{2,50}... | collective-permute-start | bytes 196616 | tf_op jit(solution)/shard_map/ppermute | solution.py:271
  77.2 2.8 %collective-permute-start.24 = (f32[8,16,128]{2,1,0:T(8,128)S(1)}, f32[8,16,128]{2,1,0:T(8,128)S(1)}, u32[]{:S(2)}, u32[]{:S(2)}) collective-permute-start(f32[8,16,128]{2,1,0:T(8,128)S(1)} %shard_map.61.refs_0_), channel_id=1, source_target_pairs={{0,32},{16,48},{32,0},{48,16},{1,33},{17,49},{33,1},{49,17},{2,34}... | collective-permute-start | bytes 196616 | tf_op jit(solution)/shard_map/ppermute | solution.py:271
  80.0 1.0 collective-permute-start.23
  81.0 3.7 %collective-permute-done.24.refs_2_ = f32[8,16,128]{2,1,0:T(8,128)S(1)} collective-permute-done((f32[8,16,128]{2,1,0:T(8,128)S(1)}, f32[8,16,128]{2,1,0:T(8,128)S(1)}, u32[]{:S(2)}, u32[]{:S(2)}) %collective-permute-start.24) | collective-permute-done | bytes 65568 | tf_op jit(solution)/shard_map/ppermute | solution.py:271
  84.7 3.7 %collective-permute-done.23.refs_1_ = f32[8,16,128]{2,1,0:T(8,128)S(1)} collective-permute-done((f32[8,16,128]{2,1,0:T(8,128)S(1)}, f32[8,16,128]{2,1,0:T(8,128)S(1)}, u32[]{:S(2)}, u32[]{:S(2)}) %collective-permute-start.23) | collective-permute-done | bytes 65568 | tf_op jit(solution)/shard_map/ppermute | solution.py:271
  88.4 0.1 collective-permute-start.26
  88.5 3.1 %collective-permute-done.26.there_ref = f32[8,16,128]{2,1,0:T(8,128)S(1)} collective-permute-done((f32[8,16,128]{2,1,0:T(8,128)S(1)}, f32[8,16,128]{2,1,0:T(8,128)S(1)}, u32[]{:S(2)}, u32[]{:S(2)}) %collective-permute-start.26) | collective-permute-done | bytes 65568 | tf_op jit(solution)/shard_map/ppermute | solution.py:275
  91.6 0.1 shard_map.63
  91.7 1.4 %collective-permute-start.29 = (f32[7,32,128]{2,1,0:T(8,128)S(1)}, f32[7,32,128]{2,1,0:T(8,128)S(1)}, u32[]{:S(2)}, u32[]{:S(2)}) collective-permute-start(f32[7,32,128]{2,1,0:T(8,128)S(1)} %get-tuple-element.58.refs_0_), channel_id=1, source_target_pairs={{0,192},{64,128},{128,64},{192,0},{1,193},{65,129},{129,65},{193,1... | collective-permute-start | bytes 344072 | tf_op jit(solution)/shard_map/ppermute | solution.py:271
  93.1 0.2 collective-permute-start.28
  93.2 1.7 %collective-permute-start.27 = (f32[7,32,128]{2,1,0:T(8,128)S(1)}, f32[7,32,128]{2,1,0:T(8,128)S(1)}, u32[]{:S(2)}, u32[]{:S(2)}) collective-permute-start(f32[7,32,128]{2,1,0:T(8,128)S(1)} %get-tuple-element.58.refs_0_), channel_id=1, source_target_pairs={{0,64},{64,0},{128,192},{192,128},{1,65},{65,1},{129,193},{193,129... | collective-permute-start | bytes 344072 | tf_op jit(solution)/shard_map/ppermute | solution.py:271
  95.0 3.0 %collective-permute-start.30 = (f32[7,32,128]{2,1,0:T(8,128)S(1)}, f32[7,32,128]{2,1,0:T(8,128)S(1)}, u32[]{:S(2)}, u32[]{:S(2)}) collective-permute-start(f32[7,32,128]{2,1,0:T(8,128)S(1)} %get-tuple-element.58.refs_0_), channel_id=1, source_target_pairs={{0,4},{4,0},{1,5},{5,1},{2,6},{6,2},{3,7},{7,3},{8,12},{12,8},{9,1... | collective-permute-start | bytes 344072 | tf_op jit(solution)/shard_map/ppermute | solution.py:275
  97.9 3.6 %shard_map.64 = (f32[64,64]{1,0:T(8,128)S(1)}, bf16[8,80,3456]{2,1,0:T(8,128)(2,1)S(1)}, bf16[8,80,3456]{2,1,0:T(8,128)(2,1)S(1)}) custom-call(f32[64,64]{1,0:T(8,128)S(1)} %get-tuple-element.59.gram_ref, bf16[8,80,3456]{2,1,0:T(8,128)(2,1)} %g_ref.3, bf16[8,80,3456]{2,1,0:T(8,128)(2,1)} %e_ref.3), custom_call_target="tpu_custom_call" | custom-call | flops 10000000 | bytes 5000000 | tf_op jit(solution)/shard_map/pallas_call | solution.py:412
  101.6 0.3 collective-permute-start.31
  101.9 0.3 collective-permute-start.32
  102.2 0.2 collective-permute-start.33
  102.5 0.6 collective-permute-done.31.refs_5_
  103.0 0.2 collective-permute-done.32.refs_6_
  103.3 0.3 collective-permute-done.33.refs_7_
  103.5 4.5 %shard_map.65 = (bf16[8,80,3456]{2,1,0:T(8,128)(2,1)}, f32[64,3456]{1,0:T(8,128)}) custom-call(s32[1]{0:T(128)} %bitcast.core_ref, s32[1]{0:T(128)} %bitcast.1.x_ref, f32[7,32,128]{2,1,0:T(8,128)S(1)} %get-tuple-element.58.refs_0_, f32[7,32,128]{2,1,0:T(8,128)S(1)} %collective-permute-done.27.refs_1_, f32[7,32,128]{2,1,0:T(8,128)S(1)} %collective-permute-done.28.refs_2_, ...), custom_call_target="tpu_custom_call" | custom-call | tf_op jit(solution)/shard_map/pallas_call | solution.py:457
  (20 shorter events, 0.2 us)
Async XLA Ops:
  5.2 5.0 %collective-permute-start.2 = (f32[80,64]{1,0:T(8,128)S(1)}, f32[80,64]{1,0:T(8,128)S(1)}, u32[]{:S(2)}, u32[]{:S(2)}) collective-permute-start(f32[80,64]{1,0:T(8,128)S(1)} %get-tuple-element.37.own), channel_id=1, source_target_pairs={{0,3},{1,2},{2,1},{3,0},{4,7},{5,6},{6,5},{7,4},{8,11},{9,10},{10,... | collective-permute-start | bytes 61448 | tf_op jit(solution)/shard_map/ppermute | solution.py:271
  8.8 4.5 %collective-permute-start.1 = (f32[80,64]{1,0:T(8,128)S(1)}, f32[80,64]{1,0:T(8,128)S(1)}, u32[]{:S(2)}, u32[]{:S(2)}) collective-permute-start(f32[80,64]{1,0:T(8,128)S(1)} %get-tuple-element.37.own), channel_id=1, source_target_pairs={{0,2},{1,3},{2,0},{3,1},{4,6},{5,7},{6,4},{7,5},{8,10},{9,11},{10,... | collective-permute-start | bytes 61448 | tf_op jit(solution)/shard_map/ppermute | solution.py:271
  9.2 4.1 %collective-permute-start = (f32[80,64]{1,0:T(8,128)S(1)}, f32[80,64]{1,0:T(8,128)S(1)}, u32[]{:S(2)}, u32[]{:S(2)}) collective-permute-start(f32[80,64]{1,0:T(8,128)S(1)} %get-tuple-element.37.own), channel_id=1, source_target_pairs={{0,1},{1,0},{2,3},{3,2},{4,5},{5,4},{6,7},{7,6},{8,9},{9,8},{10,11... | collective-permute-start | bytes 61448 | tf_op jit(solution)/shard_map/ppermute | solution.py:271
  14.2 3.2 %collective-permute-start.3 = (bf16[30,32,128]{2,1,0:T(8,128)(2,1)S(1)}, bf16[30,32,128]{2,1,0:T(8,128)(2,1)S(1)}, u32[]{:S(2)}, u32[]{:S(2)}) collective-permute-start(bf16[30,32,128]{2,1,0:T(8,128)(2,1)S(1)} %get-tuple-element.41), channel_id=1, source_target_pairs={{0,4},{4,0},{1,5},{5,1},{2,6},{6,2},{3,7},{7,3},{8,12},{12,8},{9,1... | collective-permute-start | bytes 737288 | tf_op jit(solution)/shard_map/ppermute | solution.py:275
  17.5 3.9 %collective-permute-start.4 = (bf16[8,32,128]{2,1,0:T(8,128)(2,1)S(1)}, bf16[8,32,128]{2,1,0:T(8,128)(2,1)S(1)}, u32[]{:S(2)}, u32[]{:S(2)}) collective-permute-start(bf16[8,32,128]{2,1,0:T(8,128)(2,1)S(1)} %get-tuple-element.43), channel_id=1, source_target_pairs={{0,64},{64,0},{128,192},{192,128},{1,65},{65,1},{129,193},{193,129... | collective-permute-start | bytes 196616 | tf_op jit(solution)/shard_map/ppermute | solution.py:271
  18.8 5.4 %collective-permute-start.5 = (bf16[8,32,128]{2,1,0:T(8,128)(2,1)S(1)}, bf16[8,32,128]{2,1,0:T(8,128)(2,1)S(1)}, u32[]{:S(2)}, u32[]{:S(2)}) collective-permute-start(bf16[8,32,128]{2,1,0:T(8,128)(2,1)S(1)} %get-tuple-element.44), channel_id=1, source_target_pairs={{0,128},{64,192},{128,0},{192,64},{1,129},{65,193},{129,1},{193,65... | collective-permute-start | bytes 196616 | tf_op jit(solution)/shard_map/ppermute | solution.py:271
  21.3 4.5 %collective-permute-start.6 = (bf16[8,32,128]{2,1,0:T(8,128)(2,1)S(1)}, bf16[8,32,128]{2,1,0:T(8,128)(2,1)S(1)}, u32[]{:S(2)}, u32[]{:S(2)}) collective-permute-start(bf16[8,32,128]{2,1,0:T(8,128)(2,1)S(1)} %get-tuple-element.45), channel_id=1, source_target_pairs={{0,192},{64,128},{128,64},{192,0},{1,193},{65,129},{129,65},{193,1... | collective-permute-start | bytes 196616 | tf_op jit(solution)/shard_map/ppermute | solution.py:271
  25.8 3.4 %collective-permute-start.7 = (bf16[8,32,128]{2,1,0:T(8,128)(2,1)S(1)}, bf16[8,32,128]{2,1,0:T(8,128)(2,1)S(1)}, u32[]{:S(2)}, u32[]{:S(2)}) collective-permute-start(bf16[8,32,128]{2,1,0:T(8,128)(2,1)S(1)} %shard_map.53.refs_0_), channel_id=1, source_target_pairs={{0,8},{8,0},{1,9},{9,1},{2,10},{10,2},{3,11},{11,3},{4,12},{12,4},... | collective-permute-start | bytes 196616 | tf_op jit(solution)/shard_map/ppermute | solution.py:275
  29.2 10.8 %collective-permute-start.10 = (bf16[8,32,128]{2,1,0:T(8,128)(2,1)S(1)}, bf16[8,32,128]{2,1,0:T(8,128)(2,1)S(1)}, u32[]{:S(2)}, u32[]{:S(2)}) collective-permute-start(bf16[8,32,128]{2,1,0:T(8,128)(2,1)S(1)} %shard_map.54.refs_0_), channel_id=1, source_target_pairs={{0,48},{16,32},{32,16},{48,0},{1,49},{17,33},{33,17},{49,1},{2,50}... | collective-permute-start | bytes 196616 | tf_op jit(solution)/shard_map/ppermute | solution.py:271
  35.1 16.6 %collective-permute-start.12 = (bf16[80,896]{1,0:T(8,128)(2,1)S(1)}, bf16[80,896]{1,0:T(8,128)(2,1)S(1)}, u32[]{:S(2)}, u32[]{:S(2)}) collective-permute-start(bf16[80,896]{1,0:T(8,128)(2,1)S(1)} %get-tuple-element.47), channel_id=1, source_target_pairs={{0,64},{64,0},{128,192},{192,128},{1,65},{65,1},{129,193},{193,129... | collective-permute-start | bytes 430088 | tf_op jit(solution)/shard_map/ppermute | solution.py:271
  35.2 16.5 %collective-permute-start.13 = (bf16[80,896]{1,0:T(8,128)(2,1)S(1)}, bf16[80,896]{1,0:T(8,128)(2,1)S(1)}, u32[]{:S(2)}, u32[]{:S(2)}) collective-permute-start(bf16[80,896]{1,0:T(8,128)(2,1)S(1)} %get-tuple-element.48), channel_id=1, source_target_pairs={{0,128},{64,192},{128,0},{192,64},{1,129},{65,193},{129,1},{193,65... | collective-permute-start | bytes 430088 | tf_op jit(solution)/shard_map/ppermute | solution.py:271
  37.6 14.1 %collective-permute-start.14 = (bf16[80,896]{1,0:T(8,128)(2,1)S(1)}, bf16[80,896]{1,0:T(8,128)(2,1)S(1)}, u32[]{:S(2)}, u32[]{:S(2)}) collective-permute-start(bf16[80,896]{1,0:T(8,128)(2,1)S(1)} %get-tuple-element.49), channel_id=1, source_target_pairs={{0,192},{64,128},{128,64},{192,0},{1,193},{65,129},{129,65},{193,1... | collective-permute-start | bytes 430088 | tf_op jit(solution)/shard_map/ppermute | solution.py:271
  39.0 7.6 %collective-permute-start.9 = (bf16[8,32,128]{2,1,0:T(8,128)(2,1)S(1)}, bf16[8,32,128]{2,1,0:T(8,128)(2,1)S(1)}, u32[]{:S(2)}, u32[]{:S(2)}) collective-permute-start(bf16[8,32,128]{2,1,0:T(8,128)(2,1)S(1)} %shard_map.54.refs_0_), channel_id=1, source_target_pairs={{0,32},{16,48},{32,0},{48,16},{1,33},{17,49},{33,1},{49,17},{2,34}... | collective-permute-start | bytes 196616 | tf_op jit(solution)/shard_map/ppermute | solution.py:271
  39.9 6.6 %collective-permute-start.8 = (bf16[8,32,128]{2,1,0:T(8,128)(2,1)S(1)}, bf16[8,32,128]{2,1,0:T(8,128)(2,1)S(1)}, u32[]{:S(2)}, u32[]{:S(2)}) collective-permute-start(bf16[8,32,128]{2,1,0:T(8,128)(2,1)S(1)} %shard_map.54.refs_0_), channel_id=1, source_target_pairs={{0,16},{16,0},{32,48},{48,32},{1,17},{17,1},{33,49},{49,33},{2,18}... | collective-permute-start | bytes 196616 | tf_op jit(solution)/shard_map/ppermute | solution.py:271
  46.6 6.0 %collective-permute-start.11 = (bf16[8,32,128]{2,1,0:T(8,128)(2,1)S(1)}, bf16[8,32,128]{2,1,0:T(8,128)(2,1)S(1)}, u32[]{:S(2)}, u32[]{:S(2)}) collective-permute-start(bf16[8,32,128]{2,1,0:T(8,128)(2,1)S(1)} %shard_map.55.part_ref), channel_id=1, source_target_pairs={{0,4},{4,0},{1,5},{5,1},{2,6},{6,2},{3,7},{7,3},{8,12},{12,8},{9,1... | collective-permute-start | bytes 196616 | tf_op jit(solution)/shard_map/ppermute | solution.py:275
  53.0 7.0 %collective-permute-start.17 = (f32[64,384]{1,0:T(8,128)S(1)}, f32[64,384]{1,0:T(8,128)S(1)}, u32[]{:S(2)}, u32[]{:S(2)}) collective-permute-start(f32[64,384]{1,0:T(8,128)S(1)} %get-tuple-element.50.refs_0_), channel_id=1, source_target_pairs={{0,192},{64,128},{128,64},{192,0},{1,193},{65,129},{129,65},{193,1... | collective-permute-start | bytes 294920 | tf_op jit(solution)/shard_map/ppermute | solution.py:271
  53.4 6.6 %collective-permute-start.16 = (f32[64,384]{1,0:T(8,128)S(1)}, f32[64,384]{1,0:T(8,128)S(1)}, u32[]{:S(2)}, u32[]{:S(2)}) collective-permute-start(f32[64,384]{1,0:T(8,128)S(1)} %get-tuple-element.50.refs_0_), channel_id=1, source_target_pairs={{0,128},{64,192},{128,0},{192,64},{1,129},{65,193},{129,1},{193,65... | collective-permute-start | bytes 294920 | tf_op jit(solution)/shard_map/ppermute | solution.py:271
  53.5 7.2 %collective-permute-start.15 = (f32[64,384]{1,0:T(8,128)S(1)}, f32[64,384]{1,0:T(8,128)S(1)}, u32[]{:S(2)}, u32[]{:S(2)}) collective-permute-start(f32[64,384]{1,0:T(8,128)S(1)} %get-tuple-element.50.refs_0_), channel_id=1, source_target_pairs={{0,64},{64,0},{128,192},{192,128},{1,65},{65,1},{129,193},{193,129... | collective-permute-start | bytes 294920 | tf_op jit(solution)/shard_map/ppermute | solution.py:271
  60.7 6.5 %collective-permute-start.20 = (f32[64,320]{1,0:T(8,128)S(1)}, f32[64,320]{1,0:T(8,128)S(1)}, u32[]{:S(2)}, u32[]{:S(2)}) collective-permute-start(f32[64,320]{1,0:T(8,128)S(1)} %get-tuple-element.52.refs_0_), channel_id=1, source_target_pairs={{0,3},{1,2},{2,1},{3,0},{4,7},{5,6},{6,5},{7,4},{8,11},{9,10},{10,... | collective-permute-start | bytes 245768 | tf_op jit(solution)/shard_map/ppermute | solution.py:271
  61.8 5.5 %collective-permute-start.19 = (f32[64,320]{1,0:T(8,128)S(1)}, f32[64,320]{1,0:T(8,128)S(1)}, u32[]{:S(2)}, u32[]{:S(2)}) collective-permute-start(f32[64,320]{1,0:T(8,128)S(1)} %get-tuple-element.52.refs_0_), channel_id=1, source_target_pairs={{0,2},{1,3},{2,0},{3,1},{4,6},{5,7},{6,4},{7,5},{8,10},{9,11},{10,... | collective-permute-start | bytes 245768 | tf_op jit(solution)/shard_map/ppermute | solution.py:271
  62.6 4.8 %collective-permute-start.18 = (f32[64,320]{1,0:T(8,128)S(1)}, f32[64,320]{1,0:T(8,128)S(1)}, u32[]{:S(2)}, u32[]{:S(2)}) collective-permute-start(f32[64,320]{1,0:T(8,128)S(1)} %get-tuple-element.52.refs_0_), channel_id=1, source_target_pairs={{0,1},{1,0},{2,3},{3,2},{4,5},{5,4},{6,7},{7,6},{8,9},{9,8},{10,11... | collective-permute-start | bytes 245768 | tf_op jit(solution)/shard_map/ppermute | solution.py:271
  68.3 3.7 %collective-permute-start.21 = (f32[8,32,128]{2,1,0:T(8,128)S(1)}, f32[8,32,128]{2,1,0:T(8,128)S(1)}, u32[]{:S(2)}, u32[]{:S(2)}) collective-permute-start(f32[8,32,128]{2,1,0:T(8,128)S(1)} %get-tuple-element.55), channel_id=1, source_target_pairs={{0,4},{4,0},{1,5},{5,1},{2,6},{6,2},{3,7},{7,3},{8,12},{12,8},{9,1... | collective-permute-start | bytes 393224 | tf_op jit(solution)/shard_map/ppermute | solution.py:275
  72.0 3.2 %collective-permute-start.22 = (f32[8,16,128]{2,1,0:T(8,128)S(1)}, f32[8,16,128]{2,1,0:T(8,128)S(1)}, u32[]{:S(2)}, u32[]{:S(2)}) collective-permute-start(f32[8,16,128]{2,1,0:T(8,128)S(1)} %get-tuple-element.57), channel_id=1, source_target_pairs={{0,8},{8,0},{1,9},{9,1},{2,10},{10,2},{3,11},{11,3},{4,12},{12,4},... | collective-permute-start | bytes 196616 | tf_op jit(solution)/shard_map/ppermute | solution.py:275
  75.2 5.7 %collective-permute-start.25 = (f32[8,16,128]{2,1,0:T(8,128)S(1)}, f32[8,16,128]{2,1,0:T(8,128)S(1)}, u32[]{:S(2)}, u32[]{:S(2)}) collective-permute-start(f32[8,16,128]{2,1,0:T(8,128)S(1)} %shard_map.61.refs_0_), channel_id=1, source_target_pairs={{0,48},{16,32},{32,16},{48,0},{1,49},{17,33},{33,17},{49,1},{2,50}... | collective-permute-start | bytes 196616 | tf_op jit(solution)/shard_map/ppermute | solution.py:271
  77.2 7.5 %collective-permute-start.24 = (f32[8,16,128]{2,1,0:T(8,128)S(1)}, f32[8,16,128]{2,1,0:T(8,128)S(1)}, u32[]{:S(2)}, u32[]{:S(2)}) collective-permute-start(f32[8,16,128]{2,1,0:T(8,128)S(1)} %shard_map.61.refs_0_), channel_id=1, source_target_pairs={{0,32},{16,48},{32,0},{48,16},{1,33},{17,49},{33,1},{49,17},{2,34}... | collective-permute-start | bytes 196616 | tf_op jit(solution)/shard_map/ppermute | solution.py:271
  80.0 8.4 %collective-permute-start.23 = (f32[8,16,128]{2,1,0:T(8,128)S(1)}, f32[8,16,128]{2,1,0:T(8,128)S(1)}, u32[]{:S(2)}, u32[]{:S(2)}) collective-permute-start(f32[8,16,128]{2,1,0:T(8,128)S(1)} %shard_map.61.refs_0_), channel_id=1, source_target_pairs={{0,16},{16,0},{32,48},{48,32},{1,17},{17,1},{33,49},{49,33},{2,18}... | collective-permute-start | bytes 196616 | tf_op jit(solution)/shard_map/ppermute | solution.py:271
  88.4 3.2 %collective-permute-start.26 = (f32[8,16,128]{2,1,0:T(8,128)S(1)}, f32[8,16,128]{2,1,0:T(8,128)S(1)}, u32[]{:S(2)}, u32[]{:S(2)}) collective-permute-start(f32[8,16,128]{2,1,0:T(8,128)S(1)} %shard_map.62.here_ref), channel_id=1, source_target_pairs={{0,8},{8,0},{1,9},{9,1},{2,10},{10,2},{3,11},{11,3},{4,12},{12,4},... | collective-permute-start | bytes 196616 | tf_op jit(solution)/shard_map/ppermute | solution.py:275
  91.7 9.9 %collective-permute-start.29 = (f32[7,32,128]{2,1,0:T(8,128)S(1)}, f32[7,32,128]{2,1,0:T(8,128)S(1)}, u32[]{:S(2)}, u32[]{:S(2)}) collective-permute-start(f32[7,32,128]{2,1,0:T(8,128)S(1)} %get-tuple-element.58.refs_0_), channel_id=1, source_target_pairs={{0,192},{64,128},{128,64},{192,0},{1,193},{65,129},{129,65},{193,1... | collective-permute-start | bytes 344072 | tf_op jit(solution)/shard_map/ppermute | solution.py:271
  93.1 8.5 %collective-permute-start.28 = (f32[7,32,128]{2,1,0:T(8,128)S(1)}, f32[7,32,128]{2,1,0:T(8,128)S(1)}, u32[]{:S(2)}, u32[]{:S(2)}) collective-permute-start(f32[7,32,128]{2,1,0:T(8,128)S(1)} %get-tuple-element.58.refs_0_), channel_id=1, source_target_pairs={{0,128},{64,192},{128,0},{192,64},{1,129},{65,193},{129,1},{193,65... | collective-permute-start | bytes 344072 | tf_op jit(solution)/shard_map/ppermute | solution.py:271
  93.2 8.4 %collective-permute-start.27 = (f32[7,32,128]{2,1,0:T(8,128)S(1)}, f32[7,32,128]{2,1,0:T(8,128)S(1)}, u32[]{:S(2)}, u32[]{:S(2)}) collective-permute-start(f32[7,32,128]{2,1,0:T(8,128)S(1)} %get-tuple-element.58.refs_0_), channel_id=1, source_target_pairs={{0,64},{64,0},{128,192},{192,128},{1,65},{65,1},{129,193},{193,129... | collective-permute-start | bytes 344072 | tf_op jit(solution)/shard_map/ppermute | solution.py:271
  95.0 7.5 %collective-permute-start.30 = (f32[7,32,128]{2,1,0:T(8,128)S(1)}, f32[7,32,128]{2,1,0:T(8,128)S(1)}, u32[]{:S(2)}, u32[]{:S(2)}) collective-permute-start(f32[7,32,128]{2,1,0:T(8,128)S(1)} %get-tuple-element.58.refs_0_), channel_id=1, source_target_pairs={{0,4},{4,0},{1,5},{5,1},{2,6},{6,2},{3,7},{7,3},{8,12},{12,8},{9,1... | collective-permute-start | bytes 344072 | tf_op jit(solution)/shard_map/ppermute | solution.py:275
  101.6 1.4 %collective-permute-start.31 = (f32[7,32,128]{2,1,0:T(8,128)S(1)}, f32[7,32,128]{2,1,0:T(8,128)S(1)}, u32[]{:S(2)}, u32[]{:S(2)}) collective-permute-start(f32[7,32,128]{2,1,0:T(8,128)S(1)} %collective-permute-done.27.refs_1_), channel_id=1, source_target_pairs={{0,4},{4,0},{1,5},{5,1},{2,6},{6,2},{3,7},{7,3},{8,12},{12,8},{9,1... | collective-permute-start | bytes 344072 | tf_op jit(solution)/shard_map/ppermute | solution.py:275
  101.9 1.3 %collective-permute-start.32 = (f32[7,32,128]{2,1,0:T(8,128)S(1)}, f32[7,32,128]{2,1,0:T(8,128)S(1)}, u32[]{:S(2)}, u32[]{:S(2)}) collective-permute-start(f32[7,32,128]{2,1,0:T(8,128)S(1)} %collective-permute-done.28.refs_2_), channel_id=1, source_target_pairs={{0,4},{4,0},{1,5},{5,1},{2,6},{6,2},{3,7},{7,3},{8,12},{12,8},{9,1... | collective-permute-start | bytes 344072 | tf_op jit(solution)/shard_map/ppermute | solution.py:275
  102.2 1.3 %collective-permute-start.33 = (f32[7,32,128]{2,1,0:T(8,128)S(1)}, f32[7,32,128]{2,1,0:T(8,128)S(1)}, u32[]{:S(2)}, u32[]{:S(2)}) collective-permute-start(f32[7,32,128]{2,1,0:T(8,128)S(1)} %collective-permute-done.29.refs_3_), channel_id=1, source_target_pairs={{0,4},{4,0},{1,5},{5,1},{2,6},{6,2},{3,7},{7,3},{8,12},{12,8},{9,1... | collective-permute-start | bytes 344072 | tf_op jit(solution)/shard_map/ppermute | solution.py:275

commit v4 on v3

--- a/solution.py
+++ b/solution.py
@@ -10,6 +10,7 @@
 
 X, FAR, NEAR, CORES, Y = 4, 4, 2, 2, 4
 LANES = 128
+SENT, SHARED = (0, 2, 1, 3), (0, 1, 3, 2)
 F32, BF16 = jnp.float32, jnp.bfloat16
 HIGH = lax.Precision.HIGHEST
 VMEM = pl.BlockSpec(memory_space=pltpu.VMEM)
@@ -32,7 +33,7 @@
     return pltpu.CompilerParams(vmem_limit_bytes=mib << 20, **more)
 
 
-def start_kernel(height, x_ref, g_ref, e_ref, q_ref, high_ref, low_ref, p_ref, *refs):
+def start_kernel(height, x_ref, g_ref, e_ref, q_ref, high_ref, p_ref, *refs):
     *piece_refs, g_near, e_near, q_near, sems, q_sem = refs
     replicas, rows, columns = g_ref.shape
     steps = rows // height
@@ -57,14 +58,12 @@
             total = (g_near[0, row, at] + e_near[0, row, at]).astype(F32)
             for replica in range(1, replicas):
                 total = total + (g_near[replica, row, at] + e_near[replica, row, at]).astype(F32)
-            high_ref[row, at], low_ref[row, at] = split(total * (1.0 / replicas), 2)
+            high_ref[row, at] = (total * (1.0 / replicas)).astype(BF16)
         if index >= steps - 2:
             if index == steps - 2:
                 q_copy.wait()
                 row = pl.ds(0, rows - height)
-            both = jnp.concatenate([high_ref[row, :columns], low_ref[row]], axis=0)
-            term = dot(both, q_near[...], ((1,), (1,)))
-            p_ref[row] = term[: row.size] + term[row.size :]
+            p_ref[row] = dot(high_ref[row, :columns], q_near[...], ((1,), (1,)))
     high_ref[:, columns:] = jnp.zeros((rows, high_ref.shape[1] - columns), BF16)
     for flip, piece_ref in enumerate(piece_refs):
         width = piece_ref.shape[1]
@@ -82,10 +81,9 @@
     return pl.pallas_call(
         functools.partial(start_kernel, height),
         in_specs=[SMEM] + [far] * 3,
-        out_specs=[VMEM] * (3 + X),
+        out_specs=[VMEM] * (2 + X),
         out_shape=[
             jax.ShapeDtypeStruct((rows, X * width), BF16),
-            jax.ShapeDtypeStruct((rows, columns), BF16),
             jax.ShapeDtypeStruct((rows, q_turned.shape[0]), F32),
         ]
         + [jax.ShapeDtypeStruct((rows, width), BF16)] * X,
@@ -105,8 +103,8 @@
     return jnp.concatenate([gram[:half], gram[half:]], axis=1)
 
 
-def right_kernel(blocks, core_ref, own, one, two, three, high_ref, low_ref, mine_ref, theirs_ref):
-    p = (own[...] + two[...]) + (one[...] + three[...])
+def right_kernel(blocks, core_ref, own, one, two, three, high_ref, mine_ref, theirs_ref):
+    p = total_of([own, one, two, three])
     rank = p.shape[1]
     half = rank // 2
     first = core_ref[0] == 0
@@ -115,8 +113,7 @@
     for block in range(blocks):
         at = pl.ds(block * LANES, LANES)
         top = dot(stack, high_ref[:, at])
-        low = dot(stack[: 2 * rank], low_ref[:, at])
-        u = top[:rank] + ((top[rank : 2 * rank] + low[:rank]) + (top[2 * rank :] + low[rank:]))
+        u = top[:rank] + (top[rank : 2 * rank] + top[2 * rank :])
         mine_ref[block] = jnp.where(first, u[:half], u[half:])
         theirs_ref[block] = jnp.where(first, u[half:], u[:half]).astype(BF16)
     gram = fold(dot(turned, p, ((1,), (0,)), HIGH))
@@ -125,19 +122,19 @@
         theirs_ref[blocks + index] = part
 
 
-def right(place, parts, high, low):
+def right(place, parts, high, columns):
     rank = parts[0].shape[1]
-    blocks = low.shape[1] // LANES
+    blocks = columns // LANES
     return pl.pallas_call(
         functools.partial(right_kernel, blocks),
-        in_specs=[SMEM] + [VMEM] * 6,
+        in_specs=[SMEM] + [VMEM] * 5,
         out_specs=[VMEM] * 2,
         out_shape=[
             jax.ShapeDtypeStruct((blocks + 1, rank // 2, LANES), F32),
             jax.ShapeDtypeStruct((blocks + 3, rank // 2, LANES), BF16),
         ],
         compiler_params=params(24),
-    )(place["core"], *parts, high, low)
+    )(place["core"], *parts, high)
 
 
 def next_right_kernel(core_ref, x_ref, inverse_ref, *refs):
@@ -178,7 +175,7 @@
 def total_of(refs, *at):
     found = [ref[at] if at else ref[...] for ref in refs]
     if len(found) == 4:
-        found = [found[0] + found[2], found[1] + found[3]]
+        found = [found[0] + found[3], found[1] + found[2]]
     return found[0] + found[1]
 
 
@@ -250,7 +247,7 @@
 def sum_coarse_kernel(*refs):
     found = [unpack(ref) for ref in refs[:-1]]
     if len(found) == 4:
-        found = [[a + b for a, b in zip(found[k], found[k + 2])] for k in range(2)]
+        found = [[a + b for a, b in zip(found[k], found[3 - k])] for k in range(2)]
     pack(refs[-1], *[a + b for a, b in zip(*found)])
 
 
@@ -266,9 +263,13 @@
 
 
 def around(value, axis):
-    if not isinstance(value, (list, tuple)):
-        value = [value] * 4
-    return [value[0]] + [lax.ppermute(value[flip], axis, [(i, i ^ flip) for i in range(4)]) for flip in range(1, 4)]
+    if isinstance(value, (list, tuple)):
+        return [value[0]] + [flipped(value[flip], axis, flip) for flip in SENT[1:]]
+    return [value] + [flipped(value, axis, flip) for flip in SHARED[1:]]
+
+
+def flipped(value, axis, flip):
+    return lax.ppermute(value, axis, [(i, i ^ flip) for i in range(4)])
 
 
 def swap(value, axis):
@@ -299,9 +300,8 @@
 def gather(core_ref, x_ref, refs, u_ref, per):
     first = core_ref[0] == 0
     parts = u_ref.shape[0] // (2 * refs[0].shape[1])
-    for flip in range(X):
+    for flip, a_ref, b_ref in zip(SHARED, refs[:X], refs[X:]):
         owner = x_ref[0] ^ flip
-        a_ref, b_ref = refs[flip], refs[X + flip]
         for index in range(per):
             at = pl.ds(pl.multiple_of((owner * per + index) * LANES, LANES), LANES)
             u = whole(first, a_ref[index].astype(F32), b_ref[index].astype(F32))
@@ -311,7 +311,7 @@
 def left_kernel(core_ref, x_ref, part_ref, other_ref, *refs):
     *piece_refs, mean_ref, out_ref = refs
     height = piece_refs[0].shape[0]
-    for flip, piece_ref in enumerate(piece_refs):
+    for flip, piece_ref in zip(SENT, piece_refs):
         mean_ref[pl.ds(pl.multiple_of((x_ref[0] ^ flip) * height, height), height)] = piece_ref[...]
     per = part_ref.shape[0] - 1
     first = core_ref[0] == 0
@@ -347,7 +347,7 @@
     t_ref[...] = total_of(in_refs, slice(None), slice(0, rows))
     half = gram_ref.shape[0] // 2
     part = half // X
-    for flip, in_ref in enumerate(in_refs):
+    for flip, in_ref in zip(SHARED, in_refs):
         quarter = in_ref[: 2 * part, rows:]
         place = (x_ref[0] ^ flip) * part
         gram_ref[pl.ds(pl.multiple_of(place, part), part)] = quarter[:part]
@@ -470,10 +470,10 @@
 
 def per_device(gradient, error_buffer, q_start):
     place = {axis: lax.axis_index(axis).astype(jnp.int32).reshape(1) for axis in ("x", "near", "core")}
-    high, low, term, *pieces = start(place, gradient, error_buffer, q_start.T)
+    high, term, *pieces = start(place, gradient, error_buffer, q_start.T)
     parts = around(term, "y")
     pieces = around(pieces, "x")
-    part = coarse_sum(place, *right(place, parts, high, low))
+    part = coarse_sum(place, *right(place, parts, high, gradient.shape[2]))
     mean, term = left(place, part, pieces)
     rank, width = term.shape
     term, gram = small(

time: 108 us -> 105 us (0.972)
  waiting for transfers between devices: 36.2 us -> 32.7 us
    ppermute x10, starting transfers between devices: 16.8 us -> 18.8 us  [swap(): return lax.ppermute(value, axis, [(0, 1), (1, 0)])]
    ppermute x24, waiting for transfers between devices: 25.4 us -> 23.6 us  [flipped(): return lax.ppermute(value, axis, [(i, i ^ flip) for i in range(4)])]
    ppermute x10, waiting for transfers between devices: 10.8 us -> 9.08 us  [swap(): return lax.ppermute(value, axis, [(0, 1), (1, 0)])]
    ppermute x24, starting transfers between devices: 35.9 us -> 34.3 us  [flipped(): return lax.ppermute(value, axis, [(i, i ^ flip) for i in range(4)])]
  transfers between devices with their start and end apart: 34 -> 34, of which waited for: 19 -> 21; matrix products, arithmetic and copies ran while one was open for 0% -> 0% of each run, Pallas kernels for 6% -> 7%
where the time goes in v4:
time: 105 us
  starting transfers between devices  53.2 us (51%)
  waiting for transfers between devices  32.7 us (31%)
  Pallas kernels  18 us (17%)
    ppermute x24, starting transfers between devices, flipped(): return lax.ppermute(value, axis, [(i, i ^ flip) for i in range(4)])  34.3 us
    ppermute x24, waiting for transfers between devices, flipped(): return lax.ppermute(value, axis, [(i, i ^ flip) for i in range(4)])  23.6 us
    ppermute x10, starting transfers between devices, swap(): return lax.ppermute(value, axis, [(0, 1), (1, 0)])  18.8 us
    ppermute x10, waiting for transfers between devices, swap(): return lax.ppermute(value, axis, [(0, 1), (1, 0)])  9.08 us
    pallas_call x1, Pallas kernels, end(): pl.pallas_call(end_kernel, grid=(columns // width,), in_specs=[SMEM] * 2...  4.48 us
    pallas_call x1, Pallas kernels, start(): pl.pallas_call(functools.partial(start_kernel, height), in_specs=[SMEM] +...  4.36 us
    pallas_call x1, Pallas kernels, inverse_and_fetch(): pl.pallas_call(fetch_kernel, in_specs=[VMEM, far, far], out_specs=[VMEM]...  3.62 us
    pallas_call x1, Pallas kernels, inverse_of(): pl.pallas_call(inverse_kernel, in_specs=[VMEM], out_specs=VMEM, out_shape...  3.24 us
  transfers between devices with their start and end apart: 34, of which 21 were waited for; matrix products, arithmetic and copies ran while one was open for 0% of the time, Pallas kernels for 7%

profile of v4, /device:TPU:1, one launch (start us, length us, event | category | flops | bytes accessed | tf_op | source)
XLA Modules:
  0.0 104.5 jit_solution(4378782800544530011)
XLA Ops:
  0.6 4.4 %shard_map.50 = (bf16[80,3584]{1,0:T(8,128)(2,1)S(1)}, f32[80,64]{1,0:T(8,128)S(1)}, bf16[80,896]{1,0:T(8,128)(2,1)S(1)}, bf16[80,896]{1,0:T(8,128)(2,1)S(1)}, b...) custom-call(s32[1]{0:T(128)} %bitcast.1.x_ref, bf16[8,80,3456]{2,1,0:T(8,128)(2,1)} %g_ref.3, ...), custom_call_target="tpu_custom_call" | custom-call | tf_op jit(solution)/shard_map/pallas_call | solution.py:81
  5.0 3.8 %collective-permute-start.2 = (f32[80,64]{1,0:T(8,128)S(1)}, f32[80,64]{1,0:T(8,128)S(1)}, u32[]{:S(2)}, u32[]{:S(2)}) collective-permute-start(f32[80,64]{1,0:T(8,128)S(1)} %get-tuple-element.36.own), channel_id=1, source_target_pairs={{0,2},{1,3},{2,0},{3,1},{4,6},{5,7},{6,4},{7,5},{8,10},{9,11},{10,... | collective-permute-start | bytes 61448 | tf_op jit(solution)/shard_map/ppermute | solution.py:272
  8.8 0.8 collective-permute-start.1
  9.6 0.6 collective-permute-done.2.three
  10.2 3.2 %collective-permute-done.1.two = f32[80,64]{1,0:T(8,128)S(1)} collective-permute-done((f32[80,64]{1,0:T(8,128)S(1)}, f32[80,64]{1,0:T(8,128)S(1)}, u32[]{:S(2)}, u32[]{:S(2)}) %collective-permute-start.1) | collective-permute-done | bytes 20512 | tf_op jit(solution)/shard_map/ppermute | solution.py:272
  13.4 0.7 shard_map.51
  14.1 1.7 %collective-permute-start.3 = (bf16[30,32,128]{2,1,0:T(8,128)(2,1)S(1)}, bf16[30,32,128]{2,1,0:T(8,128)(2,1)S(1)}, u32[]{:S(2)}, u32[]{:S(2)}) collective-permute-start(bf16[30,32,128]{2,1,0:T(8,128)(2,1)S(1)} %get-tuple-element.39), channel_id=1, source_target_pairs={{0,4},{4,0},{1,5},{5,1},{2,6},{6,2},{3,7},{7,3},{8,12},{12,8},{9,1... | collective-permute-start | bytes 737288 | tf_op jit(solution)/shard_map/ppermute | solution.py:276
  15.8 1.1 %collective-permute-done.3.b_ref = bf16[30,32,128]{2,1,0:T(8,128)(2,1)S(1)} collective-permute-done((bf16[30,32,128]{2,1,0:T(8,128)(2,1)S(1)}, bf16[30,32,128]{2,1,0:T(8,128)(2,1)S(1)}, u32[]{:S(2)}, u32[]{:S(2)}) %collective-permute-start.3) | collective-permute-done | bytes 245792 | tf_op jit(solution)/shard_map/ppermute | solution.py:276
  16.9 0.1 shard_map.52
  17.0 2.8 %collective-permute-start.4 = (bf16[8,32,128]{2,1,0:T(8,128)(2,1)S(1)}, bf16[8,32,128]{2,1,0:T(8,128)(2,1)S(1)}, u32[]{:S(2)}, u32[]{:S(2)}) collective-permute-start(bf16[8,32,128]{2,1,0:T(8,128)(2,1)S(1)} %get-tuple-element.41), channel_id=1, source_target_pairs={{0,128},{64,192},{128,0},{192,64},{1,129},{65,193},{129,1},{193,65... | collective-permute-start | bytes 196616 | tf_op jit(solution)/shard_map/ppermute | solution.py:272
  19.8 0.3 collective-permute-start.5
  20.1 0.6 collective-permute-start.6
  20.7 1.0 collective-permute-done.4.refs_1_
  21.7 1.6 %collective-permute-done.5.refs_2_ = bf16[8,32,128]{2,1,0:T(8,128)(2,1)S(1)} collective-permute-done((bf16[8,32,128]{2,1,0:T(8,128)(2,1)S(1)}, bf16[8,32,128]{2,1,0:T(8,128)(2,1)S(1)}, u32[]{:S(2)}, u32[]{:S(2)}) %collective-permute-start.5) | collective-permute-done | bytes 65568 | tf_op jit(solution)/shard_map/ppermute | solution.py:272
  23.3 1.1 %collective-permute-done.6.refs_3_ = bf16[8,32,128]{2,1,0:T(8,128)(2,1)S(1)} collective-permute-done((bf16[8,32,128]{2,1,0:T(8,128)(2,1)S(1)}, bf16[8,32,128]{2,1,0:T(8,128)(2,1)S(1)}, u32[]{:S(2)}, u32[]{:S(2)}) %collective-permute-start.6) | collective-permute-done | bytes 65568 | tf_op jit(solution)/shard_map/ppermute | solution.py:272
  24.5 1.7 %collective-permute-start.7 = (bf16[8,32,128]{2,1,0:T(8,128)(2,1)S(1)}, bf16[8,32,128]{2,1,0:T(8,128)(2,1)S(1)}, u32[]{:S(2)}, u32[]{:S(2)}) collective-permute-start(bf16[8,32,128]{2,1,0:T(8,128)(2,1)S(1)} %shard_map.53.refs_0_), channel_id=1, source_target_pairs={{0,8},{8,0},{1,9},{9,1},{2,10},{10,2},{3,11},{11,3},{4,12},{12,4},... | collective-permute-start | bytes 196616 | tf_op jit(solution)/shard_map/ppermute | solution.py:276
  26.2 1.7 %collective-permute-done.7.refs_1_ = bf16[8,32,128]{2,1,0:T(8,128)(2,1)S(1)} collective-permute-done((bf16[8,32,128]{2,1,0:T(8,128)(2,1)S(1)}, bf16[8,32,128]{2,1,0:T(8,128)(2,1)S(1)}, u32[]{:S(2)}, u32[]{:S(2)}) %collective-permute-start.7) | collective-permute-done | bytes 65568 | tf_op jit(solution)/shard_map/ppermute | solution.py:276
  27.9 6.8 %collective-permute-start.10 = (bf16[8,32,128]{2,1,0:T(8,128)(2,1)S(1)}, bf16[8,32,128]{2,1,0:T(8,128)(2,1)S(1)}, u32[]{:S(2)}, u32[]{:S(2)}) collective-permute-start(bf16[8,32,128]{2,1,0:T(8,128)(2,1)S(1)} %shard_map.54.refs_0_), channel_id=1, source_target_pairs={{0,32},{16,48},{32,0},{48,16},{1,33},{17,49},{33,1},{49,17},{2,34}... | collective-permute-start | bytes 196616 | tf_op jit(solution)/shard_map/ppermute | solution.py:272
  34.7 1.6 %collective-permute-start.12 = (bf16[80,896]{1,0:T(8,128)(2,1)S(1)}, bf16[80,896]{1,0:T(8,128)(2,1)S(1)}, u32[]{:S(2)}, u32[]{:S(2)}) collective-permute-start(bf16[80,896]{1,0:T(8,128)(2,1)S(1)} %get-tuple-element.45), channel_id=1, source_target_pairs={{0,128},{64,192},{128,0},{192,64},{1,129},{65,193},{129,1},{193,65... | collective-permute-start | bytes 430088 | tf_op jit(solution)/shard_map/ppermute | solution.py:272
  36.3 0.8 collective-permute-start.13
  37.1 0.9 collective-permute-start.14
  38.0 1.2 %collective-permute-start.8 = (bf16[8,32,128]{2,1,0:T(8,128)(2,1)S(1)}, bf16[8,32,128]{2,1,0:T(8,128)(2,1)S(1)}, u32[]{:S(2)}, u32[]{:S(2)}) collective-permute-start(bf16[8,32,128]{2,1,0:T(8,128)(2,1)S(1)} %shard_map.54.refs_0_), channel_id=1, source_target_pairs={{0,16},{16,0},{32,48},{48,32},{1,17},{17,1},{33,49},{49,33},{2,18}... | collective-permute-start | bytes 196616 | tf_op jit(solution)/shard_map/ppermute | solution.py:272
  39.2 4.1 %collective-permute-done.9.refs_2_ = bf16[8,32,128]{2,1,0:T(8,128)(2,1)S(1)} collective-permute-done((bf16[8,32,128]{2,1,0:T(8,128)(2,1)S(1)}, bf16[8,32,128]{2,1,0:T(8,128)(2,1)S(1)}, u32[]{:S(2)}, u32[]{:S(2)}) %collective-permute-start.9) | collective-permute-done | bytes 65568 | tf_op jit(solution)/shard_map/ppermute | solution.py:272
  43.3 0.4 collective-permute-done.8.refs_1_
  43.7 5.8 %collective-permute-start.11 = (bf16[8,32,128]{2,1,0:T(8,128)(2,1)S(1)}, bf16[8,32,128]{2,1,0:T(8,128)(2,1)S(1)}, u32[]{:S(2)}, u32[]{:S(2)}) collective-permute-start(bf16[8,32,128]{2,1,0:T(8,128)(2,1)S(1)} %shard_map.55.part_ref), channel_id=1, source_target_pairs={{0,4},{4,0},{1,5},{5,1},{2,6},{6,2},{3,7},{7,3},{8,12},{12,8},{9,1... | collective-permute-start | bytes 196616 | tf_op jit(solution)/shard_map/ppermute | solution.py:276
  49.6 0.0 collective-permute-done.13.refs_2_
  49.6 0.0 collective-permute-done.14.refs_3_
  49.6 0.9 collective-permute-done.11.other_ref
  50.5 0.3 shard_map.56
  50.8 0.1 collective-permute-start.17
  51.0 1.8 %collective-permute-start.16 = (f32[64,384]{1,0:T(8,128)S(1)}, f32[64,384]{1,0:T(8,128)S(1)}, u32[]{:S(2)}, u32[]{:S(2)}) collective-permute-start(f32[64,384]{1,0:T(8,128)S(1)} %get-tuple-element.48.refs_0_), channel_id=1, source_target_pairs={{0,192},{64,128},{128,64},{192,0},{1,193},{65,129},{129,65},{193,1... | collective-permute-start | bytes 294920 | tf_op jit(solution)/shard_map/ppermute | solution.py:272
  52.8 0.8 collective-permute-start.15
  53.6 2.9 %collective-permute-done.17.refs_3_ = f32[64,384]{1,0:T(8,128)S(1)} collective-permute-done((f32[64,384]{1,0:T(8,128)S(1)}, f32[64,384]{1,0:T(8,128)S(1)}, u32[]{:S(2)}, u32[]{:S(2)}) %collective-permute-start.17) | collective-permute-done | bytes 98336 | tf_op jit(solution)/shard_map/ppermute | solution.py:272
  56.5 2.4 %collective-permute-done.16.refs_2_ = f32[64,384]{1,0:T(8,128)S(1)} collective-permute-done((f32[64,384]{1,0:T(8,128)S(1)}, f32[64,384]{1,0:T(8,128)S(1)}, u32[]{:S(2)}, u32[]{:S(2)}) %collective-permute-start.16) | collective-permute-done | bytes 98336 | tf_op jit(solution)/shard_map/ppermute | solution.py:272
  58.9 0.1 shard_map.57
  59.0 1.5 %collective-permute-start.20 = (f32[64,320]{1,0:T(8,128)S(1)}, f32[64,320]{1,0:T(8,128)S(1)}, u32[]{:S(2)}, u32[]{:S(2)}) collective-permute-start(f32[64,320]{1,0:T(8,128)S(1)} %get-tuple-element.50.refs_0_), channel_id=1, source_target_pairs={{0,2},{1,3},{2,0},{3,1},{4,6},{5,7},{6,4},{7,5},{8,10},{9,11},{10,... | collective-permute-start | bytes 245768 | tf_op jit(solution)/shard_map/ppermute | solution.py:272
  60.4 0.7 collective-permute-start.19
  61.1 0.7 collective-permute-start.18
  61.8 3.2 %shard_map.58.inverse_ref = f32[64,64]{1,0:T(8,128)S(1)} custom-call(f32[64,64]{1,0:T(8,128)S(1)} %get-tuple-element.49.gram_ref), custom_call_target="tpu_custom_call" | custom-call | flops 10000000 | bytes 5000000 | tf_op jit(solution)/shard_map/pallas_call | solution.py:388
  65.1 2.2 %collective-permute-done.19.refs_2_ = f32[64,320]{1,0:T(8,128)S(1)} collective-permute-done((f32[64,320]{1,0:T(8,128)S(1)}, f32[64,320]{1,0:T(8,128)S(1)}, u32[]{:S(2)}, u32[]{:S(2)}) %collective-permute-start.19) | collective-permute-done | bytes 81952 | tf_op jit(solution)/shard_map/ppermute | solution.py:272
  67.3 0.9 shard_map.59
  68.2 0.8 collective-permute-start.21
  69.0 1.0 collective-permute-done.21.refs_1_
  70.0 1.4 %collective-permute-start.22 = (f32[8,16,128]{2,1,0:T(8,128)S(1)}, f32[8,16,128]{2,1,0:T(8,128)S(1)}, u32[]{:S(2)}, u32[]{:S(2)}) collective-permute-start(f32[8,16,128]{2,1,0:T(8,128)S(1)} %get-tuple-element.55), channel_id=1, source_target_pairs={{0,8},{8,0},{1,9},{9,1},{2,10},{10,2},{3,11},{11,3},{4,12},{12,4},... | collective-permute-start | bytes 196616 | tf_op jit(solution)/shard_map/ppermute | solution.py:276
  71.4 1.8 %collective-permute-done.22.refs_1_ = f32[8,16,128]{2,1,0:T(8,128)S(1)} collective-permute-done((f32[8,16,128]{2,1,0:T(8,128)S(1)}, f32[8,16,128]{2,1,0:T(8,128)S(1)}, u32[]{:S(2)}, u32[]{:S(2)}) %collective-permute-start.22) | collective-permute-done | bytes 65568 | tf_op jit(solution)/shard_map/ppermute | solution.py:276
  73.2 3.7 %collective-permute-start.25 = (f32[8,16,128]{2,1,0:T(8,128)S(1)}, f32[8,16,128]{2,1,0:T(8,128)S(1)}, u32[]{:S(2)}, u32[]{:S(2)}) collective-permute-start(f32[8,16,128]{2,1,0:T(8,128)S(1)} %shard_map.61.refs_0_), channel_id=1, source_target_pairs={{0,32},{16,48},{32,0},{48,16},{1,33},{17,49},{33,1},{49,17},{2,34}... | collective-permute-start | bytes 196616 | tf_op jit(solution)/shard_map/ppermute | solution.py:272
  76.9 0.5 collective-permute-start.24
  77.4 1.5 %collective-permute-start.23 = (f32[8,16,128]{2,1,0:T(8,128)S(1)}, f32[8,16,128]{2,1,0:T(8,128)S(1)}, u32[]{:S(2)}, u32[]{:S(2)}) collective-permute-start(f32[8,16,128]{2,1,0:T(8,128)S(1)} %shard_map.61.refs_0_), channel_id=1, source_target_pairs={{0,16},{16,0},{32,48},{48,32},{1,17},{17,1},{33,49},{49,33},{2,18}... | collective-permute-start | bytes 196616 | tf_op jit(solution)/shard_map/ppermute | solution.py:272
  78.9 1.4 %collective-permute-done.25.refs_3_ = f32[8,16,128]{2,1,0:T(8,128)S(1)} collective-permute-done((f32[8,16,128]{2,1,0:T(8,128)S(1)}, f32[8,16,128]{2,1,0:T(8,128)S(1)}, u32[]{:S(2)}, u32[]{:S(2)}) %collective-permute-start.25) | collective-permute-done | bytes 65568 | tf_op jit(solution)/shard_map/ppermute | solution.py:272
  80.3 2.6 %collective-permute-done.24.refs_2_ = f32[8,16,128]{2,1,0:T(8,128)S(1)} collective-permute-done((f32[8,16,128]{2,1,0:T(8,128)S(1)}, f32[8,16,128]{2,1,0:T(8,128)S(1)}, u32[]{:S(2)}, u32[]{:S(2)}) %collective-permute-start.24) | collective-permute-done | bytes 65568 | tf_op jit(solution)/shard_map/ppermute | solution.py:272
  82.9 1.8 %collective-permute-start.26 = (f32[8,16,128]{2,1,0:T(8,128)S(1)}, f32[8,16,128]{2,1,0:T(8,128)S(1)}, u32[]{:S(2)}, u32[]{:S(2)}) collective-permute-start(f32[8,16,128]{2,1,0:T(8,128)S(1)} %shard_map.62.here_ref), channel_id=1, source_target_pairs={{0,8},{8,0},{1,9},{9,1},{2,10},{10,2},{3,11},{11,3},{4,12},{12,4},... | collective-permute-start | bytes 196616 | tf_op jit(solution)/shard_map/ppermute | solution.py:276
  84.7 1.7 %collective-permute-done.26.there_ref = f32[8,16,128]{2,1,0:T(8,128)S(1)} collective-permute-done((f32[8,16,128]{2,1,0:T(8,128)S(1)}, f32[8,16,128]{2,1,0:T(8,128)S(1)}, u32[]{:S(2)}, u32[]{:S(2)}) %collective-permute-start.26) | collective-permute-done | bytes 65568 | tf_op jit(solution)/shard_map/ppermute | solution.py:276
  86.4 0.1 shard_map.63
  86.5 3.2 %collective-permute-start.29 = (f32[7,32,128]{2,1,0:T(8,128)S(1)}, f32[7,32,128]{2,1,0:T(8,128)S(1)}, u32[]{:S(2)}, u32[]{:S(2)}) collective-permute-start(f32[7,32,128]{2,1,0:T(8,128)S(1)} %get-tuple-element.56.refs_0_), channel_id=1, source_target_pairs={{0,128},{64,192},{128,0},{192,64},{1,129},{65,193},{129,1},{193,65... | collective-permute-start | bytes 344072 | tf_op jit(solution)/shard_map/ppermute | solution.py:272
  89.7 0.2 collective-permute-start.28
  89.9 4.3 %collective-permute-start.30 = (f32[7,32,128]{2,1,0:T(8,128)S(1)}, f32[7,32,128]{2,1,0:T(8,128)S(1)}, u32[]{:S(2)}, u32[]{:S(2)}) collective-permute-start(f32[7,32,128]{2,1,0:T(8,128)S(1)} %get-tuple-element.56.refs_0_), channel_id=1, source_target_pairs={{0,4},{4,0},{1,5},{5,1},{2,6},{6,2},{3,7},{7,3},{8,12},{12,8},{9,1... | collective-permute-start | bytes 344072 | tf_op jit(solution)/shard_map/ppermute | solution.py:276
  94.2 3.6 %shard_map.64 = (f32[64,64]{1,0:T(8,128)S(1)}, bf16[8,80,3456]{2,1,0:T(8,128)(2,1)S(1)}, bf16[8,80,3456]{2,1,0:T(8,128)(2,1)S(1)}) custom-call(f32[64,64]{1,0:T(8,128)S(1)} %get-tuple-element.57.gram_ref, bf16[8,80,3456]{2,1,0:T(8,128)(2,1)} %g_ref.3, bf16[8,80,3456]{2,1,0:T(8,128)(2,1)} %e_ref.3), custom_call_target="tpu_custom_call" | custom-call | flops 10000000 | bytes 5000000 | tf_op jit(solution)/shard_map/pallas_call | solution.py:412
  97.9 0.7 collective-permute-start.31
  98.6 0.0 collective-permute-start.32
  98.6 0.5 collective-permute-start.33
  99.1 0.5 collective-permute-done.31.refs_5_
  99.5 0.4 collective-permute-done.32.refs_6_
  99.9 0.2 collective-permute-done.33.refs_7_
  100.1 4.5 %shard_map.65 = (bf16[8,80,3456]{2,1,0:T(8,128)(2,1)}, f32[64,3456]{1,0:T(8,128)}) custom-call(s32[1]{0:T(128)} %bitcast.core_ref, s32[1]{0:T(128)} %bitcast.1.x_ref, f32[7,32,128]{2,1,0:T(8,128)S(1)} %get-tuple-element.56.refs_0_, f32[7,32,128]{2,1,0:T(8,128)S(1)} %collective-permute-done.27.refs_1_, f32[7,32,128]{2,1,0:T(8,128)S(1)} %collective-permute-done.28.refs_2_, ...), custom_call_target="tpu_custom_call" | custom-call | tf_op jit(solution)/shard_map/pallas_call | solution.py:457
  (20 shorter events, 0.2 us)
Async XLA Ops:
  5.0 5.2 %collective-permute-start.2 = (f32[80,64]{1,0:T(8,128)S(1)}, f32[80,64]{1,0:T(8,128)S(1)}, u32[]{:S(2)}, u32[]{:S(2)}) collective-permute-start(f32[80,64]{1,0:T(8,128)S(1)} %get-tuple-element.36.own), channel_id=1, source_target_pairs={{0,2},{1,3},{2,0},{3,1},{4,6},{5,7},{6,4},{7,5},{8,10},{9,11},{10,... | collective-permute-start | bytes 61448 | tf_op jit(solution)/shard_map/ppermute | solution.py:272
  8.8 4.6 %collective-permute-start.1 = (f32[80,64]{1,0:T(8,128)S(1)}, f32[80,64]{1,0:T(8,128)S(1)}, u32[]{:S(2)}, u32[]{:S(2)}) collective-permute-start(f32[80,64]{1,0:T(8,128)S(1)} %get-tuple-element.36.own), channel_id=1, source_target_pairs={{0,3},{1,2},{2,1},{3,0},{4,7},{5,6},{6,5},{7,4},{8,11},{9,10},{10,... | collective-permute-start | bytes 61448 | tf_op jit(solution)/shard_map/ppermute | solution.py:272
  9.6 3.8 %collective-permute-start = (f32[80,64]{1,0:T(8,128)S(1)}, f32[80,64]{1,0:T(8,128)S(1)}, u32[]{:S(2)}, u32[]{:S(2)}) collective-permute-start(f32[80,64]{1,0:T(8,128)S(1)} %get-tuple-element.36.own), channel_id=1, source_target_pairs={{0,1},{1,0},{2,3},{3,2},{4,5},{5,4},{6,7},{7,6},{8,9},{9,8},{10,11... | collective-permute-start | bytes 61448 | tf_op jit(solution)/shard_map/ppermute | solution.py:272
  14.1 2.8 %collective-permute-start.3 = (bf16[30,32,128]{2,1,0:T(8,128)(2,1)S(1)}, bf16[30,32,128]{2,1,0:T(8,128)(2,1)S(1)}, u32[]{:S(2)}, u32[]{:S(2)}) collective-permute-start(bf16[30,32,128]{2,1,0:T(8,128)(2,1)S(1)} %get-tuple-element.39), channel_id=1, source_target_pairs={{0,4},{4,0},{1,5},{5,1},{2,6},{6,2},{3,7},{7,3},{8,12},{12,8},{9,1... | collective-permute-start | bytes 737288 | tf_op jit(solution)/shard_map/ppermute | solution.py:276
  17.0 4.7 %collective-permute-start.4 = (bf16[8,32,128]{2,1,0:T(8,128)(2,1)S(1)}, bf16[8,32,128]{2,1,0:T(8,128)(2,1)S(1)}, u32[]{:S(2)}, u32[]{:S(2)}) collective-permute-start(bf16[8,32,128]{2,1,0:T(8,128)(2,1)S(1)} %get-tuple-element.41), channel_id=1, source_target_pairs={{0,128},{64,192},{128,0},{192,64},{1,129},{65,193},{129,1},{193,65... | collective-permute-start | bytes 196616 | tf_op jit(solution)/shard_map/ppermute | solution.py:272
  19.8 3.5 %collective-permute-start.5 = (bf16[8,32,128]{2,1,0:T(8,128)(2,1)S(1)}, bf16[8,32,128]{2,1,0:T(8,128)(2,1)S(1)}, u32[]{:S(2)}, u32[]{:S(2)}) collective-permute-start(bf16[8,32,128]{2,1,0:T(8,128)(2,1)S(1)} %get-tuple-element.42), channel_id=1, source_target_pairs={{0,64},{64,0},{128,192},{192,128},{1,65},{65,1},{129,193},{193,129... | collective-permute-start | bytes 196616 | tf_op jit(solution)/shard_map/ppermute | solution.py:272
  20.1 4.3 %collective-permute-start.6 = (bf16[8,32,128]{2,1,0:T(8,128)(2,1)S(1)}, bf16[8,32,128]{2,1,0:T(8,128)(2,1)S(1)}, u32[]{:S(2)}, u32[]{:S(2)}) collective-permute-start(bf16[8,32,128]{2,1,0:T(8,128)(2,1)S(1)} %get-tuple-element.43), channel_id=1, source_target_pairs={{0,192},{64,128},{128,64},{192,0},{1,193},{65,129},{129,65},{193,1... | collective-permute-start | bytes 196616 | tf_op jit(solution)/shard_map/ppermute | solution.py:272
  24.5 3.4 %collective-permute-start.7 = (bf16[8,32,128]{2,1,0:T(8,128)(2,1)S(1)}, bf16[8,32,128]{2,1,0:T(8,128)(2,1)S(1)}, u32[]{:S(2)}, u32[]{:S(2)}) collective-permute-start(bf16[8,32,128]{2,1,0:T(8,128)(2,1)S(1)} %shard_map.53.refs_0_), channel_id=1, source_target_pairs={{0,8},{8,0},{1,9},{9,1},{2,10},{10,2},{3,11},{11,3},{4,12},{12,4},... | collective-permute-start | bytes 196616 | tf_op jit(solution)/shard_map/ppermute | solution.py:276
  27.9 10.1 %collective-permute-start.10 = (bf16[8,32,128]{2,1,0:T(8,128)(2,1)S(1)}, bf16[8,32,128]{2,1,0:T(8,128)(2,1)S(1)}, u32[]{:S(2)}, u32[]{:S(2)}) collective-permute-start(bf16[8,32,128]{2,1,0:T(8,128)(2,1)S(1)} %shard_map.54.refs_0_), channel_id=1, source_target_pairs={{0,32},{16,48},{32,0},{48,16},{1,33},{17,49},{33,1},{49,17},{2,34}... | collective-permute-start | bytes 196616 | tf_op jit(solution)/shard_map/ppermute | solution.py:272
  34.7 14.9 %collective-permute-start.12 = (bf16[80,896]{1,0:T(8,128)(2,1)S(1)}, bf16[80,896]{1,0:T(8,128)(2,1)S(1)}, u32[]{:S(2)}, u32[]{:S(2)}) collective-permute-start(bf16[80,896]{1,0:T(8,128)(2,1)S(1)} %get-tuple-element.45), channel_id=1, source_target_pairs={{0,128},{64,192},{128,0},{192,64},{1,129},{65,193},{129,1},{193,65... | collective-permute-start | bytes 430088 | tf_op jit(solution)/shard_map/ppermute | solution.py:272
  36.3 13.3 %collective-permute-start.13 = (bf16[80,896]{1,0:T(8,128)(2,1)S(1)}, bf16[80,896]{1,0:T(8,128)(2,1)S(1)}, u32[]{:S(2)}, u32[]{:S(2)}) collective-permute-start(bf16[80,896]{1,0:T(8,128)(2,1)S(1)} %get-tuple-element.46), channel_id=1, source_target_pairs={{0,64},{64,0},{128,192},{192,128},{1,65},{65,1},{129,193},{193,129... | collective-permute-start | bytes 430088 | tf_op jit(solution)/shard_map/ppermute | solution.py:272
  37.1 12.5 %collective-permute-start.14 = (bf16[80,896]{1,0:T(8,128)(2,1)S(1)}, bf16[80,896]{1,0:T(8,128)(2,1)S(1)}, u32[]{:S(2)}, u32[]{:S(2)}) collective-permute-start(bf16[80,896]{1,0:T(8,128)(2,1)S(1)} %get-tuple-element.47), channel_id=1, source_target_pairs={{0,192},{64,128},{128,64},{192,0},{1,193},{65,129},{129,65},{193,1... | collective-permute-start | bytes 430088 | tf_op jit(solution)/shard_map/ppermute | solution.py:272
  38.0 5.3 %collective-permute-start.9 = (bf16[8,32,128]{2,1,0:T(8,128)(2,1)S(1)}, bf16[8,32,128]{2,1,0:T(8,128)(2,1)S(1)}, u32[]{:S(2)}, u32[]{:S(2)}) collective-permute-start(bf16[8,32,128]{2,1,0:T(8,128)(2,1)S(1)} %shard_map.54.refs_0_), channel_id=1, source_target_pairs={{0,48},{16,32},{32,16},{48,0},{1,49},{17,33},{33,17},{49,1},{2,50}... | collective-permute-start | bytes 196616 | tf_op jit(solution)/shard_map/ppermute | solution.py:272
  38.0 5.7 %collective-permute-start.8 = (bf16[8,32,128]{2,1,0:T(8,128)(2,1)S(1)}, bf16[8,32,128]{2,1,0:T(8,128)(2,1)S(1)}, u32[]{:S(2)}, u32[]{:S(2)}) collective-permute-start(bf16[8,32,128]{2,1,0:T(8,128)(2,1)S(1)} %shard_map.54.refs_0_), channel_id=1, source_target_pairs={{0,16},{16,0},{32,48},{48,32},{1,17},{17,1},{33,49},{49,33},{2,18}... | collective-permute-start | bytes 196616 | tf_op jit(solution)/shard_map/ppermute | solution.py:272
  43.7 6.8 %collective-permute-start.11 = (bf16[8,32,128]{2,1,0:T(8,128)(2,1)S(1)}, bf16[8,32,128]{2,1,0:T(8,128)(2,1)S(1)}, u32[]{:S(2)}, u32[]{:S(2)}) collective-permute-start(bf16[8,32,128]{2,1,0:T(8,128)(2,1)S(1)} %shard_map.55.part_ref), channel_id=1, source_target_pairs={{0,4},{4,0},{1,5},{5,1},{2,6},{6,2},{3,7},{7,3},{8,12},{12,8},{9,1... | collective-permute-start | bytes 196616 | tf_op jit(solution)/shard_map/ppermute | solution.py:276
  50.8 5.7 %collective-permute-start.17 = (f32[64,384]{1,0:T(8,128)S(1)}, f32[64,384]{1,0:T(8,128)S(1)}, u32[]{:S(2)}, u32[]{:S(2)}) collective-permute-start(f32[64,384]{1,0:T(8,128)S(1)} %get-tuple-element.48.refs_0_), channel_id=1, source_target_pairs={{0,128},{64,192},{128,0},{192,64},{1,129},{65,193},{129,1},{193,65... | collective-permute-start | bytes 294920 | tf_op jit(solution)/shard_map/ppermute | solution.py:272
  51.0 7.9 %collective-permute-start.16 = (f32[64,384]{1,0:T(8,128)S(1)}, f32[64,384]{1,0:T(8,128)S(1)}, u32[]{:S(2)}, u32[]{:S(2)}) collective-permute-start(f32[64,384]{1,0:T(8,128)S(1)} %get-tuple-element.48.refs_0_), channel_id=1, source_target_pairs={{0,192},{64,128},{128,64},{192,0},{1,193},{65,129},{129,65},{193,1... | collective-permute-start | bytes 294920 | tf_op jit(solution)/shard_map/ppermute | solution.py:272
  52.8 6.1 %collective-permute-start.15 = (f32[64,384]{1,0:T(8,128)S(1)}, f32[64,384]{1,0:T(8,128)S(1)}, u32[]{:S(2)}, u32[]{:S(2)}) collective-permute-start(f32[64,384]{1,0:T(8,128)S(1)} %get-tuple-element.48.refs_0_), channel_id=1, source_target_pairs={{0,64},{64,0},{128,192},{192,128},{1,65},{65,1},{129,193},{193,129... | collective-permute-start | bytes 294920 | tf_op jit(solution)/shard_map/ppermute | solution.py:272
  59.0 6.1 %collective-permute-start.20 = (f32[64,320]{1,0:T(8,128)S(1)}, f32[64,320]{1,0:T(8,128)S(1)}, u32[]{:S(2)}, u32[]{:S(2)}) collective-permute-start(f32[64,320]{1,0:T(8,128)S(1)} %get-tuple-element.50.refs_0_), channel_id=1, source_target_pairs={{0,2},{1,3},{2,0},{3,1},{4,6},{5,7},{6,4},{7,5},{8,10},{9,11},{10,... | collective-permute-start | bytes 245768 | tf_op jit(solution)/shard_map/ppermute | solution.py:272
  60.4 6.9 %collective-permute-start.19 = (f32[64,320]{1,0:T(8,128)S(1)}, f32[64,320]{1,0:T(8,128)S(1)}, u32[]{:S(2)}, u32[]{:S(2)}) collective-permute-start(f32[64,320]{1,0:T(8,128)S(1)} %get-tuple-element.50.refs_0_), channel_id=1, source_target_pairs={{0,3},{1,2},{2,1},{3,0},{4,7},{5,6},{6,5},{7,4},{8,11},{9,10},{10,... | collective-permute-start | bytes 245768 | tf_op jit(solution)/shard_map/ppermute | solution.py:272
  61.1 6.2 %collective-permute-start.18 = (f32[64,320]{1,0:T(8,128)S(1)}, f32[64,320]{1,0:T(8,128)S(1)}, u32[]{:S(2)}, u32[]{:S(2)}) collective-permute-start(f32[64,320]{1,0:T(8,128)S(1)} %get-tuple-element.50.refs_0_), channel_id=1, source_target_pairs={{0,1},{1,0},{2,3},{3,2},{4,5},{5,4},{6,7},{7,6},{8,9},{9,8},{10,11... | collective-permute-start | bytes 245768 | tf_op jit(solution)/shard_map/ppermute | solution.py:272
  68.2 1.8 %collective-permute-start.21 = (f32[8,32,128]{2,1,0:T(8,128)S(1)}, f32[8,32,128]{2,1,0:T(8,128)S(1)}, u32[]{:S(2)}, u32[]{:S(2)}) collective-permute-start(f32[8,32,128]{2,1,0:T(8,128)S(1)} %get-tuple-element.53), channel_id=1, source_target_pairs={{0,4},{4,0},{1,5},{5,1},{2,6},{6,2},{3,7},{7,3},{8,12},{12,8},{9,1... | collective-permute-start | bytes 393224 | tf_op jit(solution)/shard_map/ppermute | solution.py:276
  70.0 3.2 %collective-permute-start.22 = (f32[8,16,128]{2,1,0:T(8,128)S(1)}, f32[8,16,128]{2,1,0:T(8,128)S(1)}, u32[]{:S(2)}, u32[]{:S(2)}) collective-permute-start(f32[8,16,128]{2,1,0:T(8,128)S(1)} %get-tuple-element.55), channel_id=1, source_target_pairs={{0,8},{8,0},{1,9},{9,1},{2,10},{10,2},{3,11},{11,3},{4,12},{12,4},... | collective-permute-start | bytes 196616 | tf_op jit(solution)/shard_map/ppermute | solution.py:276
  73.2 7.1 %collective-permute-start.25 = (f32[8,16,128]{2,1,0:T(8,128)S(1)}, f32[8,16,128]{2,1,0:T(8,128)S(1)}, u32[]{:S(2)}, u32[]{:S(2)}) collective-permute-start(f32[8,16,128]{2,1,0:T(8,128)S(1)} %shard_map.61.refs_0_), channel_id=1, source_target_pairs={{0,32},{16,48},{32,0},{48,16},{1,33},{17,49},{33,1},{49,17},{2,34}... | collective-permute-start | bytes 196616 | tf_op jit(solution)/shard_map/ppermute | solution.py:272
  76.9 6.0 %collective-permute-start.24 = (f32[8,16,128]{2,1,0:T(8,128)S(1)}, f32[8,16,128]{2,1,0:T(8,128)S(1)}, u32[]{:S(2)}, u32[]{:S(2)}) collective-permute-start(f32[8,16,128]{2,1,0:T(8,128)S(1)} %shard_map.61.refs_0_), channel_id=1, source_target_pairs={{0,48},{16,32},{32,16},{48,0},{1,49},{17,33},{33,17},{49,1},{2,50}... | collective-permute-start | bytes 196616 | tf_op jit(solution)/shard_map/ppermute | solution.py:272
  77.4 5.5 %collective-permute-start.23 = (f32[8,16,128]{2,1,0:T(8,128)S(1)}, f32[8,16,128]{2,1,0:T(8,128)S(1)}, u32[]{:S(2)}, u32[]{:S(2)}) collective-permute-start(f32[8,16,128]{2,1,0:T(8,128)S(1)} %shard_map.61.refs_0_), channel_id=1, source_target_pairs={{0,16},{16,0},{32,48},{48,32},{1,17},{17,1},{33,49},{49,33},{2,18}... | collective-permute-start | bytes 196616 | tf_op jit(solution)/shard_map/ppermute | solution.py:272
  82.9 3.5 %collective-permute-start.26 = (f32[8,16,128]{2,1,0:T(8,128)S(1)}, f32[8,16,128]{2,1,0:T(8,128)S(1)}, u32[]{:S(2)}, u32[]{:S(2)}) collective-permute-start(f32[8,16,128]{2,1,0:T(8,128)S(1)} %shard_map.62.here_ref), channel_id=1, source_target_pairs={{0,8},{8,0},{1,9},{9,1},{2,10},{10,2},{3,11},{11,3},{4,12},{12,4},... | collective-permute-start | bytes 196616 | tf_op jit(solution)/shard_map/ppermute | solution.py:276
  86.5 11.4 %collective-permute-start.29 = (f32[7,32,128]{2,1,0:T(8,128)S(1)}, f32[7,32,128]{2,1,0:T(8,128)S(1)}, u32[]{:S(2)}, u32[]{:S(2)}) collective-permute-start(f32[7,32,128]{2,1,0:T(8,128)S(1)} %get-tuple-element.56.refs_0_), channel_id=1, source_target_pairs={{0,128},{64,192},{128,0},{192,64},{1,129},{65,193},{129,1},{193,65... | collective-permute-start | bytes 344072 | tf_op jit(solution)/shard_map/ppermute | solution.py:272
  89.7 8.1 %collective-permute-start.28 = (f32[7,32,128]{2,1,0:T(8,128)S(1)}, f32[7,32,128]{2,1,0:T(8,128)S(1)}, u32[]{:S(2)}, u32[]{:S(2)}) collective-permute-start(f32[7,32,128]{2,1,0:T(8,128)S(1)} %get-tuple-element.56.refs_0_), channel_id=1, source_target_pairs={{0,192},{64,128},{128,64},{192,0},{1,193},{65,129},{129,65},{193,1... | collective-permute-start | bytes 344072 | tf_op jit(solution)/shard_map/ppermute | solution.py:272
  89.9 8.0 %collective-permute-start.27 = (f32[7,32,128]{2,1,0:T(8,128)S(1)}, f32[7,32,128]{2,1,0:T(8,128)S(1)}, u32[]{:S(2)}, u32[]{:S(2)}) collective-permute-start(f32[7,32,128]{2,1,0:T(8,128)S(1)} %get-tuple-element.56.refs_0_), channel_id=1, source_target_pairs={{0,64},{64,0},{128,192},{192,128},{1,65},{65,1},{129,193},{193,129... | collective-permute-start | bytes 344072 | tf_op jit(solution)/shard_map/ppermute | solution.py:272
  89.9 9.2 %collective-permute-start.30 = (f32[7,32,128]{2,1,0:T(8,128)S(1)}, f32[7,32,128]{2,1,0:T(8,128)S(1)}, u32[]{:S(2)}, u32[]{:S(2)}) collective-permute-start(f32[7,32,128]{2,1,0:T(8,128)S(1)} %get-tuple-element.56.refs_0_), channel_id=1, source_target_pairs={{0,4},{4,0},{1,5},{5,1},{2,6},{6,2},{3,7},{7,3},{8,12},{12,8},{9,1... | collective-permute-start | bytes 344072 | tf_op jit(solution)/shard_map/ppermute | solution.py:276
  97.9 1.7 %collective-permute-start.31 = (f32[7,32,128]{2,1,0:T(8,128)S(1)}, f32[7,32,128]{2,1,0:T(8,128)S(1)}, u32[]{:S(2)}, u32[]{:S(2)}) collective-permute-start(f32[7,32,128]{2,1,0:T(8,128)S(1)} %collective-permute-done.27.refs_1_), channel_id=1, source_target_pairs={{0,4},{4,0},{1,5},{5,1},{2,6},{6,2},{3,7},{7,3},{8,12},{12,8},{9,1... | collective-permute-start | bytes 344072 | tf_op jit(solution)/shard_map/ppermute | solution.py:276
  98.6 1.3 %collective-permute-start.32 = (f32[7,32,128]{2,1,0:T(8,128)S(1)}, f32[7,32,128]{2,1,0:T(8,128)S(1)}, u32[]{:S(2)}, u32[]{:S(2)}) collective-permute-start(f32[7,32,128]{2,1,0:T(8,128)S(1)} %collective-permute-done.28.refs_2_), channel_id=1, source_target_pairs={{0,4},{4,0},{1,5},{5,1},{2,6},{6,2},{3,7},{7,3},{8,12},{12,8},{9,1... | collective-permute-start | bytes 344072 | tf_op jit(solution)/shard_map/ppermute | solution.py:276
  98.6 1.5 %collective-permute-start.33 = (f32[7,32,128]{2,1,0:T(8,128)S(1)}, f32[7,32,128]{2,1,0:T(8,128)S(1)}, u32[]{:S(2)}, u32[]{:S(2)}) collective-permute-start(f32[7,32,128]{2,1,0:T(8,128)S(1)} %collective-permute-done.29.refs_3_), channel_id=1, source_target_pairs={{0,4},{4,0},{1,5},{5,1},{2,6},{6,2},{3,7},{7,3},{8,12},{12,8},{9,1... | collective-permute-start | bytes 344072 | tf_op jit(solution)/shard_map/ppermute | solution.py:276

commit v5 on v4

--- a/solution.py
+++ b/solution.py
@@ -27,6 +27,16 @@
 
 def dot(a, b, contract=((1,), (0,)), precision=None):
     return lax.dot_general(a, b, (contract, ((), ())), precision=precision, preferred_element_type=F32)
+
+
+def fold(value):
+    half = value.shape[0] // 2
+    return jnp.concatenate([value[:half], value[half:]], axis=1)
+
+
+def unfold(value):
+    half = value.shape[1] // 2
+    return jnp.concatenate([value[:, :half], value[:, half:]], axis=0)
 
 
 def params(mib, **more):
@@ -49,6 +59,7 @@
         if index == 0:
             q_copy = pltpu.make_async_copy(q_ref, q_near, q_sem)
             q_copy.start()
+    terms = []
     for index, pair in enumerate(copies):
         for copy in pair:
             copy.wait()
@@ -63,7 +74,8 @@
             if index == steps - 2:
                 q_copy.wait()
                 row = pl.ds(0, rows - height)
-            p_ref[row] = dot(high_ref[row, :columns], q_near[...], ((1,), (1,)))
+            terms.append(dot(high_ref[row, :columns], q_near[...], ((1,), (1,))))
+    p_ref[...] = fold(jnp.concatenate(terms, axis=0))
     high_ref[:, columns:] = jnp.zeros((rows, high_ref.shape[1] - columns), BF16)
     for flip, piece_ref in enumerate(piece_refs):
         width = piece_ref.shape[1]
@@ -84,7 +96,7 @@
         out_specs=[VMEM] * (2 + X),
         out_shape=[
             jax.ShapeDtypeStruct((rows, X * width), BF16),
-            jax.ShapeDtypeStruct((rows, q_turned.shape[0]), F32),
+            jax.ShapeDtypeStruct((rows // 2, 2 * q_turned.shape[0]), F32),
         ]
         + [jax.ShapeDtypeStruct((rows, width), BF16)] * X,
         scratch_shapes=[
@@ -98,13 +110,8 @@
     )(place["x"], *in_hbm(gradient, error, q_turned))
 
 
-def fold(gram):
-    half = gram.shape[0] // 2
-    return jnp.concatenate([gram[:half], gram[half:]], axis=1)
-
-
 def right_kernel(blocks, core_ref, own, one, two, three, high_ref, mine_ref, theirs_ref):
-    p = total_of([own, one, two, three])
+    p = unfold(total_of([own, one, two, three]))
     rank = p.shape[1]
     half = rank // 2
     first = core_ref[0] == 0
@@ -123,7 +130,7 @@
 
 
 def right(place, parts, high, columns):
-    rank = parts[0].shape[1]
+    rank = parts[0].shape[1] // 2
     blocks = columns // LANES
     return pl.pallas_call(
         functools.partial(right_kernel, blocks),
@@ -140,7 +147,11 @@
 def next_right_kernel(core_ref, x_ref, inverse_ref, *refs):
     *in_refs, mean_ref, mine_ref, theirs_ref, p_ref, all_ref = refs
     first = core_ref[0] == 0
-    turned = dot(inverse_ref[...], total_of(in_refs), ((1,), (0,)), HIGH)
+    rank = inverse_ref.shape[0]
+    t = total_of(in_refs)
+    whole_blocks = t.shape[0] // rank
+    t = [t[block * rank : (block + 1) * rank] for block in range(whole_blocks)] + [unfold(t[whole_blocks * rank :])]
+    turned = dot(inverse_ref[...], jnp.concatenate(t, axis=1), ((1,), (0,)), HIGH)
     rank = turned.shape[0]
     half = rank // 2
     blocks = mine_ref.shape[0] - 1
@@ -343,9 +354,14 @@
 
 def left_sum_kernel(x_ref, *refs):
     *in_refs, t_ref, gram_ref = refs
-    rows = t_ref.shape[1]
-    t_ref[...] = total_of(in_refs, slice(None), slice(0, rows))
-    half = gram_ref.shape[0] // 2
+    rank = gram_ref.shape[0]
+    half = rank // 2
+    rows = in_refs[0].shape[1] - rank
+    t = total_of(in_refs, slice(None), slice(0, rows))
+    whole_blocks = rows // LANES
+    for block in range(whole_blocks):
+        t_ref[block * rank : (block + 1) * rank] = t[:, block * LANES : (block + 1) * LANES]
+    t_ref[whole_blocks * rank :] = fold(t[:, whole_blocks * LANES :])
     part = half // X
     for flip, in_ref in zip(SHARED, in_refs):
         quarter = in_ref[: 2 * part, rows:]
@@ -477,7 +493,7 @@
     mean, term = left(place, part, pieces)
     rank, width = term.shape
     term, gram = small(
-        left_sum_kernel, (place["x"], *around(term, "x")), [(rank, width - rank), (rank, rank)], 1
+        left_sum_kernel, (place["x"], *around(term, "x")), [(rank * (width - rank) // LANES, LANES), (rank, rank)], 1
     )
     mine, theirs, p = next_right(place, inverse_of(gram), around(term, "y"), mean)
     here, there, ready = all_sum(place, mine, theirs, gradient, error_buffer)

time: 105 us -> 104 us (level)
  waiting for transfers between devices: 32.7 us -> 31.3 us
    ppermute x24, waiting for transfers between devices: 23.6 us -> 22.2 us  [flipped(): return lax.ppermute(value, axis, [(i, i ^ flip) for i in range(4)])]
where the time goes in v5:
time: 104 us
  starting transfers between devices  53.7 us (52%)
  waiting for transfers between devices  31.3 us (30%)
  Pallas kernels  18.1 us (17%)
    ppermute x24, starting transfers between devices, flipped(): return lax.ppermute(value, axis, [(i, i ^ flip) for i in range(4)])  34.3 us
    ppermute x24, waiting for transfers between devices, flipped(): return lax.ppermute(value, axis, [(i, i ^ flip) for i in range(4)])  22.2 us
    ppermute x10, starting transfers between devices, swap(): return lax.ppermute(value, axis, [(0, 1), (1, 0)])  19.4 us
    ppermute x10, waiting for transfers between devices, swap(): return lax.ppermute(value, axis, [(0, 1), (1, 0)])  9.09 us
    pallas_call x1, Pallas kernels, end(): pl.pallas_call(end_kernel, grid=(columns // width,), in_specs=[SMEM] * 2...  4.48 us
    pallas_call x1, Pallas kernels, start(): pl.pallas_call(functools.partial(start_kernel, height), in_specs=[SMEM] +...  4.43 us
    pallas_call x1, Pallas kernels, inverse_and_fetch(): pl.pallas_call(fetch_kernel, in_specs=[VMEM, far, far], out_specs=[VMEM]...  3.62 us
    pallas_call x1, Pallas kernels, inverse_of(): pl.pallas_call(inverse_kernel, in_specs=[VMEM], out_specs=VMEM, out_shape...  3.24 us
  transfers between devices with their start and end apart: 34, of which 21 were waited for; matrix products, arithmetic and copies ran while one was open for 0% of the time, Pallas kernels for 7%

profile of v5, /device:TPU:1, one launch (start us, length us, event | category | flops | bytes accessed | tf_op | source)
XLA Modules:
  0.0 103.8 jit_solution(2611980206564450647)
XLA Ops:
  0.6 4.4 %shard_map.50 = (bf16[80,3584]{1,0:T(8,128)(2,1)S(1)}, f32[40,128]{1,0:T(8,128)S(1)}, bf16[80,896]{1,0:T(8,128)(2,1)S(1)}, bf16[80,896]{1,0:T(8,128)(2,1)S(1)}, ...) custom-call(s32[1]{0:T(128)} %bitcast.1.x_ref, bf16[8,80,3456]{2,1,0:T(8,128)(2,1)} %g_ref.3, ...), custom_call_target="tpu_custom_call" | custom-call | tf_op jit(solution)/shard_map/pallas_call | solution.py:93
  5.1 3.8 %collective-permute-start.2 = (f32[40,128]{1,0:T(8,128)S(1)}, f32[40,128]{1,0:T(8,128)S(1)}, u32[]{:S(2)}, u32[]{:S(2)}) collective-permute-start(f32[40,128]{1,0:T(8,128)S(1)} %get-tuple-element.36.own), channel_id=1, source_target_pairs={{0,2},{1,3},{2,0},{3,1},{4,6},{5,7},{6,4},{7,5},{8,10},{9,11},{10,... | collective-permute-start | bytes 61448 | tf_op jit(solution)/shard_map/ppermute | solution.py:283
  8.9 0.8 collective-permute-start.1
  9.7 0.0 collective-permute-start
  9.7 0.4 collective-permute-done.2.three
  10.1 3.0 %collective-permute-done.1.two = f32[40,128]{1,0:T(8,128)S(1)} collective-permute-done((f32[40,128]{1,0:T(8,128)S(1)}, f32[40,128]{1,0:T(8,128)S(1)}, u32[]{:S(2)}, u32[]{:S(2)}) %collective-permute-start.1) | collective-permute-done | bytes 20512 | tf_op jit(solution)/shard_map/ppermute | solution.py:283
  13.0 0.0 collective-permute-done.one
  13.0 0.7 shard_map.51
  13.8 1.9 %collective-permute-start.3 = (bf16[30,32,128]{2,1,0:T(8,128)(2,1)S(1)}, bf16[30,32,128]{2,1,0:T(8,128)(2,1)S(1)}, u32[]{:S(2)}, u32[]{:S(2)}) collective-permute-start(bf16[30,32,128]{2,1,0:T(8,128)(2,1)S(1)} %get-tuple-element.39), channel_id=1, source_target_pairs={{0,4},{4,0},{1,5},{5,1},{2,6},{6,2},{3,7},{7,3},{8,12},{12,8},{9,1... | collective-permute-start | bytes 737288 | tf_op jit(solution)/shard_map/ppermute | solution.py:287
  15.7 1.1 %collective-permute-done.3.b_ref = bf16[30,32,128]{2,1,0:T(8,128)(2,1)S(1)} collective-permute-done((bf16[30,32,128]{2,1,0:T(8,128)(2,1)S(1)}, bf16[30,32,128]{2,1,0:T(8,128)(2,1)S(1)}, u32[]{:S(2)}, u32[]{:S(2)}) %collective-permute-start.3) | collective-permute-done | bytes 245792 | tf_op jit(solution)/shard_map/ppermute | solution.py:287
  16.8 0.1 shard_map.52
  16.9 2.8 %collective-permute-start.4 = (bf16[8,32,128]{2,1,0:T(8,128)(2,1)S(1)}, bf16[8,32,128]{2,1,0:T(8,128)(2,1)S(1)}, u32[]{:S(2)}, u32[]{:S(2)}) collective-permute-start(bf16[8,32,128]{2,1,0:T(8,128)(2,1)S(1)} %get-tuple-element.41), channel_id=1, source_target_pairs={{0,128},{64,192},{128,0},{192,64},{1,129},{65,193},{129,1},{193,65... | collective-permute-start | bytes 196616 | tf_op jit(solution)/shard_map/ppermute | solution.py:283
  19.7 0.3 collective-permute-start.5
  20.0 0.5 collective-permute-start.6
  20.6 1.0 collective-permute-done.4.refs_1_
  21.6 1.6 %collective-permute-done.5.refs_2_ = bf16[8,32,128]{2,1,0:T(8,128)(2,1)S(1)} collective-permute-done((bf16[8,32,128]{2,1,0:T(8,128)(2,1)S(1)}, bf16[8,32,128]{2,1,0:T(8,128)(2,1)S(1)}, u32[]{:S(2)}, u32[]{:S(2)}) %collective-permute-start.5) | collective-permute-done | bytes 65568 | tf_op jit(solution)/shard_map/ppermute | solution.py:283
  23.2 1.1 %collective-permute-done.6.refs_3_ = bf16[8,32,128]{2,1,0:T(8,128)(2,1)S(1)} collective-permute-done((bf16[8,32,128]{2,1,0:T(8,128)(2,1)S(1)}, bf16[8,32,128]{2,1,0:T(8,128)(2,1)S(1)}, u32[]{:S(2)}, u32[]{:S(2)}) %collective-permute-start.6) | collective-permute-done | bytes 65568 | tf_op jit(solution)/shard_map/ppermute | solution.py:283
  24.4 1.7 %collective-permute-start.7 = (bf16[8,32,128]{2,1,0:T(8,128)(2,1)S(1)}, bf16[8,32,128]{2,1,0:T(8,128)(2,1)S(1)}, u32[]{:S(2)}, u32[]{:S(2)}) collective-permute-start(bf16[8,32,128]{2,1,0:T(8,128)(2,1)S(1)} %shard_map.53.refs_0_), channel_id=1, source_target_pairs={{0,8},{8,0},{1,9},{9,1},{2,10},{10,2},{3,11},{11,3},{4,12},{12,4},... | collective-permute-start | bytes 196616 | tf_op jit(solution)/shard_map/ppermute | solution.py:287
  26.1 1.7 %collective-permute-done.7.refs_1_ = bf16[8,32,128]{2,1,0:T(8,128)(2,1)S(1)} collective-permute-done((bf16[8,32,128]{2,1,0:T(8,128)(2,1)S(1)}, bf16[8,32,128]{2,1,0:T(8,128)(2,1)S(1)}, u32[]{:S(2)}, u32[]{:S(2)}) %collective-permute-start.7) | collective-permute-done | bytes 65568 | tf_op jit(solution)/shard_map/ppermute | solution.py:287
  27.8 6.8 %collective-permute-start.10 = (bf16[8,32,128]{2,1,0:T(8,128)(2,1)S(1)}, bf16[8,32,128]{2,1,0:T(8,128)(2,1)S(1)}, u32[]{:S(2)}, u32[]{:S(2)}) collective-permute-start(bf16[8,32,128]{2,1,0:T(8,128)(2,1)S(1)} %shard_map.54.refs_0_), channel_id=1, source_target_pairs={{0,32},{16,48},{32,0},{48,16},{1,33},{17,49},{33,1},{49,17},{2,34}... | collective-permute-start | bytes 196616 | tf_op jit(solution)/shard_map/ppermute | solution.py:283
  34.6 1.6 %collective-permute-start.12 = (bf16[80,896]{1,0:T(8,128)(2,1)S(1)}, bf16[80,896]{1,0:T(8,128)(2,1)S(1)}, u32[]{:S(2)}, u32[]{:S(2)}) collective-permute-start(bf16[80,896]{1,0:T(8,128)(2,1)S(1)} %get-tuple-element.45), channel_id=1, source_target_pairs={{0,128},{64,192},{128,0},{192,64},{1,129},{65,193},{129,1},{193,65... | collective-permute-start | bytes 430088 | tf_op jit(solution)/shard_map/ppermute | solution.py:283
  36.2 0.8 collective-permute-start.13
  37.0 0.9 collective-permute-start.14
  37.9 1.2 %collective-permute-start.8 = (bf16[8,32,128]{2,1,0:T(8,128)(2,1)S(1)}, bf16[8,32,128]{2,1,0:T(8,128)(2,1)S(1)}, u32[]{:S(2)}, u32[]{:S(2)}) collective-permute-start(bf16[8,32,128]{2,1,0:T(8,128)(2,1)S(1)} %shard_map.54.refs_0_), channel_id=1, source_target_pairs={{0,16},{16,0},{32,48},{48,32},{1,17},{17,1},{33,49},{49,33},{2,18}... | collective-permute-start | bytes 196616 | tf_op jit(solution)/shard_map/ppermute | solution.py:283
  39.1 4.1 %collective-permute-done.9.refs_2_ = bf16[8,32,128]{2,1,0:T(8,128)(2,1)S(1)} collective-permute-done((bf16[8,32,128]{2,1,0:T(8,128)(2,1)S(1)}, bf16[8,32,128]{2,1,0:T(8,128)(2,1)S(1)}, u32[]{:S(2)}, u32[]{:S(2)}) %collective-permute-start.9) | collective-permute-done | bytes 65568 | tf_op jit(solution)/shard_map/ppermute | solution.py:283
  43.2 0.4 collective-permute-done.8.refs_1_
  43.6 5.9 %collective-permute-start.11 = (bf16[8,32,128]{2,1,0:T(8,128)(2,1)S(1)}, bf16[8,32,128]{2,1,0:T(8,128)(2,1)S(1)}, u32[]{:S(2)}, u32[]{:S(2)}) collective-permute-start(bf16[8,32,128]{2,1,0:T(8,128)(2,1)S(1)} %shard_map.55.part_ref), channel_id=1, source_target_pairs={{0,4},{4,0},{1,5},{5,1},{2,6},{6,2},{3,7},{7,3},{8,12},{12,8},{9,1... | collective-permute-start | bytes 196616 | tf_op jit(solution)/shard_map/ppermute | solution.py:287
  49.5 0.9 collective-permute-done.11.other_ref
  50.4 0.3 shard_map.56
  50.8 0.1 collective-permute-start.17
  50.9 1.8 %collective-permute-start.16 = (f32[64,384]{1,0:T(8,128)S(1)}, f32[64,384]{1,0:T(8,128)S(1)}, u32[]{:S(2)}, u32[]{:S(2)}) collective-permute-start(f32[64,384]{1,0:T(8,128)S(1)} %get-tuple-element.48.refs_0_), channel_id=1, source_target_pairs={{0,192},{64,128},{128,64},{192,0},{1,193},{65,129},{129,65},{193,1... | collective-permute-start | bytes 294920 | tf_op jit(solution)/shard_map/ppermute | solution.py:283
  52.7 0.8 collective-permute-start.15
  53.5 2.9 %collective-permute-done.17.refs_3_ = f32[64,384]{1,0:T(8,128)S(1)} collective-permute-done((f32[64,384]{1,0:T(8,128)S(1)}, f32[64,384]{1,0:T(8,128)S(1)}, u32[]{:S(2)}, u32[]{:S(2)}) %collective-permute-start.17) | collective-permute-done | bytes 98336 | tf_op jit(solution)/shard_map/ppermute | solution.py:283
  56.4 2.4 %collective-permute-done.16.refs_2_ = f32[64,384]{1,0:T(8,128)S(1)} collective-permute-done((f32[64,384]{1,0:T(8,128)S(1)}, f32[64,384]{1,0:T(8,128)S(1)}, u32[]{:S(2)}, u32[]{:S(2)}) %collective-permute-start.16) | collective-permute-done | bytes 98336 | tf_op jit(solution)/shard_map/ppermute | solution.py:283
  58.8 0.1 shard_map.57
  58.9 1.5 %collective-permute-start.20 = (f32[160,128]{1,0:T(8,128)S(1)}, f32[160,128]{1,0:T(8,128)S(1)}, u32[]{:S(2)}, u32[]{:S(2)}) collective-permute-start(f32[160,128]{1,0:T(8,128)S(1)} %get-tuple-element.50.refs_0_), channel_id=1, source_target_pairs={{0,2},{1,3},{2,0},{3,1},{4,6},{5,7},{6,4},{7,5},{8,10},{9,11},{10,... | collective-permute-start | bytes 245768 | tf_op jit(solution)/shard_map/ppermute | solution.py:283
  60.4 0.7 collective-permute-start.19
  61.1 0.7 collective-permute-start.18
  61.8 3.2 %shard_map.58.inverse_ref = f32[64,64]{1,0:T(8,128)S(1)} custom-call(f32[64,64]{1,0:T(8,128)S(1)} %get-tuple-element.49.gram_ref), custom_call_target="tpu_custom_call" | custom-call | flops 10000000 | bytes 5000000 | tf_op jit(solution)/shard_map/pallas_call | solution.py:404
  65.0 1.3 %collective-permute-done.19.refs_2_ = f32[160,128]{1,0:T(8,128)S(1)} collective-permute-done((f32[160,128]{1,0:T(8,128)S(1)}, f32[160,128]{1,0:T(8,128)S(1)}, u32[]{:S(2)}, u32[]{:S(2)}) %collective-permute-start.19) | collective-permute-done | bytes 81952 | tf_op jit(solution)/shard_map/ppermute | solution.py:283
  66.3 0.9 shard_map.59
  67.2 1.1 %collective-permute-start.21 = (f32[8,32,128]{2,1,0:T(8,128)S(1)}, f32[8,32,128]{2,1,0:T(8,128)S(1)}, u32[]{:S(2)}, u32[]{:S(2)}) collective-permute-start(f32[8,32,128]{2,1,0:T(8,128)S(1)} %get-tuple-element.53), channel_id=1, source_target_pairs={{0,4},{4,0},{1,5},{5,1},{2,6},{6,2},{3,7},{7,3},{8,12},{12,8},{9,1... | collective-permute-start | bytes 393224 | tf_op jit(solution)/shard_map/ppermute | solution.py:287
  68.3 1.0 collective-permute-done.21.refs_1_
  69.3 1.4 %collective-permute-start.22 = (f32[8,16,128]{2,1,0:T(8,128)S(1)}, f32[8,16,128]{2,1,0:T(8,128)S(1)}, u32[]{:S(2)}, u32[]{:S(2)}) collective-permute-start(f32[8,16,128]{2,1,0:T(8,128)S(1)} %get-tuple-element.55), channel_id=1, source_target_pairs={{0,8},{8,0},{1,9},{9,1},{2,10},{10,2},{3,11},{11,3},{4,12},{12,4},... | collective-permute-start | bytes 196616 | tf_op jit(solution)/shard_map/ppermute | solution.py:287
  70.7 1.8 %collective-permute-done.22.refs_1_ = f32[8,16,128]{2,1,0:T(8,128)S(1)} collective-permute-done((f32[8,16,128]{2,1,0:T(8,128)S(1)}, f32[8,16,128]{2,1,0:T(8,128)S(1)}, u32[]{:S(2)}, u32[]{:S(2)}) %collective-permute-start.22) | collective-permute-done | bytes 65568 | tf_op jit(solution)/shard_map/ppermute | solution.py:287
  72.5 3.7 %collective-permute-start.25 = (f32[8,16,128]{2,1,0:T(8,128)S(1)}, f32[8,16,128]{2,1,0:T(8,128)S(1)}, u32[]{:S(2)}, u32[]{:S(2)}) collective-permute-start(f32[8,16,128]{2,1,0:T(8,128)S(1)} %shard_map.61.refs_0_), channel_id=1, source_target_pairs={{0,32},{16,48},{32,0},{48,16},{1,33},{17,49},{33,1},{49,17},{2,34}... | collective-permute-start | bytes 196616 | tf_op jit(solution)/shard_map/ppermute | solution.py:283
  76.2 0.5 collective-permute-start.24
  76.7 1.6 %collective-permute-start.23 = (f32[8,16,128]{2,1,0:T(8,128)S(1)}, f32[8,16,128]{2,1,0:T(8,128)S(1)}, u32[]{:S(2)}, u32[]{:S(2)}) collective-permute-start(f32[8,16,128]{2,1,0:T(8,128)S(1)} %shard_map.61.refs_0_), channel_id=1, source_target_pairs={{0,16},{16,0},{32,48},{48,32},{1,17},{17,1},{33,49},{49,33},{2,18}... | collective-permute-start | bytes 196616 | tf_op jit(solution)/shard_map/ppermute | solution.py:283
  78.2 1.4 %collective-permute-done.25.refs_3_ = f32[8,16,128]{2,1,0:T(8,128)S(1)} collective-permute-done((f32[8,16,128]{2,1,0:T(8,128)S(1)}, f32[8,16,128]{2,1,0:T(8,128)S(1)}, u32[]{:S(2)}, u32[]{:S(2)}) %collective-permute-start.25) | collective-permute-done | bytes 65568 | tf_op jit(solution)/shard_map/ppermute | solution.py:283
  79.6 2.6 %collective-permute-done.24.refs_2_ = f32[8,16,128]{2,1,0:T(8,128)S(1)} collective-permute-done((f32[8,16,128]{2,1,0:T(8,128)S(1)}, f32[8,16,128]{2,1,0:T(8,128)S(1)}, u32[]{:S(2)}, u32[]{:S(2)}) %collective-permute-start.24) | collective-permute-done | bytes 65568 | tf_op jit(solution)/shard_map/ppermute | solution.py:283
  82.2 1.8 %collective-permute-start.26 = (f32[8,16,128]{2,1,0:T(8,128)S(1)}, f32[8,16,128]{2,1,0:T(8,128)S(1)}, u32[]{:S(2)}, u32[]{:S(2)}) collective-permute-start(f32[8,16,128]{2,1,0:T(8,128)S(1)} %shard_map.62.here_ref), channel_id=1, source_target_pairs={{0,8},{8,0},{1,9},{9,1},{2,10},{10,2},{3,11},{11,3},{4,12},{12,4},... | collective-permute-start | bytes 196616 | tf_op jit(solution)/shard_map/ppermute | solution.py:287
  84.0 1.7 %collective-permute-done.26.there_ref = f32[8,16,128]{2,1,0:T(8,128)S(1)} collective-permute-done((f32[8,16,128]{2,1,0:T(8,128)S(1)}, f32[8,16,128]{2,1,0:T(8,128)S(1)}, u32[]{:S(2)}, u32[]{:S(2)}) %collective-permute-start.26) | collective-permute-done | bytes 65568 | tf_op jit(solution)/shard_map/ppermute | solution.py:287
  85.7 0.1 shard_map.63
  85.7 2.8 %collective-permute-start.29 = (f32[7,32,128]{2,1,0:T(8,128)S(1)}, f32[7,32,128]{2,1,0:T(8,128)S(1)}, u32[]{:S(2)}, u32[]{:S(2)}) collective-permute-start(f32[7,32,128]{2,1,0:T(8,128)S(1)} %get-tuple-element.56.refs_0_), channel_id=1, source_target_pairs={{0,128},{64,192},{128,0},{192,64},{1,129},{65,193},{129,1},{193,65... | collective-permute-start | bytes 344072 | tf_op jit(solution)/shard_map/ppermute | solution.py:283
  88.6 0.6 collective-permute-start.28
  89.1 4.3 %collective-permute-start.30 = (f32[7,32,128]{2,1,0:T(8,128)S(1)}, f32[7,32,128]{2,1,0:T(8,128)S(1)}, u32[]{:S(2)}, u32[]{:S(2)}) collective-permute-start(f32[7,32,128]{2,1,0:T(8,128)S(1)} %get-tuple-element.56.refs_0_), channel_id=1, source_target_pairs={{0,4},{4,0},{1,5},{5,1},{2,6},{6,2},{3,7},{7,3},{8,12},{12,8},{9,1... | collective-permute-start | bytes 344072 | tf_op jit(solution)/shard_map/ppermute | solution.py:287
  93.5 3.6 %shard_map.64 = (f32[64,64]{1,0:T(8,128)S(1)}, bf16[8,80,3456]{2,1,0:T(8,128)(2,1)S(1)}, bf16[8,80,3456]{2,1,0:T(8,128)(2,1)S(1)}) custom-call(f32[64,64]{1,0:T(8,128)S(1)} %get-tuple-element.57.gram_ref, bf16[8,80,3456]{2,1,0:T(8,128)(2,1)} %g_ref.3, bf16[8,80,3456]{2,1,0:T(8,128)(2,1)} %e_ref.3), custom_call_target="tpu_custom_call" | custom-call | flops 10000000 | bytes 5000000 | tf_op jit(solution)/shard_map/pallas_call | solution.py:428
  97.2 0.7 collective-permute-start.31
  97.9 0.0 collective-permute-start.32
  97.9 0.5 collective-permute-start.33
  98.4 0.5 collective-permute-done.31.refs_5_
  98.8 0.4 collective-permute-done.32.refs_6_
  99.2 0.2 collective-permute-done.33.refs_7_
  99.4 4.5 %shard_map.65 = (bf16[8,80,3456]{2,1,0:T(8,128)(2,1)}, f32[64,3456]{1,0:T(8,128)}) custom-call(s32[1]{0:T(128)} %bitcast.core_ref, s32[1]{0:T(128)} %bitcast.1.x_ref, f32[7,32,128]{2,1,0:T(8,128)S(1)} %get-tuple-element.56.refs_0_, f32[7,32,128]{2,1,0:T(8,128)S(1)} %collective-permute-done.27.refs_1_, f32[7,32,128]{2,1,0:T(8,128)S(1)} %collective-permute-done.28.refs_2_, ...), custom_call_target="tpu_custom_call" | custom-call | tf_op jit(solution)/shard_map/pallas_call | solution.py:473
  (20 shorter events, 0.2 us)
Async XLA Ops:
  5.1 5.0 %collective-permute-start.2 = (f32[40,128]{1,0:T(8,128)S(1)}, f32[40,128]{1,0:T(8,128)S(1)}, u32[]{:S(2)}, u32[]{:S(2)}) collective-permute-start(f32[40,128]{1,0:T(8,128)S(1)} %get-tuple-element.36.own), channel_id=1, source_target_pairs={{0,2},{1,3},{2,0},{3,1},{4,6},{5,7},{6,4},{7,5},{8,10},{9,11},{10,... | collective-permute-start | bytes 61448 | tf_op jit(solution)/shard_map/ppermute | solution.py:283
  8.9 4.1 %collective-permute-start.1 = (f32[40,128]{1,0:T(8,128)S(1)}, f32[40,128]{1,0:T(8,128)S(1)}, u32[]{:S(2)}, u32[]{:S(2)}) collective-permute-start(f32[40,128]{1,0:T(8,128)S(1)} %get-tuple-element.36.own), channel_id=1, source_target_pairs={{0,3},{1,2},{2,1},{3,0},{4,7},{5,6},{6,5},{7,4},{8,11},{9,10},{10,... | collective-permute-start | bytes 61448 | tf_op jit(solution)/shard_map/ppermute | solution.py:283
  9.7 3.4 %collective-permute-start = (f32[40,128]{1,0:T(8,128)S(1)}, f32[40,128]{1,0:T(8,128)S(1)}, u32[]{:S(2)}, u32[]{:S(2)}) collective-permute-start(f32[40,128]{1,0:T(8,128)S(1)} %get-tuple-element.36.own), channel_id=1, source_target_pairs={{0,1},{1,0},{2,3},{3,2},{4,5},{5,4},{6,7},{7,6},{8,9},{9,8},{10,11... | collective-permute-start | bytes 61448 | tf_op jit(solution)/shard_map/ppermute | solution.py:283
  13.8 3.0 %collective-permute-start.3 = (bf16[30,32,128]{2,1,0:T(8,128)(2,1)S(1)}, bf16[30,32,128]{2,1,0:T(8,128)(2,1)S(1)}, u32[]{:S(2)}, u32[]{:S(2)}) collective-permute-start(bf16[30,32,128]{2,1,0:T(8,128)(2,1)S(1)} %get-tuple-element.39), channel_id=1, source_target_pairs={{0,4},{4,0},{1,5},{5,1},{2,6},{6,2},{3,7},{7,3},{8,12},{12,8},{9,1... | collective-permute-start | bytes 737288 | tf_op jit(solution)/shard_map/ppermute | solution.py:287
  16.9 4.7 %collective-permute-start.4 = (bf16[8,32,128]{2,1,0:T(8,128)(2,1)S(1)}, bf16[8,32,128]{2,1,0:T(8,128)(2,1)S(1)}, u32[]{:S(2)}, u32[]{:S(2)}) collective-permute-start(bf16[8,32,128]{2,1,0:T(8,128)(2,1)S(1)} %get-tuple-element.41), channel_id=1, source_target_pairs={{0,128},{64,192},{128,0},{192,64},{1,129},{65,193},{129,1},{193,65... | collective-permute-start | bytes 196616 | tf_op jit(solution)/shard_map/ppermute | solution.py:283
  19.7 3.5 %collective-permute-start.5 = (bf16[8,32,128]{2,1,0:T(8,128)(2,1)S(1)}, bf16[8,32,128]{2,1,0:T(8,128)(2,1)S(1)}, u32[]{:S(2)}, u32[]{:S(2)}) collective-permute-start(bf16[8,32,128]{2,1,0:T(8,128)(2,1)S(1)} %get-tuple-element.42), channel_id=1, source_target_pairs={{0,64},{64,0},{128,192},{192,128},{1,65},{65,1},{129,193},{193,129... | collective-permute-start | bytes 196616 | tf_op jit(solution)/shard_map/ppermute | solution.py:283
  20.0 4.3 %collective-permute-start.6 = (bf16[8,32,128]{2,1,0:T(8,128)(2,1)S(1)}, bf16[8,32,128]{2,1,0:T(8,128)(2,1)S(1)}, u32[]{:S(2)}, u32[]{:S(2)}) collective-permute-start(bf16[8,32,128]{2,1,0:T(8,128)(2,1)S(1)} %get-tuple-element.43), channel_id=1, source_target_pairs={{0,192},{64,128},{128,64},{192,0},{1,193},{65,129},{129,65},{193,1... | collective-permute-start | bytes 196616 | tf_op jit(solution)/shard_map/ppermute | solution.py:283
  24.4 3.4 %collective-permute-start.7 = (bf16[8,32,128]{2,1,0:T(8,128)(2,1)S(1)}, bf16[8,32,128]{2,1,0:T(8,128)(2,1)S(1)}, u32[]{:S(2)}, u32[]{:S(2)}) collective-permute-start(bf16[8,32,128]{2,1,0:T(8,128)(2,1)S(1)} %shard_map.53.refs_0_), channel_id=1, source_target_pairs={{0,8},{8,0},{1,9},{9,1},{2,10},{10,2},{3,11},{11,3},{4,12},{12,4},... | collective-permute-start | bytes 196616 | tf_op jit(solution)/shard_map/ppermute | solution.py:287
  27.8 10.1 %collective-permute-start.10 = (bf16[8,32,128]{2,1,0:T(8,128)(2,1)S(1)}, bf16[8,32,128]{2,1,0:T(8,128)(2,1)S(1)}, u32[]{:S(2)}, u32[]{:S(2)}) collective-permute-start(bf16[8,32,128]{2,1,0:T(8,128)(2,1)S(1)} %shard_map.54.refs_0_), channel_id=1, source_target_pairs={{0,32},{16,48},{32,0},{48,16},{1,33},{17,49},{33,1},{49,17},{2,34}... | collective-permute-start | bytes 196616 | tf_op jit(solution)/shard_map/ppermute | solution.py:283
  34.6 14.9 %collective-permute-start.12 = (bf16[80,896]{1,0:T(8,128)(2,1)S(1)}, bf16[80,896]{1,0:T(8,128)(2,1)S(1)}, u32[]{:S(2)}, u32[]{:S(2)}) collective-permute-start(bf16[80,896]{1,0:T(8,128)(2,1)S(1)} %get-tuple-element.45), channel_id=1, source_target_pairs={{0,128},{64,192},{128,0},{192,64},{1,129},{65,193},{129,1},{193,65... | collective-permute-start | bytes 430088 | tf_op jit(solution)/shard_map/ppermute | solution.py:283
  36.2 13.3 %collective-permute-start.13 = (bf16[80,896]{1,0:T(8,128)(2,1)S(1)}, bf16[80,896]{1,0:T(8,128)(2,1)S(1)}, u32[]{:S(2)}, u32[]{:S(2)}) collective-permute-start(bf16[80,896]{1,0:T(8,128)(2,1)S(1)} %get-tuple-element.46), channel_id=1, source_target_pairs={{0,64},{64,0},{128,192},{192,128},{1,65},{65,1},{129,193},{193,129... | collective-permute-start | bytes 430088 | tf_op jit(solution)/shard_map/ppermute | solution.py:283
  37.0 12.5 %collective-permute-start.14 = (bf16[80,896]{1,0:T(8,128)(2,1)S(1)}, bf16[80,896]{1,0:T(8,128)(2,1)S(1)}, u32[]{:S(2)}, u32[]{:S(2)}) collective-permute-start(bf16[80,896]{1,0:T(8,128)(2,1)S(1)} %get-tuple-element.47), channel_id=1, source_target_pairs={{0,192},{64,128},{128,64},{192,0},{1,193},{65,129},{129,65},{193,1... | collective-permute-start | bytes 430088 | tf_op jit(solution)/shard_map/ppermute | solution.py:283
  37.9 5.3 %collective-permute-start.9 = (bf16[8,32,128]{2,1,0:T(8,128)(2,1)S(1)}, bf16[8,32,128]{2,1,0:T(8,128)(2,1)S(1)}, u32[]{:S(2)}, u32[]{:S(2)}) collective-permute-start(bf16[8,32,128]{2,1,0:T(8,128)(2,1)S(1)} %shard_map.54.refs_0_), channel_id=1, source_target_pairs={{0,48},{16,32},{32,16},{48,0},{1,49},{17,33},{33,17},{49,1},{2,50}... | collective-permute-start | bytes 196616 | tf_op jit(solution)/shard_map/ppermute | solution.py:283
  37.9 5.7 %collective-permute-start.8 = (bf16[8,32,128]{2,1,0:T(8,128)(2,1)S(1)}, bf16[8,32,128]{2,1,0:T(8,128)(2,1)S(1)}, u32[]{:S(2)}, u32[]{:S(2)}) collective-permute-start(bf16[8,32,128]{2,1,0:T(8,128)(2,1)S(1)} %shard_map.54.refs_0_), channel_id=1, source_target_pairs={{0,16},{16,0},{32,48},{48,32},{1,17},{17,1},{33,49},{49,33},{2,18}... | collective-permute-start | bytes 196616 | tf_op jit(solution)/shard_map/ppermute | solution.py:283
  43.6 6.8 %collective-permute-start.11 = (bf16[8,32,128]{2,1,0:T(8,128)(2,1)S(1)}, bf16[8,32,128]{2,1,0:T(8,128)(2,1)S(1)}, u32[]{:S(2)}, u32[]{:S(2)}) collective-permute-start(bf16[8,32,128]{2,1,0:T(8,128)(2,1)S(1)} %shard_map.55.part_ref), channel_id=1, source_target_pairs={{0,4},{4,0},{1,5},{5,1},{2,6},{6,2},{3,7},{7,3},{8,12},{12,8},{9,1... | collective-permute-start | bytes 196616 | tf_op jit(solution)/shard_map/ppermute | solution.py:287
  50.8 5.7 %collective-permute-start.17 = (f32[64,384]{1,0:T(8,128)S(1)}, f32[64,384]{1,0:T(8,128)S(1)}, u32[]{:S(2)}, u32[]{:S(2)}) collective-permute-start(f32[64,384]{1,0:T(8,128)S(1)} %get-tuple-element.48.refs_0_), channel_id=1, source_target_pairs={{0,128},{64,192},{128,0},{192,64},{1,129},{65,193},{129,1},{193,65... | collective-permute-start | bytes 294920 | tf_op jit(solution)/shard_map/ppermute | solution.py:283
  50.9 7.9 %collective-permute-start.16 = (f32[64,384]{1,0:T(8,128)S(1)}, f32[64,384]{1,0:T(8,128)S(1)}, u32[]{:S(2)}, u32[]{:S(2)}) collective-permute-start(f32[64,384]{1,0:T(8,128)S(1)} %get-tuple-element.48.refs_0_), channel_id=1, source_target_pairs={{0,192},{64,128},{128,64},{192,0},{1,193},{65,129},{129,65},{193,1... | collective-permute-start | bytes 294920 | tf_op jit(solution)/shard_map/ppermute | solution.py:283
  52.7 6.1 %collective-permute-start.15 = (f32[64,384]{1,0:T(8,128)S(1)}, f32[64,384]{1,0:T(8,128)S(1)}, u32[]{:S(2)}, u32[]{:S(2)}) collective-permute-start(f32[64,384]{1,0:T(8,128)S(1)} %get-tuple-element.48.refs_0_), channel_id=1, source_target_pairs={{0,64},{64,0},{128,192},{192,128},{1,65},{65,1},{129,193},{193,129... | collective-permute-start | bytes 294920 | tf_op jit(solution)/shard_map/ppermute | solution.py:283
  58.9 6.1 %collective-permute-start.20 = (f32[160,128]{1,0:T(8,128)S(1)}, f32[160,128]{1,0:T(8,128)S(1)}, u32[]{:S(2)}, u32[]{:S(2)}) collective-permute-start(f32[160,128]{1,0:T(8,128)S(1)} %get-tuple-element.50.refs_0_), channel_id=1, source_target_pairs={{0,2},{1,3},{2,0},{3,1},{4,6},{5,7},{6,4},{7,5},{8,10},{9,11},{10,... | collective-permute-start | bytes 245768 | tf_op jit(solution)/shard_map/ppermute | solution.py:283
  60.4 5.9 %collective-permute-start.19 = (f32[160,128]{1,0:T(8,128)S(1)}, f32[160,128]{1,0:T(8,128)S(1)}, u32[]{:S(2)}, u32[]{:S(2)}) collective-permute-start(f32[160,128]{1,0:T(8,128)S(1)} %get-tuple-element.50.refs_0_), channel_id=1, source_target_pairs={{0,3},{1,2},{2,1},{3,0},{4,7},{5,6},{6,5},{7,4},{8,11},{9,10},{10,... | collective-permute-start | bytes 245768 | tf_op jit(solution)/shard_map/ppermute | solution.py:283
  61.1 5.2 %collective-permute-start.18 = (f32[160,128]{1,0:T(8,128)S(1)}, f32[160,128]{1,0:T(8,128)S(1)}, u32[]{:S(2)}, u32[]{:S(2)}) collective-permute-start(f32[160,128]{1,0:T(8,128)S(1)} %get-tuple-element.50.refs_0_), channel_id=1, source_target_pairs={{0,1},{1,0},{2,3},{3,2},{4,5},{5,4},{6,7},{7,6},{8,9},{9,8},{10,11... | collective-permute-start | bytes 245768 | tf_op jit(solution)/shard_map/ppermute | solution.py:283
  67.2 2.1 %collective-permute-start.21 = (f32[8,32,128]{2,1,0:T(8,128)S(1)}, f32[8,32,128]{2,1,0:T(8,128)S(1)}, u32[]{:S(2)}, u32[]{:S(2)}) collective-permute-start(f32[8,32,128]{2,1,0:T(8,128)S(1)} %get-tuple-element.53), channel_id=1, source_target_pairs={{0,4},{4,0},{1,5},{5,1},{2,6},{6,2},{3,7},{7,3},{8,12},{12,8},{9,1... | collective-permute-start | bytes 393224 | tf_op jit(solution)/shard_map/ppermute | solution.py:287
  69.3 3.2 %collective-permute-start.22 = (f32[8,16,128]{2,1,0:T(8,128)S(1)}, f32[8,16,128]{2,1,0:T(8,128)S(1)}, u32[]{:S(2)}, u32[]{:S(2)}) collective-permute-start(f32[8,16,128]{2,1,0:T(8,128)S(1)} %get-tuple-element.55), channel_id=1, source_target_pairs={{0,8},{8,0},{1,9},{9,1},{2,10},{10,2},{3,11},{11,3},{4,12},{12,4},... | collective-permute-start | bytes 196616 | tf_op jit(solution)/shard_map/ppermute | solution.py:287
  72.5 7.1 %collective-permute-start.25 = (f32[8,16,128]{2,1,0:T(8,128)S(1)}, f32[8,16,128]{2,1,0:T(8,128)S(1)}, u32[]{:S(2)}, u32[]{:S(2)}) collective-permute-start(f32[8,16,128]{2,1,0:T(8,128)S(1)} %shard_map.61.refs_0_), channel_id=1, source_target_pairs={{0,32},{16,48},{32,0},{48,16},{1,33},{17,49},{33,1},{49,17},{2,34}... | collective-permute-start | bytes 196616 | tf_op jit(solution)/shard_map/ppermute | solution.py:283
  76.2 6.0 %collective-permute-start.24 = (f32[8,16,128]{2,1,0:T(8,128)S(1)}, f32[8,16,128]{2,1,0:T(8,128)S(1)}, u32[]{:S(2)}, u32[]{:S(2)}) collective-permute-start(f32[8,16,128]{2,1,0:T(8,128)S(1)} %shard_map.61.refs_0_), channel_id=1, source_target_pairs={{0,48},{16,32},{32,16},{48,0},{1,49},{17,33},{33,17},{49,1},{2,50}... | collective-permute-start | bytes 196616 | tf_op jit(solution)/shard_map/ppermute | solution.py:283
  76.7 5.5 %collective-permute-start.23 = (f32[8,16,128]{2,1,0:T(8,128)S(1)}, f32[8,16,128]{2,1,0:T(8,128)S(1)}, u32[]{:S(2)}, u32[]{:S(2)}) collective-permute-start(f32[8,16,128]{2,1,0:T(8,128)S(1)} %shard_map.61.refs_0_), channel_id=1, source_target_pairs={{0,16},{16,0},{32,48},{48,32},{1,17},{17,1},{33,49},{49,33},{2,18}... | collective-permute-start | bytes 196616 | tf_op jit(solution)/shard_map/ppermute | solution.py:283
  82.2 3.5 %collective-permute-start.26 = (f32[8,16,128]{2,1,0:T(8,128)S(1)}, f32[8,16,128]{2,1,0:T(8,128)S(1)}, u32[]{:S(2)}, u32[]{:S(2)}) collective-permute-start(f32[8,16,128]{2,1,0:T(8,128)S(1)} %shard_map.62.here_ref), channel_id=1, source_target_pairs={{0,8},{8,0},{1,9},{9,1},{2,10},{10,2},{3,11},{11,3},{4,12},{12,4},... | collective-permute-start | bytes 196616 | tf_op jit(solution)/shard_map/ppermute | solution.py:287
  85.7 11.4 %collective-permute-start.29 = (f32[7,32,128]{2,1,0:T(8,128)S(1)}, f32[7,32,128]{2,1,0:T(8,128)S(1)}, u32[]{:S(2)}, u32[]{:S(2)}) collective-permute-start(f32[7,32,128]{2,1,0:T(8,128)S(1)} %get-tuple-element.56.refs_0_), channel_id=1, source_target_pairs={{0,128},{64,192},{128,0},{192,64},{1,129},{65,193},{129,1},{193,65... | collective-permute-start | bytes 344072 | tf_op jit(solution)/shard_map/ppermute | solution.py:283
  88.6 8.6 %collective-permute-start.28 = (f32[7,32,128]{2,1,0:T(8,128)S(1)}, f32[7,32,128]{2,1,0:T(8,128)S(1)}, u32[]{:S(2)}, u32[]{:S(2)}) collective-permute-start(f32[7,32,128]{2,1,0:T(8,128)S(1)} %get-tuple-element.56.refs_0_), channel_id=1, source_target_pairs={{0,192},{64,128},{128,64},{192,0},{1,193},{65,129},{129,65},{193,1... | collective-permute-start | bytes 344072 | tf_op jit(solution)/shard_map/ppermute | solution.py:283
  89.1 8.0 %collective-permute-start.27 = (f32[7,32,128]{2,1,0:T(8,128)S(1)}, f32[7,32,128]{2,1,0:T(8,128)S(1)}, u32[]{:S(2)}, u32[]{:S(2)}) collective-permute-start(f32[7,32,128]{2,1,0:T(8,128)S(1)} %get-tuple-element.56.refs_0_), channel_id=1, source_target_pairs={{0,64},{64,0},{128,192},{192,128},{1,65},{65,1},{129,193},{193,129... | collective-permute-start | bytes 344072 | tf_op jit(solution)/shard_map/ppermute | solution.py:283
  89.1 9.2 %collective-permute-start.30 = (f32[7,32,128]{2,1,0:T(8,128)S(1)}, f32[7,32,128]{2,1,0:T(8,128)S(1)}, u32[]{:S(2)}, u32[]{:S(2)}) collective-permute-start(f32[7,32,128]{2,1,0:T(8,128)S(1)} %get-tuple-element.56.refs_0_), channel_id=1, source_target_pairs={{0,4},{4,0},{1,5},{5,1},{2,6},{6,2},{3,7},{7,3},{8,12},{12,8},{9,1... | collective-permute-start | bytes 344072 | tf_op jit(solution)/shard_map/ppermute | solution.py:287
  97.2 1.7 %collective-permute-start.31 = (f32[7,32,128]{2,1,0:T(8,128)S(1)}, f32[7,32,128]{2,1,0:T(8,128)S(1)}, u32[]{:S(2)}, u32[]{:S(2)}) collective-permute-start(f32[7,32,128]{2,1,0:T(8,128)S(1)} %collective-permute-done.27.refs_1_), channel_id=1, source_target_pairs={{0,4},{4,0},{1,5},{5,1},{2,6},{6,2},{3,7},{7,3},{8,12},{12,8},{9,1... | collective-permute-start | bytes 344072 | tf_op jit(solution)/shard_map/ppermute | solution.py:287
  97.9 1.3 %collective-permute-start.32 = (f32[7,32,128]{2,1,0:T(8,128)S(1)}, f32[7,32,128]{2,1,0:T(8,128)S(1)}, u32[]{:S(2)}, u32[]{:S(2)}) collective-permute-start(f32[7,32,128]{2,1,0:T(8,128)S(1)} %collective-permute-done.28.refs_2_), channel_id=1, source_target_pairs={{0,4},{4,0},{1,5},{5,1},{2,6},{6,2},{3,7},{7,3},{8,12},{12,8},{9,1... | collective-permute-start | bytes 344072 | tf_op jit(solution)/shard_map/ppermute | solution.py:287
  97.9 1.5 %collective-permute-start.33 = (f32[7,32,128]{2,1,0:T(8,128)S(1)}, f32[7,32,128]{2,1,0:T(8,128)S(1)}, u32[]{:S(2)}, u32[]{:S(2)}) collective-permute-start(f32[7,32,128]{2,1,0:T(8,128)S(1)} %collective-permute-done.29.refs_3_), channel_id=1, source_target_pairs={{0,4},{4,0},{1,5},{5,1},{2,6},{6,2},{3,7},{7,3},{8,12},{12,8},{9,1... | collective-permute-start | bytes 344072 | tf_op jit(solution)/shard_map/ppermute | solution.py:287

commit v6 on v5

--- a/solution.py
+++ b/solution.py
@@ -465,7 +465,7 @@
             new_ref[replica, :, part] = (corrected.astype(F32) - recon).astype(BF16)
 
 
-def end(place, here, there, p, inverse, gradient, error, width=1152):
+def end(place, here, there, p, inverse, gradient, error, width=384):
     replicas, rows, columns = gradient.shape
     rank = p.shape[1]
     per = here[0].shape[0]

time: 104 us -> 106 us (1.019)
  Pallas kernels: 18.1 us -> 20.4 us
    pallas_call x1, Pallas kernels: 4.48 us -> 6.76 us  [end(): pl.pallas_call(end_kernel, grid=(columns // width,), in_specs=[SMEM] * 2...]
where the time goes in v6:
time: 106 us
  starting transfers between devices  53.7 us (51%)
  waiting for transfers between devices  31.3 us (30%)
  Pallas kernels  20.4 us (19%)
    ppermute x24, starting transfers between devices, flipped(): return lax.ppermute(value, axis, [(i, i ^ flip) for i in range(4)])  34.3 us
    ppermute x24, waiting for transfers between devices, flipped(): return lax.ppermute(value, axis, [(i, i ^ flip) for i in range(4)])  22.2 us
    ppermute x10, starting transfers between devices, swap(): return lax.ppermute(value, axis, [(0, 1), (1, 0)])  19.4 us
    ppermute x10, waiting for transfers between devices, swap(): return lax.ppermute(value, axis, [(0, 1), (1, 0)])  9.09 us
    pallas_call x1, Pallas kernels, end(): pl.pallas_call(end_kernel, grid=(columns // width,), in_specs=[SMEM] * 2...  6.76 us
    pallas_call x1, Pallas kernels, start(): pl.pallas_call(functools.partial(start_kernel, height), in_specs=[SMEM] +...  4.43 us
    pallas_call x1, Pallas kernels, inverse_and_fetch(): pl.pallas_call(fetch_kernel, in_specs=[VMEM, far, far], out_specs=[VMEM]...  3.62 us
    pallas_call x1, Pallas kernels, inverse_of(): pl.pallas_call(inverse_kernel, in_specs=[VMEM], out_specs=VMEM, out_shape...  3.24 us
  transfers between devices with their start and end apart: 34, of which 21 were waited for; matrix products, arithmetic and copies ran while one was open for 0% of the time, Pallas kernels for 7%

profile of v6, /device:TPU:1, one launch (start us, length us, event | category | flops | bytes accessed | tf_op | source)
XLA Modules:
  0.0 106.1 jit_solution(1800381994239677217)
XLA Ops:
  0.6 4.4 %shard_map.50 = (bf16[80,3584]{1,0:T(8,128)(2,1)S(1)}, f32[40,128]{1,0:T(8,128)S(1)}, bf16[80,896]{1,0:T(8,128)(2,1)S(1)}, bf16[80,896]{1,0:T(8,128)(2,1)S(1)}, ...) custom-call(s32[1]{0:T(128)} %bitcast.1.x_ref, bf16[8,80,3456]{2,1,0:T(8,128)(2,1)} %g_ref.3, ...), custom_call_target="tpu_custom_call" | custom-call | tf_op jit(solution)/shard_map/pallas_call | solution.py:93
  5.1 3.8 %collective-permute-start.2 = (f32[40,128]{1,0:T(8,128)S(1)}, f32[40,128]{1,0:T(8,128)S(1)}, u32[]{:S(2)}, u32[]{:S(2)}) collective-permute-start(f32[40,128]{1,0:T(8,128)S(1)} %get-tuple-element.36.own), channel_id=1, source_target_pairs={{0,2},{1,3},{2,0},{3,1},{4,6},{5,7},{6,4},{7,5},{8,10},{9,11},{10,... | collective-permute-start | bytes 61448 | tf_op jit(solution)/shard_map/ppermute | solution.py:283
  8.9 0.8 collective-permute-start.1
  9.7 0.0 collective-permute-start
  9.7 0.4 collective-permute-done.2.three
  10.1 3.0 %collective-permute-done.1.two = f32[40,128]{1,0:T(8,128)S(1)} collective-permute-done((f32[40,128]{1,0:T(8,128)S(1)}, f32[40,128]{1,0:T(8,128)S(1)}, u32[]{:S(2)}, u32[]{:S(2)}) %collective-permute-start.1) | collective-permute-done | bytes 20512 | tf_op jit(solution)/shard_map/ppermute | solution.py:283
  13.0 0.7 shard_map.51
  13.8 1.9 %collective-permute-start.3 = (bf16[30,32,128]{2,1,0:T(8,128)(2,1)S(1)}, bf16[30,32,128]{2,1,0:T(8,128)(2,1)S(1)}, u32[]{:S(2)}, u32[]{:S(2)}) collective-permute-start(bf16[30,32,128]{2,1,0:T(8,128)(2,1)S(1)} %get-tuple-element.39), channel_id=1, source_target_pairs={{0,4},{4,0},{1,5},{5,1},{2,6},{6,2},{3,7},{7,3},{8,12},{12,8},{9,1... | collective-permute-start | bytes 737288 | tf_op jit(solution)/shard_map/ppermute | solution.py:287
  15.7 1.1 %collective-permute-done.3.b_ref = bf16[30,32,128]{2,1,0:T(8,128)(2,1)S(1)} collective-permute-done((bf16[30,32,128]{2,1,0:T(8,128)(2,1)S(1)}, bf16[30,32,128]{2,1,0:T(8,128)(2,1)S(1)}, u32[]{:S(2)}, u32[]{:S(2)}) %collective-permute-start.3) | collective-permute-done | bytes 245792 | tf_op jit(solution)/shard_map/ppermute | solution.py:287
  16.8 0.1 shard_map.52
  16.9 2.8 %collective-permute-start.4 = (bf16[8,32,128]{2,1,0:T(8,128)(2,1)S(1)}, bf16[8,32,128]{2,1,0:T(8,128)(2,1)S(1)}, u32[]{:S(2)}, u32[]{:S(2)}) collective-permute-start(bf16[8,32,128]{2,1,0:T(8,128)(2,1)S(1)} %get-tuple-element.41), channel_id=1, source_target_pairs={{0,128},{64,192},{128,0},{192,64},{1,129},{65,193},{129,1},{193,65... | collective-permute-start | bytes 196616 | tf_op jit(solution)/shard_map/ppermute | solution.py:283
  19.7 0.3 collective-permute-start.5
  20.0 0.5 collective-permute-start.6
  20.6 1.0 collective-permute-done.4.refs_1_
  21.6 1.6 %collective-permute-done.5.refs_2_ = bf16[8,32,128]{2,1,0:T(8,128)(2,1)S(1)} collective-permute-done((bf16[8,32,128]{2,1,0:T(8,128)(2,1)S(1)}, bf16[8,32,128]{2,1,0:T(8,128)(2,1)S(1)}, u32[]{:S(2)}, u32[]{:S(2)}) %collective-permute-start.5) | collective-permute-done | bytes 65568 | tf_op jit(solution)/shard_map/ppermute | solution.py:283
  23.2 1.1 %collective-permute-done.6.refs_3_ = bf16[8,32,128]{2,1,0:T(8,128)(2,1)S(1)} collective-permute-done((bf16[8,32,128]{2,1,0:T(8,128)(2,1)S(1)}, bf16[8,32,128]{2,1,0:T(8,128)(2,1)S(1)}, u32[]{:S(2)}, u32[]{:S(2)}) %collective-permute-start.6) | collective-permute-done | bytes 65568 | tf_op jit(solution)/shard_map/ppermute | solution.py:283
  24.4 1.7 %collective-permute-start.7 = (bf16[8,32,128]{2,1,0:T(8,128)(2,1)S(1)}, bf16[8,32,128]{2,1,0:T(8,128)(2,1)S(1)}, u32[]{:S(2)}, u32[]{:S(2)}) collective-permute-start(bf16[8,32,128]{2,1,0:T(8,128)(2,1)S(1)} %shard_map.53.refs_0_), channel_id=1, source_target_pairs={{0,8},{8,0},{1,9},{9,1},{2,10},{10,2},{3,11},{11,3},{4,12},{12,4},... | collective-permute-start | bytes 196616 | tf_op jit(solution)/shard_map/ppermute | solution.py:287
  26.1 1.7 %collective-permute-done.7.refs_1_ = bf16[8,32,128]{2,1,0:T(8,128)(2,1)S(1)} collective-permute-done((bf16[8,32,128]{2,1,0:T(8,128)(2,1)S(1)}, bf16[8,32,128]{2,1,0:T(8,128)(2,1)S(1)}, u32[]{:S(2)}, u32[]{:S(2)}) %collective-permute-start.7) | collective-permute-done | bytes 65568 | tf_op jit(solution)/shard_map/ppermute | solution.py:287
  27.8 6.8 %collective-permute-start.10 = (bf16[8,32,128]{2,1,0:T(8,128)(2,1)S(1)}, bf16[8,32,128]{2,1,0:T(8,128)(2,1)S(1)}, u32[]{:S(2)}, u32[]{:S(2)}) collective-permute-start(bf16[8,32,128]{2,1,0:T(8,128)(2,1)S(1)} %shard_map.54.refs_0_), channel_id=1, source_target_pairs={{0,32},{16,48},{32,0},{48,16},{1,33},{17,49},{33,1},{49,17},{2,34}... | collective-permute-start | bytes 196616 | tf_op jit(solution)/shard_map/ppermute | solution.py:283
  34.6 1.6 %collective-permute-start.12 = (bf16[80,896]{1,0:T(8,128)(2,1)S(1)}, bf16[80,896]{1,0:T(8,128)(2,1)S(1)}, u32[]{:S(2)}, u32[]{:S(2)}) collective-permute-start(bf16[80,896]{1,0:T(8,128)(2,1)S(1)} %get-tuple-element.45), channel_id=1, source_target_pairs={{0,128},{64,192},{128,0},{192,64},{1,129},{65,193},{129,1},{193,65... | collective-permute-start | bytes 430088 | tf_op jit(solution)/shard_map/ppermute | solution.py:283
  36.2 0.8 collective-permute-start.13
  37.0 0.9 collective-permute-start.14
  37.9 1.2 %collective-permute-start.8 = (bf16[8,32,128]{2,1,0:T(8,128)(2,1)S(1)}, bf16[8,32,128]{2,1,0:T(8,128)(2,1)S(1)}, u32[]{:S(2)}, u32[]{:S(2)}) collective-permute-start(bf16[8,32,128]{2,1,0:T(8,128)(2,1)S(1)} %shard_map.54.refs_0_), channel_id=1, source_target_pairs={{0,16},{16,0},{32,48},{48,32},{1,17},{17,1},{33,49},{49,33},{2,18}... | collective-permute-start | bytes 196616 | tf_op jit(solution)/shard_map/ppermute | solution.py:283
  39.1 4.1 %collective-permute-done.9.refs_2_ = bf16[8,32,128]{2,1,0:T(8,128)(2,1)S(1)} collective-permute-done((bf16[8,32,128]{2,1,0:T(8,128)(2,1)S(1)}, bf16[8,32,128]{2,1,0:T(8,128)(2,1)S(1)}, u32[]{:S(2)}, u32[]{:S(2)}) %collective-permute-start.9) | collective-permute-done | bytes 65568 | tf_op jit(solution)/shard_map/ppermute | solution.py:283
  43.2 0.4 collective-permute-done.8.refs_1_
  43.6 5.9 %collective-permute-start.11 = (bf16[8,32,128]{2,1,0:T(8,128)(2,1)S(1)}, bf16[8,32,128]{2,1,0:T(8,128)(2,1)S(1)}, u32[]{:S(2)}, u32[]{:S(2)}) collective-permute-start(bf16[8,32,128]{2,1,0:T(8,128)(2,1)S(1)} %shard_map.55.part_ref), channel_id=1, source_target_pairs={{0,4},{4,0},{1,5},{5,1},{2,6},{6,2},{3,7},{7,3},{8,12},{12,8},{9,1... | collective-permute-start | bytes 196616 | tf_op jit(solution)/shard_map/ppermute | solution.py:287
  49.5 0.0 collective-permute-done.12.refs_1_
  49.5 0.9 collective-permute-done.11.other_ref
  50.4 0.3 shard_map.56
  50.8 0.1 collective-permute-start.17
  50.9 1.8 %collective-permute-start.16 = (f32[64,384]{1,0:T(8,128)S(1)}, f32[64,384]{1,0:T(8,128)S(1)}, u32[]{:S(2)}, u32[]{:S(2)}) collective-permute-start(f32[64,384]{1,0:T(8,128)S(1)} %get-tuple-element.48.refs_0_), channel_id=1, source_target_pairs={{0,192},{64,128},{128,64},{192,0},{1,193},{65,129},{129,65},{193,1... | collective-permute-start | bytes 294920 | tf_op jit(solution)/shard_map/ppermute | solution.py:283
  52.7 0.8 collective-permute-start.15
  53.5 2.9 %collective-permute-done.17.refs_3_ = f32[64,384]{1,0:T(8,128)S(1)} collective-permute-done((f32[64,384]{1,0:T(8,128)S(1)}, f32[64,384]{1,0:T(8,128)S(1)}, u32[]{:S(2)}, u32[]{:S(2)}) %collective-permute-start.17) | collective-permute-done | bytes 98336 | tf_op jit(solution)/shard_map/ppermute | solution.py:283
  56.4 2.4 %collective-permute-done.16.refs_2_ = f32[64,384]{1,0:T(8,128)S(1)} collective-permute-done((f32[64,384]{1,0:T(8,128)S(1)}, f32[64,384]{1,0:T(8,128)S(1)}, u32[]{:S(2)}, u32[]{:S(2)}) %collective-permute-start.16) | collective-permute-done | bytes 98336 | tf_op jit(solution)/shard_map/ppermute | solution.py:283
  58.8 0.1 shard_map.57
  58.9 1.5 %collective-permute-start.20 = (f32[160,128]{1,0:T(8,128)S(1)}, f32[160,128]{1,0:T(8,128)S(1)}, u32[]{:S(2)}, u32[]{:S(2)}) collective-permute-start(f32[160,128]{1,0:T(8,128)S(1)} %get-tuple-element.50.refs_0_), channel_id=1, source_target_pairs={{0,2},{1,3},{2,0},{3,1},{4,6},{5,7},{6,4},{7,5},{8,10},{9,11},{10,... | collective-permute-start | bytes 245768 | tf_op jit(solution)/shard_map/ppermute | solution.py:283
  60.4 0.7 collective-permute-start.19
  61.1 0.7 collective-permute-start.18
  61.8 3.2 %shard_map.58.inverse_ref = f32[64,64]{1,0:T(8,128)S(1)} custom-call(f32[64,64]{1,0:T(8,128)S(1)} %get-tuple-element.49.gram_ref), custom_call_target="tpu_custom_call" | custom-call | flops 10000000 | bytes 5000000 | tf_op jit(solution)/shard_map/pallas_call | solution.py:404
  65.0 1.3 %collective-permute-done.19.refs_2_ = f32[160,128]{1,0:T(8,128)S(1)} collective-permute-done((f32[160,128]{1,0:T(8,128)S(1)}, f32[160,128]{1,0:T(8,128)S(1)}, u32[]{:S(2)}, u32[]{:S(2)}) %collective-permute-start.19) | collective-permute-done | bytes 81952 | tf_op jit(solution)/shard_map/ppermute | solution.py:283
  66.3 0.9 shard_map.59
  67.2 1.1 %collective-permute-start.21 = (f32[8,32,128]{2,1,0:T(8,128)S(1)}, f32[8,32,128]{2,1,0:T(8,128)S(1)}, u32[]{:S(2)}, u32[]{:S(2)}) collective-permute-start(f32[8,32,128]{2,1,0:T(8,128)S(1)} %get-tuple-element.53), channel_id=1, source_target_pairs={{0,4},{4,0},{1,5},{5,1},{2,6},{6,2},{3,7},{7,3},{8,12},{12,8},{9,1... | collective-permute-start | bytes 393224 | tf_op jit(solution)/shard_map/ppermute | solution.py:287
  68.3 1.0 collective-permute-done.21.refs_1_
  69.3 1.4 %collective-permute-start.22 = (f32[8,16,128]{2,1,0:T(8,128)S(1)}, f32[8,16,128]{2,1,0:T(8,128)S(1)}, u32[]{:S(2)}, u32[]{:S(2)}) collective-permute-start(f32[8,16,128]{2,1,0:T(8,128)S(1)} %get-tuple-element.55), channel_id=1, source_target_pairs={{0,8},{8,0},{1,9},{9,1},{2,10},{10,2},{3,11},{11,3},{4,12},{12,4},... | collective-permute-start | bytes 196616 | tf_op jit(solution)/shard_map/ppermute | solution.py:287
  70.7 1.8 %collective-permute-done.22.refs_1_ = f32[8,16,128]{2,1,0:T(8,128)S(1)} collective-permute-done((f32[8,16,128]{2,1,0:T(8,128)S(1)}, f32[8,16,128]{2,1,0:T(8,128)S(1)}, u32[]{:S(2)}, u32[]{:S(2)}) %collective-permute-start.22) | collective-permute-done | bytes 65568 | tf_op jit(solution)/shard_map/ppermute | solution.py:287
  72.5 3.7 %collective-permute-start.25 = (f32[8,16,128]{2,1,0:T(8,128)S(1)}, f32[8,16,128]{2,1,0:T(8,128)S(1)}, u32[]{:S(2)}, u32[]{:S(2)}) collective-permute-start(f32[8,16,128]{2,1,0:T(8,128)S(1)} %shard_map.61.refs_0_), channel_id=1, source_target_pairs={{0,32},{16,48},{32,0},{48,16},{1,33},{17,49},{33,1},{49,17},{2,34}... | collective-permute-start | bytes 196616 | tf_op jit(solution)/shard_map/ppermute | solution.py:283
  76.2 0.5 collective-permute-start.24
  76.7 1.6 %collective-permute-start.23 = (f32[8,16,128]{2,1,0:T(8,128)S(1)}, f32[8,16,128]{2,1,0:T(8,128)S(1)}, u32[]{:S(2)}, u32[]{:S(2)}) collective-permute-start(f32[8,16,128]{2,1,0:T(8,128)S(1)} %shard_map.61.refs_0_), channel_id=1, source_target_pairs={{0,16},{16,0},{32,48},{48,32},{1,17},{17,1},{33,49},{49,33},{2,18}... | collective-permute-start | bytes 196616 | tf_op jit(solution)/shard_map/ppermute | solution.py:283
  78.2 1.4 %collective-permute-done.25.refs_3_ = f32[8,16,128]{2,1,0:T(8,128)S(1)} collective-permute-done((f32[8,16,128]{2,1,0:T(8,128)S(1)}, f32[8,16,128]{2,1,0:T(8,128)S(1)}, u32[]{:S(2)}, u32[]{:S(2)}) %collective-permute-start.25) | collective-permute-done | bytes 65568 | tf_op jit(solution)/shard_map/ppermute | solution.py:283
  79.6 2.6 %collective-permute-done.24.refs_2_ = f32[8,16,128]{2,1,0:T(8,128)S(1)} collective-permute-done((f32[8,16,128]{2,1,0:T(8,128)S(1)}, f32[8,16,128]{2,1,0:T(8,128)S(1)}, u32[]{:S(2)}, u32[]{:S(2)}) %collective-permute-start.24) | collective-permute-done | bytes 65568 | tf_op jit(solution)/shard_map/ppermute | solution.py:283
  82.2 1.8 %collective-permute-start.26 = (f32[8,16,128]{2,1,0:T(8,128)S(1)}, f32[8,16,128]{2,1,0:T(8,128)S(1)}, u32[]{:S(2)}, u32[]{:S(2)}) collective-permute-start(f32[8,16,128]{2,1,0:T(8,128)S(1)} %shard_map.62.here_ref), channel_id=1, source_target_pairs={{0,8},{8,0},{1,9},{9,1},{2,10},{10,2},{3,11},{11,3},{4,12},{12,4},... | collective-permute-start | bytes 196616 | tf_op jit(solution)/shard_map/ppermute | solution.py:287
  84.0 1.7 %collective-permute-done.26.there_ref = f32[8,16,128]{2,1,0:T(8,128)S(1)} collective-permute-done((f32[8,16,128]{2,1,0:T(8,128)S(1)}, f32[8,16,128]{2,1,0:T(8,128)S(1)}, u32[]{:S(2)}, u32[]{:S(2)}) %collective-permute-start.26) | collective-permute-done | bytes 65568 | tf_op jit(solution)/shard_map/ppermute | solution.py:287
  85.7 0.1 shard_map.63
  85.7 2.8 %collective-permute-start.29 = (f32[7,32,128]{2,1,0:T(8,128)S(1)}, f32[7,32,128]{2,1,0:T(8,128)S(1)}, u32[]{:S(2)}, u32[]{:S(2)}) collective-permute-start(f32[7,32,128]{2,1,0:T(8,128)S(1)} %get-tuple-element.56.refs_0_), channel_id=1, source_target_pairs={{0,128},{64,192},{128,0},{192,64},{1,129},{65,193},{129,1},{193,65... | collective-permute-start | bytes 344072 | tf_op jit(solution)/shard_map/ppermute | solution.py:283
  88.6 0.6 collective-permute-start.28
  89.1 4.3 %collective-permute-start.30 = (f32[7,32,128]{2,1,0:T(8,128)S(1)}, f32[7,32,128]{2,1,0:T(8,128)S(1)}, u32[]{:S(2)}, u32[]{:S(2)}) collective-permute-start(f32[7,32,128]{2,1,0:T(8,128)S(1)} %get-tuple-element.56.refs_0_), channel_id=1, source_target_pairs={{0,4},{4,0},{1,5},{5,1},{2,6},{6,2},{3,7},{7,3},{8,12},{12,8},{9,1... | collective-permute-start | bytes 344072 | tf_op jit(solution)/shard_map/ppermute | solution.py:287
  93.5 3.6 %shard_map.64 = (f32[64,64]{1,0:T(8,128)S(1)}, bf16[8,80,3456]{2,1,0:T(8,128)(2,1)S(1)}, bf16[8,80,3456]{2,1,0:T(8,128)(2,1)S(1)}) custom-call(f32[64,64]{1,0:T(8,128)S(1)} %get-tuple-element.57.gram_ref, bf16[8,80,3456]{2,1,0:T(8,128)(2,1)} %g_ref.3, bf16[8,80,3456]{2,1,0:T(8,128)(2,1)} %e_ref.3), custom_call_target="tpu_custom_call" | custom-call | flops 10000000 | bytes 5000000 | tf_op jit(solution)/shard_map/pallas_call | solution.py:428
  97.2 0.7 collective-permute-start.31
  97.9 0.0 collective-permute-start.32
  97.9 0.5 collective-permute-start.33
  98.4 0.5 collective-permute-done.31.refs_5_
  98.8 0.4 collective-permute-done.32.refs_6_
  99.2 0.2 collective-permute-done.33.refs_7_
  99.4 6.8 %shard_map.65 = (bf16[8,80,3456]{2,1,0:T(8,128)(2,1)}, f32[64,3456]{1,0:T(8,128)}) custom-call(s32[1]{0:T(128)} %bitcast.core_ref, s32[1]{0:T(128)} %bitcast.1.x_ref, f32[7,32,128]{2,1,0:T(8,128)S(1)} %get-tuple-element.56.refs_0_, f32[7,32,128]{2,1,0:T(8,128)S(1)} %collective-permute-done.27.refs_1_, f32[7,32,128]{2,1,0:T(8,128)S(1)} %collective-permute-done.28.refs_2_, ...), custom_call_target="tpu_custom_call" | custom-call | tf_op jit(solution)/shard_map/pallas_call | solution.py:473
  (20 shorter events, 0.2 us)
Async XLA Ops:
  5.1 5.0 %collective-permute-start.2 = (f32[40,128]{1,0:T(8,128)S(1)}, f32[40,128]{1,0:T(8,128)S(1)}, u32[]{:S(2)}, u32[]{:S(2)}) collective-permute-start(f32[40,128]{1,0:T(8,128)S(1)} %get-tuple-element.36.own), channel_id=1, source_target_pairs={{0,2},{1,3},{2,0},{3,1},{4,6},{5,7},{6,4},{7,5},{8,10},{9,11},{10,... | collective-permute-start | bytes 61448 | tf_op jit(solution)/shard_map/ppermute | solution.py:283
  8.9 4.1 %collective-permute-start.1 = (f32[40,128]{1,0:T(8,128)S(1)}, f32[40,128]{1,0:T(8,128)S(1)}, u32[]{:S(2)}, u32[]{:S(2)}) collective-permute-start(f32[40,128]{1,0:T(8,128)S(1)} %get-tuple-element.36.own), channel_id=1, source_target_pairs={{0,3},{1,2},{2,1},{3,0},{4,7},{5,6},{6,5},{7,4},{8,11},{9,10},{10,... | collective-permute-start | bytes 61448 | tf_op jit(solution)/shard_map/ppermute | solution.py:283
  9.7 3.4 %collective-permute-start = (f32[40,128]{1,0:T(8,128)S(1)}, f32[40,128]{1,0:T(8,128)S(1)}, u32[]{:S(2)}, u32[]{:S(2)}) collective-permute-start(f32[40,128]{1,0:T(8,128)S(1)} %get-tuple-element.36.own), channel_id=1, source_target_pairs={{0,1},{1,0},{2,3},{3,2},{4,5},{5,4},{6,7},{7,6},{8,9},{9,8},{10,11... | collective-permute-start | bytes 61448 | tf_op jit(solution)/shard_map/ppermute | solution.py:283
  13.8 3.0 %collective-permute-start.3 = (bf16[30,32,128]{2,1,0:T(8,128)(2,1)S(1)}, bf16[30,32,128]{2,1,0:T(8,128)(2,1)S(1)}, u32[]{:S(2)}, u32[]{:S(2)}) collective-permute-start(bf16[30,32,128]{2,1,0:T(8,128)(2,1)S(1)} %get-tuple-element.39), channel_id=1, source_target_pairs={{0,4},{4,0},{1,5},{5,1},{2,6},{6,2},{3,7},{7,3},{8,12},{12,8},{9,1... | collective-permute-start | bytes 737288 | tf_op jit(solution)/shard_map/ppermute | solution.py:287
  16.9 4.7 %collective-permute-start.4 = (bf16[8,32,128]{2,1,0:T(8,128)(2,1)S(1)}, bf16[8,32,128]{2,1,0:T(8,128)(2,1)S(1)}, u32[]{:S(2)}, u32[]{:S(2)}) collective-permute-start(bf16[8,32,128]{2,1,0:T(8,128)(2,1)S(1)} %get-tuple-element.41), channel_id=1, source_target_pairs={{0,128},{64,192},{128,0},{192,64},{1,129},{65,193},{129,1},{193,65... | collective-permute-start | bytes 196616 | tf_op jit(solution)/shard_map/ppermute | solution.py:283
  19.7 3.5 %collective-permute-start.5 = (bf16[8,32,128]{2,1,0:T(8,128)(2,1)S(1)}, bf16[8,32,128]{2,1,0:T(8,128)(2,1)S(1)}, u32[]{:S(2)}, u32[]{:S(2)}) collective-permute-start(bf16[8,32,128]{2,1,0:T(8,128)(2,1)S(1)} %get-tuple-element.42), channel_id=1, source_target_pairs={{0,64},{64,0},{128,192},{192,128},{1,65},{65,1},{129,193},{193,129... | collective-permute-start | bytes 196616 | tf_op jit(solution)/shard_map/ppermute | solution.py:283
  20.0 4.3 %collective-permute-start.6 = (bf16[8,32,128]{2,1,0:T(8,128)(2,1)S(1)}, bf16[8,32,128]{2,1,0:T(8,128)(2,1)S(1)}, u32[]{:S(2)}, u32[]{:S(2)}) collective-permute-start(bf16[8,32,128]{2,1,0:T(8,128)(2,1)S(1)} %get-tuple-element.43), channel_id=1, source_target_pairs={{0,192},{64,128},{128,64},{192,0},{1,193},{65,129},{129,65},{193,1... | collective-permute-start | bytes 196616 | tf_op jit(solution)/shard_map/ppermute | solution.py:283
  24.4 3.4 %collective-permute-start.7 = (bf16[8,32,128]{2,1,0:T(8,128)(2,1)S(1)}, bf16[8,32,128]{2,1,0:T(8,128)(2,1)S(1)}, u32[]{:S(2)}, u32[]{:S(2)}) collective-permute-start(bf16[8,32,128]{2,1,0:T(8,128)(2,1)S(1)} %shard_map.53.refs_0_), channel_id=1, source_target_pairs={{0,8},{8,0},{1,9},{9,1},{2,10},{10,2},{3,11},{11,3},{4,12},{12,4},... | collective-permute-start | bytes 196616 | tf_op jit(solution)/shard_map/ppermute | solution.py:287
  27.8 10.1 %collective-permute-start.10 = (bf16[8,32,128]{2,1,0:T(8,128)(2,1)S(1)}, bf16[8,32,128]{2,1,0:T(8,128)(2,1)S(1)}, u32[]{:S(2)}, u32[]{:S(2)}) collective-permute-start(bf16[8,32,128]{2,1,0:T(8,128)(2,1)S(1)} %shard_map.54.refs_0_), channel_id=1, source_target_pairs={{0,32},{16,48},{32,0},{48,16},{1,33},{17,49},{33,1},{49,17},{2,34}... | collective-permute-start | bytes 196616 | tf_op jit(solution)/shard_map/ppermute | solution.py:283
  34.6 14.9 %collective-permute-start.12 = (bf16[80,896]{1,0:T(8,128)(2,1)S(1)}, bf16[80,896]{1,0:T(8,128)(2,1)S(1)}, u32[]{:S(2)}, u32[]{:S(2)}) collective-permute-start(bf16[80,896]{1,0:T(8,128)(2,1)S(1)} %get-tuple-element.45), channel_id=1, source_target_pairs={{0,128},{64,192},{128,0},{192,64},{1,129},{65,193},{129,1},{193,65... | collective-permute-start | bytes 430088 | tf_op jit(solution)/shard_map/ppermute | solution.py:283
  36.2 13.3 %collective-permute-start.13 = (bf16[80,896]{1,0:T(8,128)(2,1)S(1)}, bf16[80,896]{1,0:T(8,128)(2,1)S(1)}, u32[]{:S(2)}, u32[]{:S(2)}) collective-permute-start(bf16[80,896]{1,0:T(8,128)(2,1)S(1)} %get-tuple-element.46), channel_id=1, source_target_pairs={{0,64},{64,0},{128,192},{192,128},{1,65},{65,1},{129,193},{193,129... | collective-permute-start | bytes 430088 | tf_op jit(solution)/shard_map/ppermute | solution.py:283
  37.0 12.5 %collective-permute-start.14 = (bf16[80,896]{1,0:T(8,128)(2,1)S(1)}, bf16[80,896]{1,0:T(8,128)(2,1)S(1)}, u32[]{:S(2)}, u32[]{:S(2)}) collective-permute-start(bf16[80,896]{1,0:T(8,128)(2,1)S(1)} %get-tuple-element.47), channel_id=1, source_target_pairs={{0,192},{64,128},{128,64},{192,0},{1,193},{65,129},{129,65},{193,1... | collective-permute-start | bytes 430088 | tf_op jit(solution)/shard_map/ppermute | solution.py:283
  37.9 5.3 %collective-permute-start.9 = (bf16[8,32,128]{2,1,0:T(8,128)(2,1)S(1)}, bf16[8,32,128]{2,1,0:T(8,128)(2,1)S(1)}, u32[]{:S(2)}, u32[]{:S(2)}) collective-permute-start(bf16[8,32,128]{2,1,0:T(8,128)(2,1)S(1)} %shard_map.54.refs_0_), channel_id=1, source_target_pairs={{0,48},{16,32},{32,16},{48,0},{1,49},{17,33},{33,17},{49,1},{2,50}... | collective-permute-start | bytes 196616 | tf_op jit(solution)/shard_map/ppermute | solution.py:283
  37.9 5.7 %collective-permute-start.8 = (bf16[8,32,128]{2,1,0:T(8,128)(2,1)S(1)}, bf16[8,32,128]{2,1,0:T(8,128)(2,1)S(1)}, u32[]{:S(2)}, u32[]{:S(2)}) collective-permute-start(bf16[8,32,128]{2,1,0:T(8,128)(2,1)S(1)} %shard_map.54.refs_0_), channel_id=1, source_target_pairs={{0,16},{16,0},{32,48},{48,32},{1,17},{17,1},{33,49},{49,33},{2,18}... | collective-permute-start | bytes 196616 | tf_op jit(solution)/shard_map/ppermute | solution.py:283
  43.6 6.8 %collective-permute-start.11 = (bf16[8,32,128]{2,1,0:T(8,128)(2,1)S(1)}, bf16[8,32,128]{2,1,0:T(8,128)(2,1)S(1)}, u32[]{:S(2)}, u32[]{:S(2)}) collective-permute-start(bf16[8,32,128]{2,1,0:T(8,128)(2,1)S(1)} %shard_map.55.part_ref), channel_id=1, source_target_pairs={{0,4},{4,0},{1,5},{5,1},{2,6},{6,2},{3,7},{7,3},{8,12},{12,8},{9,1... | collective-permute-start | bytes 196616 | tf_op jit(solution)/shard_map/ppermute | solution.py:287
  50.8 5.7 %collective-permute-start.17 = (f32[64,384]{1,0:T(8,128)S(1)}, f32[64,384]{1,0:T(8,128)S(1)}, u32[]{:S(2)}, u32[]{:S(2)}) collective-permute-start(f32[64,384]{1,0:T(8,128)S(1)} %get-tuple-element.48.refs_0_), channel_id=1, source_target_pairs={{0,128},{64,192},{128,0},{192,64},{1,129},{65,193},{129,1},{193,65... | collective-permute-start | bytes 294920 | tf_op jit(solution)/shard_map/ppermute | solution.py:283
  50.9 7.9 %collective-permute-start.16 = (f32[64,384]{1,0:T(8,128)S(1)}, f32[64,384]{1,0:T(8,128)S(1)}, u32[]{:S(2)}, u32[]{:S(2)}) collective-permute-start(f32[64,384]{1,0:T(8,128)S(1)} %get-tuple-element.48.refs_0_), channel_id=1, source_target_pairs={{0,192},{64,128},{128,64},{192,0},{1,193},{65,129},{129,65},{193,1... | collective-permute-start | bytes 294920 | tf_op jit(solution)/shard_map/ppermute | solution.py:283
  52.7 6.1 %collective-permute-start.15 = (f32[64,384]{1,0:T(8,128)S(1)}, f32[64,384]{1,0:T(8,128)S(1)}, u32[]{:S(2)}, u32[]{:S(2)}) collective-permute-start(f32[64,384]{1,0:T(8,128)S(1)} %get-tuple-element.48.refs_0_), channel_id=1, source_target_pairs={{0,64},{64,0},{128,192},{192,128},{1,65},{65,1},{129,193},{193,129... | collective-permute-start | bytes 294920 | tf_op jit(solution)/shard_map/ppermute | solution.py:283
  58.9 6.1 %collective-permute-start.20 = (f32[160,128]{1,0:T(8,128)S(1)}, f32[160,128]{1,0:T(8,128)S(1)}, u32[]{:S(2)}, u32[]{:S(2)}) collective-permute-start(f32[160,128]{1,0:T(8,128)S(1)} %get-tuple-element.50.refs_0_), channel_id=1, source_target_pairs={{0,2},{1,3},{2,0},{3,1},{4,6},{5,7},{6,4},{7,5},{8,10},{9,11},{10,... | collective-permute-start | bytes 245768 | tf_op jit(solution)/shard_map/ppermute | solution.py:283
  60.4 5.9 %collective-permute-start.19 = (f32[160,128]{1,0:T(8,128)S(1)}, f32[160,128]{1,0:T(8,128)S(1)}, u32[]{:S(2)}, u32[]{:S(2)}) collective-permute-start(f32[160,128]{1,0:T(8,128)S(1)} %get-tuple-element.50.refs_0_), channel_id=1, source_target_pairs={{0,3},{1,2},{2,1},{3,0},{4,7},{5,6},{6,5},{7,4},{8,11},{9,10},{10,... | collective-permute-start | bytes 245768 | tf_op jit(solution)/shard_map/ppermute | solution.py:283
  61.1 5.2 %collective-permute-start.18 = (f32[160,128]{1,0:T(8,128)S(1)}, f32[160,128]{1,0:T(8,128)S(1)}, u32[]{:S(2)}, u32[]{:S(2)}) collective-permute-start(f32[160,128]{1,0:T(8,128)S(1)} %get-tuple-element.50.refs_0_), channel_id=1, source_target_pairs={{0,1},{1,0},{2,3},{3,2},{4,5},{5,4},{6,7},{7,6},{8,9},{9,8},{10,11... | collective-permute-start | bytes 245768 | tf_op jit(solution)/shard_map/ppermute | solution.py:283
  67.2 2.1 %collective-permute-start.21 = (f32[8,32,128]{2,1,0:T(8,128)S(1)}, f32[8,32,128]{2,1,0:T(8,128)S(1)}, u32[]{:S(2)}, u32[]{:S(2)}) collective-permute-start(f32[8,32,128]{2,1,0:T(8,128)S(1)} %get-tuple-element.53), channel_id=1, source_target_pairs={{0,4},{4,0},{1,5},{5,1},{2,6},{6,2},{3,7},{7,3},{8,12},{12,8},{9,1... | collective-permute-start | bytes 393224 | tf_op jit(solution)/shard_map/ppermute | solution.py:287
  69.3 3.2 %collective-permute-start.22 = (f32[8,16,128]{2,1,0:T(8,128)S(1)}, f32[8,16,128]{2,1,0:T(8,128)S(1)}, u32[]{:S(2)}, u32[]{:S(2)}) collective-permute-start(f32[8,16,128]{2,1,0:T(8,128)S(1)} %get-tuple-element.55), channel_id=1, source_target_pairs={{0,8},{8,0},{1,9},{9,1},{2,10},{10,2},{3,11},{11,3},{4,12},{12,4},... | collective-permute-start | bytes 196616 | tf_op jit(solution)/shard_map/ppermute | solution.py:287
  72.5 7.1 %collective-permute-start.25 = (f32[8,16,128]{2,1,0:T(8,128)S(1)}, f32[8,16,128]{2,1,0:T(8,128)S(1)}, u32[]{:S(2)}, u32[]{:S(2)}) collective-permute-start(f32[8,16,128]{2,1,0:T(8,128)S(1)} %shard_map.61.refs_0_), channel_id=1, source_target_pairs={{0,32},{16,48},{32,0},{48,16},{1,33},{17,49},{33,1},{49,17},{2,34}... | collective-permute-start | bytes 196616 | tf_op jit(solution)/shard_map/ppermute | solution.py:283
  76.2 6.0 %collective-permute-start.24 = (f32[8,16,128]{2,1,0:T(8,128)S(1)}, f32[8,16,128]{2,1,0:T(8,128)S(1)}, u32[]{:S(2)}, u32[]{:S(2)}) collective-permute-start(f32[8,16,128]{2,1,0:T(8,128)S(1)} %shard_map.61.refs_0_), channel_id=1, source_target_pairs={{0,48},{16,32},{32,16},{48,0},{1,49},{17,33},{33,17},{49,1},{2,50}... | collective-permute-start | bytes 196616 | tf_op jit(solution)/shard_map/ppermute | solution.py:283
  76.7 5.5 %collective-permute-start.23 = (f32[8,16,128]{2,1,0:T(8,128)S(1)}, f32[8,16,128]{2,1,0:T(8,128)S(1)}, u32[]{:S(2)}, u32[]{:S(2)}) collective-permute-start(f32[8,16,128]{2,1,0:T(8,128)S(1)} %shard_map.61.refs_0_), channel_id=1, source_target_pairs={{0,16},{16,0},{32,48},{48,32},{1,17},{17,1},{33,49},{49,33},{2,18}... | collective-permute-start | bytes 196616 | tf_op jit(solution)/shard_map/ppermute | solution.py:283
  82.2 3.5 %collective-permute-start.26 = (f32[8,16,128]{2,1,0:T(8,128)S(1)}, f32[8,16,128]{2,1,0:T(8,128)S(1)}, u32[]{:S(2)}, u32[]{:S(2)}) collective-permute-start(f32[8,16,128]{2,1,0:T(8,128)S(1)} %shard_map.62.here_ref), channel_id=1, source_target_pairs={{0,8},{8,0},{1,9},{9,1},{2,10},{10,2},{3,11},{11,3},{4,12},{12,4},... | collective-permute-start | bytes 196616 | tf_op jit(solution)/shard_map/ppermute | solution.py:287
  85.7 11.4 %collective-permute-start.29 = (f32[7,32,128]{2,1,0:T(8,128)S(1)}, f32[7,32,128]{2,1,0:T(8,128)S(1)}, u32[]{:S(2)}, u32[]{:S(2)}) collective-permute-start(f32[7,32,128]{2,1,0:T(8,128)S(1)} %get-tuple-element.56.refs_0_), channel_id=1, source_target_pairs={{0,128},{64,192},{128,0},{192,64},{1,129},{65,193},{129,1},{193,65... | collective-permute-start | bytes 344072 | tf_op jit(solution)/shard_map/ppermute | solution.py:283
  88.6 8.6 %collective-permute-start.28 = (f32[7,32,128]{2,1,0:T(8,128)S(1)}, f32[7,32,128]{2,1,0:T(8,128)S(1)}, u32[]{:S(2)}, u32[]{:S(2)}) collective-permute-start(f32[7,32,128]{2,1,0:T(8,128)S(1)} %get-tuple-element.56.refs_0_), channel_id=1, source_target_pairs={{0,192},{64,128},{128,64},{192,0},{1,193},{65,129},{129,65},{193,1... | collective-permute-start | bytes 344072 | tf_op jit(solution)/shard_map/ppermute | solution.py:283
  89.1 8.0 %collective-permute-start.27 = (f32[7,32,128]{2,1,0:T(8,128)S(1)}, f32[7,32,128]{2,1,0:T(8,128)S(1)}, u32[]{:S(2)}, u32[]{:S(2)}) collective-permute-start(f32[7,32,128]{2,1,0:T(8,128)S(1)} %get-tuple-element.56.refs_0_), channel_id=1, source_target_pairs={{0,64},{64,0},{128,192},{192,128},{1,65},{65,1},{129,193},{193,129... | collective-permute-start | bytes 344072 | tf_op jit(solution)/shard_map/ppermute | solution.py:283
  89.1 9.2 %collective-permute-start.30 = (f32[7,32,128]{2,1,0:T(8,128)S(1)}, f32[7,32,128]{2,1,0:T(8,128)S(1)}, u32[]{:S(2)}, u32[]{:S(2)}) collective-permute-start(f32[7,32,128]{2,1,0:T(8,128)S(1)} %get-tuple-element.56.refs_0_), channel_id=1, source_target_pairs={{0,4},{4,0},{1,5},{5,1},{2,6},{6,2},{3,7},{7,3},{8,12},{12,8},{9,1... | collective-permute-start | bytes 344072 | tf_op jit(solution)/shard_map/ppermute | solution.py:287
  97.2 1.7 %collective-permute-start.31 = (f32[7,32,128]{2,1,0:T(8,128)S(1)}, f32[7,32,128]{2,1,0:T(8,128)S(1)}, u32[]{:S(2)}, u32[]{:S(2)}) collective-permute-start(f32[7,32,128]{2,1,0:T(8,128)S(1)} %collective-permute-done.27.refs_1_), channel_id=1, source_target_pairs={{0,4},{4,0},{1,5},{5,1},{2,6},{6,2},{3,7},{7,3},{8,12},{12,8},{9,1... | collective-permute-start | bytes 344072 | tf_op jit(solution)/shard_map/ppermute | solution.py:287
  97.9 1.3 %collective-permute-start.32 = (f32[7,32,128]{2,1,0:T(8,128)S(1)}, f32[7,32,128]{2,1,0:T(8,128)S(1)}, u32[]{:S(2)}, u32[]{:S(2)}) collective-permute-start(f32[7,32,128]{2,1,0:T(8,128)S(1)} %collective-permute-done.28.refs_2_), channel_id=1, source_target_pairs={{0,4},{4,0},{1,5},{5,1},{2,6},{6,2},{3,7},{7,3},{8,12},{12,8},{9,1... | collective-permute-start | bytes 344072 | tf_op jit(solution)/shard_map/ppermute | solution.py:287
  97.9 1.5 %collective-permute-start.33 = (f32[7,32,128]{2,1,0:T(8,128)S(1)}, f32[7,32,128]{2,1,0:T(8,128)S(1)}, u32[]{:S(2)}, u32[]{:S(2)}) collective-permute-start(f32[7,32,128]{2,1,0:T(8,128)S(1)} %collective-permute-done.29.refs_3_), channel_id=1, source_target_pairs={{0,4},{4,0},{1,5},{5,1},{2,6},{6,2},{3,7},{7,3},{8,12},{12,8},{9,1... | collective-permute-start | bytes 344072 | tf_op jit(solution)/shard_map/ppermute | solution.py:287
